TPU v7x, 32 devices: a whole 2x2x4 slice. The times are simulated.
32 devices in a mesh: groups: 2 (over y), tensor: 8 (over z, x), replica: 2 (over core).
Axes of the slice: x: 2, y: 2, z: 4, core: 2. Of those that a mesh axis runs over, the one named last changes fastest.
Arguments:
- hidden: bfloat16 [4, 28672, 128], P(('groups', 'replica'), 'tensor'), parts along dimension 0, may hold values from -6 to 6
- down_weight: bfloat16 [28672, 8192], P('tensor'), may hold values from -0.03125 to 0.03125
- residual: bfloat16 [4, 64, 128, 128], P(('groups', 'replica'), 'tensor'), parts along dimension 0, may hold values from -3 to 3
- norm_gain: float32 [8192], replicated, may hold values from 0.25 to 1.75
- query_weight: bfloat16 [8192, 8192], P('tensor'), may hold values from -0.0625 to 0.0625
- prefix_len: int32 [4], P(('groups', 'replica')), parts along dimension 0, may hold values from 1 to 8192
- seg_lengths: int32 [4, 4], P(('groups', 'replica')), parts along dimension 0, may hold values from 1 to 64, 128 in all within a row
Outputs:
- residual_out: bfloat16 [4, 64, 128, 128], P(('groups', 'replica'), 'tensor'), parts along dimension 0
- query_out: bfloat16 [4, 8192, 128], P(('groups', 'replica'), 'tensor'), parts along dimension 0
There are 2 independent parts, one for each index of `groups`. A program takes and returns all parts, laid end to end along the dimension named above; an argument that names none is the same for every part. Nothing has to cross between parts.
Inputs may be any that keep to these rules, and one draw needn't show every extreme that they name: `seg_lengths`: each row holds the lengths of 4 segments that together fill the 128 tokens; the longest is exactly 64.
All inputs are finite; a program needn't handle non-finite values.
Results may differ from a plain program's by a relative error of at most 0.012.
Values may be sent and summed in bfloat16 or wider, within the bound.
No kernel may reach another device: no remote copies, remote signals or barrier semaphores. Data moves between devices by JAX's collectives and lax.ppermute only.
A program may use at most 256 MiB of HBM per device.

v0:
```python
import math

import jax
import jax.numpy as jnp
from jax import lax
from jax.sharding import PartitionSpec as P

HEAD = 128
HB = 128


eps_norm = 1e-05
eps_scale = 1e-06
code_top = 448.0
least_normal = 0.015625
rope_base = 500000.0


def hadamard_table(order_size):
    row_ids = lax.broadcasted_iota(jnp.int32, (order_size, order_size), 0)
    col_ids = lax.broadcasted_iota(jnp.int32, (order_size, order_size), 1)
    common = jnp.bitwise_and(row_ids, col_ids)
    parity = jnp.zeros((order_size, order_size), jnp.int32)
    for shift_bits in range(order_size.bit_length()):
        parity = parity + jnp.bitwise_and(jnp.right_shift(common, shift_bits), 1)
    sign_table = (1 - 2 * (parity % 2)).astype(jnp.float32)
    return sign_table / math.sqrt(order_size)


def grid_code(scaled):
    magnitude = jnp.maximum(jnp.abs(scaled), least_normal)
    binade = jnp.floor(jnp.log2(magnitude))
    spacing = jnp.exp2(binade - 3.0)
    return spacing * jnp.floor(scaled / spacing + 0.5)


def positions_of(prefix_one, length_row, token_count):
    seg_total = length_row.shape[0]
    before = lax.broadcasted_iota(jnp.int32, (seg_total, seg_total), 0) < lax.broadcasted_iota(
        jnp.int32, (seg_total, seg_total), 1
    )
    seg_starts = jnp.sum(jnp.where(before, length_row[:, None], 0), axis=0)
    token_place = lax.broadcasted_iota(jnp.int32, (token_count, seg_total), 0)
    started = token_place >= seg_starts[None, :]
    seg_start = jnp.max(jnp.where(started, seg_starts[None, :], 0), axis=1)
    return (prefix_one + token_place[:, 0] - seg_start).astype(jnp.float32)


def rotate_rows(projected, columns, positions):
    token_count = projected.shape[1]
    even_columns = columns.reshape(-1, 2)[:, 0]
    pair_index = even_columns % HEAD // 2
    inv_freq = jnp.exp(pair_index.astype(jnp.float32) * (-2.0 * math.log(rope_base) / HEAD))
    angles = inv_freq[:, None] * positions[None, :]
    cosine = jnp.cos(angles)
    sine_part = jnp.sin(angles)
    paired = projected.reshape(-1, 2, token_count)
    even_part = paired[:, 0]
    odd_part = paired[:, 1]
    rotated_pairs = jnp.stack(
        [even_part * cosine - odd_part * sine_part, even_part * sine_part + odd_part * cosine],
        axis=1,
    )
    return rotated_pairs.reshape(projected.shape)


def local(hidden, down_weight, residual, norm_gain, query_weight, prefix_len, seg_lengths):
    members = lax.axis_size("tensor")
    span_len = hidden.shape[2]
    model_width = down_weight.shape[1]
    blocks = model_width // HB
    splits = max(1, members // blocks)
    piece_len = span_len // splits
    item_total = splits * blocks
    per_device = item_total // members
    hadamard = hadamard_table(HB)
    hidden_parts = hidden[0].reshape(hidden.shape[1], splits, piece_len)
    weight_parts = down_weight.reshape(down_weight.shape[0], blocks, HB)
    partial_value = jnp.einsum(
        "fsc,fbh->sbch", hidden_parts, weight_parts, preferred_element_type=jnp.float32
    )
    rotated = jnp.einsum("sbch,hk->sbck", partial_value, hadamard, precision=lax.Precision.HIGHEST)
    block_scale = (jnp.max(jnp.abs(rotated), axis=3, keepdims=True) + eps_scale) / code_top
    block_code = grid_code(rotated / block_scale).astype(jnp.bfloat16)
    sent_codes = block_code.reshape(members, per_device, piece_len, HB)
    sent_scales = block_scale.reshape(members, per_device, piece_len)
    got_codes = lax.all_to_all(sent_codes, "tensor", split_axis=0, concat_axis=0, tiled=True)
    got_scales = lax.all_to_all(
        sent_scales.astype(jnp.bfloat16), "tensor", split_axis=0, concat_axis=0, tiled=True
    ).astype(sent_scales.dtype)
    running = jnp.sum(got_codes.astype(jnp.float32) * got_scales[..., None], axis=0)
    item_count = running.shape[0]
    unrotated = jnp.dot(running.reshape(-1, HB), hadamard, precision=lax.Precision.HIGHEST)
    restored = unrotated.reshape(item_count, piece_len, HB)
    updated = (residual[0].astype(jnp.float32) + restored).astype(jnp.bfloat16)
    gathered = lax.all_gather(updated, "tensor", axis=0, tiled=True)
    widened = gathered.astype(jnp.float32).reshape(splits, blocks, piece_len, HB)
    mean_square = jnp.mean(widened * widened, axis=(1, 3), keepdims=True)
    gain_blocks = norm_gain.reshape(1, blocks, 1, HB)
    normed = (widened * lax.rsqrt(mean_square + eps_norm) * gain_blocks).astype(jnp.bfloat16)
    column_count = query_weight.shape[0]
    weight_blocks = query_weight.reshape(column_count, blocks, HB)
    projected = jnp.einsum(
        "qbh,sbch->qsc", weight_blocks, normed, preferred_element_type=jnp.float32
    ).reshape(column_count, span_len)
    positions = positions_of(prefix_len[0], seg_lengths[0], span_len)
    columns = lax.axis_index("tensor") * column_count + lax.iota(jnp.int32, column_count)
    query_one = rotate_rows(projected, columns, positions).astype(jnp.bfloat16)
    return (updated[None], query_one[None])


def solution(mesh):
    in_specs = (
        P(("groups", "replica"), "tensor", None),
        P("tensor", None),
        P(("groups", "replica"), "tensor", None, None),
        P(),
        P("tensor", None),
        P(("groups", "replica")),
        P(("groups", "replica"), None),
    )
    out_specs = (
        P(("groups", "replica"), "tensor", None, None),
        P(("groups", "replica"), "tensor", None),
    )
    return jax.shard_map(local, mesh=mesh, in_specs=in_specs, out_specs=out_specs, check_vma=False)
```

profile of v0, /device:TPU:0, one launch (start us, length us, event | category | flops | bytes accessed | tf_op | source)
XLA Modules:
  0.0 246.9 jit_solution(5962606676760904963)
XLA Ops:
  7.2 0.0 copy-start
  7.2 71.9 %copy.51 = bf16[3584,8192]{0,1:T(8,128)(2,1)} copy(bf16[3584,8192]{1,0:T(8,128)(2,1)} %param.8) | data formatting | bytes 117440512 | tf_op jit(solution)/shard_map/reshape | solution.py:78
  79.1 0.0 copy-done
  79.1 22.8 %fusion.17 = f32[64,128,128]{2,1,0:T(8,128)S(1)} fusion(bf16[3584,64,128]{0,2,1:T(8,128)(2,1)} %bitcast.56, bf16[1,3584,128]{2,1,0:T(8,128)(2,1)S(1)} %copy-done), kind=kOutput, calls=%fused_computation.18 | convolution fusion | flops 7516192768 | bytes 63832064 | tf_op jit(solution)/shard_map/fsc,fbh->sbch/dot_general | solution.py:79
  101.9 5.5 %abs_reduce_fusion = (f32[64,128]{1,0:T(8,128)S(1)}, f32[64,128,128]{1,2,0:T(8,128)}) fusion(f32[64,128,128]{2,1,0:T(8,128)S(1)} %fusion.17), kind=kOutput, calls=%fused_computation.12 | convolution fusion | flops 1613340672 | bytes 8421376 | tf_op jit(solution)/shard_map/sbch,hk->sbck/dot_general | solution.py:82
  107.5 0.6 convert_bitcast_fusion
  108.1 7.3 %all-to-all-start.1 = ((bf16[8,8,128]{2,1,0:T(8,128)(2,1)}), bf16[8,8,128]{2,1,0:T(8,128)(2,1)S(1)}, u32[]{:S(2)}, u32[]{:S(2)}) async-start(bf16[8,8,128]{2,1,0:T(8,128)(2,1)} %get-tuple-element.6), calls=%async_computation.1 | async-start | bytes 32768 | tf_op jit(solution)/shard_map/all_to_all | solution.py:88
  115.3 5.2 %multiply_convert_fusion = bf16[64,128,128]{1,2,0:T(8,128)(2,1)} fusion(f32[64,128,128]{1,2,0:T(8,128)} %get-tuple-element.9, f32[64,128]{1,0:T(8,128)S(1)} %get-tuple-element.7), kind=kLoop, calls=%fused_computation.11 | loop fusion | flops 13631488 | bytes 6324224 | tf_op jit(solution)/shard_map/convert_element_type | solution.py:84
  120.5 0.0 copy-start.2
  120.5 0.0 copy-start.4
  120.5 1.4 all-to-all-done.1
  121.9 0.0 copy-start.3
  121.9 4.8 %all-to-all-start = ((bf16[8,8,128,128]{2,3,1,0:T(8,128)(2,1)}), bf16[8,8,128,128]{2,3,1,0:T(8,128)(2,1)S(1)}, u32[]{:S(2)}, u32[]{:S(2)}) async-start(bf16[8,8,128,128]{2,3,1,0:T(8,128)(2,1)} %bitcast.8), calls=%async_computation | async-start | bytes 4194304 | tf_op jit(solution)/shard_map/all_to_all | solution.py:87
  126.7 0.2 all-gather.2.cloned.1.call-start
  126.9 47.4 %all-to-all-done = bf16[8,8,128,128]{2,3,1,0:T(8,128)(2,1)S(1)} async-done(((bf16[8,8,128,128]{2,3,1,0:T(8,128)(2,1)}), bf16[8,8,128,128]{2,3,1,0:T(8,128)(2,1)S(1)}, u32[]{:S(2)}, u32[]{:S(2)}) %all-to-all-start) | async-done | bytes 2097184 | tf_op jit(solution)/shard_map/all_to_all | solution.py:87
  174.4 0.5 multiply_reduce_fusion
  174.9 0.0 copy-done.2
  174.9 1.7 fusion.16
  176.6 0.0 all-gather.2.cloned.1.call-update
  177.3 0.0 copy-done.4
  177.3 0.1 select_reduce_fusion.1
  177.4 0.1 select_reduce_fusion
  177.5 47.6 %all-gather.2.cloned.1.call-done = bf16[64,128,128]{2,1,0:T(8,128)(2,1)} async-done(((bf16[8,128,128]{2,1,0:T(8,128)(2,1)}), bf16[64,128,128]{2,1,0:T(8,128)(2,1)}) %all-gather.2.cloned.1.call-update) | async-done | bytes 2097168 | tf_op jit(solution)/shard_map/all_gather | solution.py:96
  225.2 2.1 fusion.3
  227.3 0.0 copy-done.3
  227.3 0.0 copy-start.1
  227.3 9.9 %fusion.11 = f32[1024,128]{0,1:T(8,128)S(1)} fusion(bf16[64,128,128]{2,1,0:T(8,128)(2,1)} %all-gather.2.cloned.1.call-done, f32[64,128]{1,0:T(8,128)S(1)} %bitcast.63, f32[128]{0:T(128)S(1)} %add_rsqrt_fusion, bf16[1024,8192]{1,0:T(8,128)(2,1)} %param.11), kind=kOutput, calls=%fused_computation.16 | convolution fusion | flops 2151677952 | bytes 19431936 | tf_op jit(solution)/shard_map/qbh,sbch->qsc/dot_general | solution.py:103
  237.2 0.2 copy.44
  237.4 0.4 fusion.74
  237.8 1.2 fusion.24
  239.1 1.0 copy.47
  240.0 0.0 copy-done.1
  (6 shorter events, 0.1 us)
Async XLA Ops:
  7.2 72.0 %copy-start = (bf16[1,3584,128]{2,1,0:T(8,128)(2,1)S(1)}, bf16[1,3584,128]{2,1,0:T(8,128)(2,1)}, u32[]{:S(2)}) copy-start(bf16[1,3584,128]{2,1,0:T(8,128)(2,1)} %param.7) | copy-start | bytes 2752516
  108.1 13.8 %all-to-all-start.1 = ((bf16[8,8,128]{2,1,0:T(8,128)(2,1)}), bf16[8,8,128]{2,1,0:T(8,128)(2,1)S(1)}, u32[]{:S(2)}, u32[]{:S(2)}) async-start(bf16[8,8,128]{2,1,0:T(8,128)(2,1)} %get-tuple-element.6), calls=%async_computation.1 | async-start | bytes 32768 | tf_op jit(solution)/shard_map/all_to_all | solution.py:88
  120.5 54.4 %copy-start.2 = (bf16[1,8,128,128]{3,2,1,0:T(8,128)(2,1)S(1)}, bf16[1,8,128,128]{3,2,1,0:T(8,128)(2,1)}, u32[]{:S(2)}) copy-start(bf16[1,8,128,128]{3,2,1,0:T(8,128)(2,1)} %param.9) | copy-start | bytes 786436
  120.5 56.8 %copy-start.4 = (s32[1,4]{1,0:T(1,128)S(1)}, s32[1,4]{1,0:T(1,128)}, u32[]{:S(2)}) copy-start(s32[1,4]{1,0:T(1,128)} %param.13) | copy-start | bytes 52
  121.9 105.3 %copy-start.3 = (f32[8192]{0:T(1024)S(1)}, f32[8192]{0:T(1024)}, u32[]{:S(2)}) copy-start(f32[8192]{0:T(1024)} %param.10) | copy-start | bytes 98308
  121.9 52.4 %all-to-all-start = ((bf16[8,8,128,128]{2,3,1,0:T(8,128)(2,1)}), bf16[8,8,128,128]{2,3,1,0:T(8,128)(2,1)S(1)}, u32[]{:S(2)}, u32[]{:S(2)}) async-start(bf16[8,8,128,128]{2,3,1,0:T(8,128)(2,1)} %bitcast.8), calls=%async_computation | async-start | bytes 4194304 | tf_op jit(solution)/shard_map/all_to_all | solution.py:87
  126.7 98.5 %all-gather.2.cloned.1.call-start = ((), (), s32[]{:S(2)}) async-start(), calls=%async_computation.2 | async-start | bytes 2359296 | tf_op jit(solution)/shard_map/all_gather | solution.py:96
  227.3 12.8 %copy-start.1 = (bf16[1,3584,128]{2,1,0:T(8,128)(2,1)S(1)}, bf16[1,3584,128]{2,1,0:T(8,128)(2,1)}, u32[]{:S(2)}) copy-start(bf16[1,3584,128]{2,1,0:T(8,128)(2,1)} %param.7) | copy-start | bytes 2752516
Sparse Core Ops, SparseCore 0:
  176.8 48.3 all-gather.1
where the time goes:
time: 249 us; the launch traced here: 247 us
  waiting for transfers between devices  96.5 us (39%)
  local copies, waits for them, and re-layouts  73.5 us (30%)
  matrix products  40 us (16%)
  between operations  14.8 us (6%)
  starting transfers between devices  12.2 us (5%)
  other arithmetic  9.86 us (4%)
    reshape x1, local copies, waits for them, and re-layouts, local(): weight_parts = down_weight.reshape(down_weight.shape[0], blocks, HB)  71.9 us
    all_gather x1, waiting for transfers between devices, local(): gathered = lax.all_gather(updated, 'tensor', axis=0, tiled=True)  47.6 us
    all_to_all x1, waiting for transfers between devices, local(): lax.all_to_all(sent_codes, 'tensor', split_axis=0, concat_axis=0, tiled=T...  47.4 us
    dot_general x1, matrix products, local(): jnp.einsum('fsc,fbh->sbch', hidden_parts, weight_parts, preferred_element...  22.8 us
    dot_general x1, matrix products, local(): jnp.einsum('qbh,sbch->qsc', weight_blocks, normed, preferred_element_type...  9.93 us
    all_to_all x1, starting transfers between devices, local(): lax.all_to_all(sent_scales.astype(jnp.bfloat16), 'tensor', split_axis=0,...  7.26 us
    dot_general x1, matrix products, local(): jnp.einsum('sbch,hk->sbck', partial_value, hadamard, precision=lax.Precis...  5.53 us
    convert_element_type x1, other arithmetic, local(): block_code = grid_code(rotated / block_scale).astype(jnp.bfloat16)  5.17 us
  transfers between devices with their start and end apart: 3, of which 3 were waited for; matrix products, arithmetic and copies ran while one was open for 2% of the time, Pallas kernels for 0%

commit v1 on v0

--- a/solution.py
+++ b/solution.py
@@ -1,8 +1,12 @@
+import functools
 import math
 
 import jax
 import jax.numpy as jnp
+import numpy as np
 from jax import lax
+from jax.experimental import pallas as pl
+from jax.experimental.pallas import tpu as pltpu
 from jax.sharding import PartitionSpec as P
 
 HEAD = 128
@@ -14,6 +18,9 @@
 code_top = 448.0
 least_normal = 0.015625
 rope_base = 500000.0
+
+bf16 = jnp.bfloat16
+f32 = jnp.float32
 
 
 def hadamard_table(order_size):
@@ -25,6 +32,16 @@
         parity = parity + jnp.bitwise_and(jnp.right_shift(common, shift_bits), 1)
     sign_table = (1 - 2 * (parity % 2)).astype(jnp.float32)
     return sign_table / math.sqrt(order_size)
+
+
+def hadamard_signs():
+    ids = np.arange(HB)
+    common = ids[:, None] & ids[None, :]
+    parity = np.zeros_like(common)
+    for shift_bits in range(HB.bit_length()):
+        parity += (common >> shift_bits) & 1
+    signs = (1 - 2 * (parity % 2)).astype(np.float32)
+    return jnp.asarray(np.concatenate([signs, signs], axis=0)).astype(bf16)
 
 
 def grid_code(scaled):
@@ -64,7 +81,7 @@
     return rotated_pairs.reshape(projected.shape)
 
 
-def local(hidden, down_weight, residual, norm_gain, query_weight, prefix_len, seg_lengths):
+def local_general(hidden, down_weight, residual, norm_gain, query_weight, prefix_len, seg_lengths):
     members = lax.axis_size("tensor")
     span_len = hidden.shape[2]
     model_width = down_weight.shape[1]
@@ -74,11 +91,10 @@
     item_total = splits * blocks
     per_device = item_total // members
     hadamard = hadamard_table(HB)
-    hidden_parts = hidden[0].reshape(hidden.shape[1], splits, piece_len)
-    weight_parts = down_weight.reshape(down_weight.shape[0], blocks, HB)
-    partial_value = jnp.einsum(
-        "fsc,fbh->sbch", hidden_parts, weight_parts, preferred_element_type=jnp.float32
-    )
+    partial_value = lax.dot_general(
+        hidden[0], down_weight, (((0,), (0,)), ((), ())), preferred_element_type=jnp.float32
+    )
+    partial_value = partial_value.reshape(splits, piece_len, blocks, HB).transpose(0, 2, 1, 3)
     rotated = jnp.einsum("sbch,hk->sbck", partial_value, hadamard, precision=lax.Precision.HIGHEST)
     block_scale = (jnp.max(jnp.abs(rotated), axis=3, keepdims=True) + eps_scale) / code_top
     block_code = grid_code(rotated / block_scale).astype(jnp.bfloat16)
@@ -109,6 +125,280 @@
     return (updated[None], query_one[None])
 
 
+def split_dot(value, signs):
+    high = value.astype(bf16)
+    low = (value - high.astype(f32)).astype(bf16)
+    return jnp.dot(jnp.concatenate([high, low], axis=1), signs, preferred_element_type=f32)
+
+
+def down_kernel(counts, units, rows_ref, weight_ref, signs_ref, *outs):
+    step = pl.program_id(0)
+    tiles = counts["tiles"]
+    per_tile = counts["per_tile"]
+    total = jnp.dot(rows_ref[...], weight_ref[...], preferred_element_type=f32)
+    signs = signs_ref[...]
+    values = []
+    for j in range(per_tile):
+        rotated = split_dot(total[:, j * HB : (j + 1) * HB], signs)
+        top = jnp.max(jnp.abs(rotated), axis=1, keepdims=True) * (1.0 / math.sqrt(HB)) + eps_scale
+        scaled = rotated * ((code_top / math.sqrt(HB)) / top)
+        magnitude = jnp.maximum(jnp.abs(scaled), least_normal)
+        binade = jnp.floor(jnp.log2(magnitude))
+        code = jnp.exp2(binade - 3.0) * jnp.floor(scaled * jnp.exp2(3.0 - binade) + 0.5)
+        values.append(code * (top * (1.0 / code_top)))
+    for k, out in enumerate(outs):
+
+        def store(out=out):
+            for j in range(per_tile):
+                out[j] = values[j].astype(out.dtype)
+
+        if len(outs) == 1:
+            store()
+        else:
+            pl.when(step // tiles == k)(store)
+
+
+def down_units(rows, down_weight, signs, units, dtypes):
+    count = len(dtypes)
+    tokens, depth = rows.shape
+    unit_width = down_weight.shape[1] // 8
+    tile = 256
+    tiles = unit_width // tile
+    per_tile = tile // HB
+    unit_blocks = unit_width // HB
+    out_specs = [
+        pl.BlockSpec(
+            (per_tile, tokens, HB),
+            functools.partial(lambda i, s, k: (jnp.clip(i - k * tiles, 0, tiles - 1), 0, 0), k=k),
+        )
+        for k in range(count)
+    ]
+    return pl.pallas_call(
+        functools.partial(down_kernel, dict(tiles=tiles, per_tile=per_tile)),
+        grid_spec=pltpu.PrefetchScalarGridSpec(
+            num_scalar_prefetch=1,
+            grid=(count * tiles,),
+            in_specs=[
+                pl.BlockSpec((tokens, depth), lambda i, s: (0, 0)),
+                pl.BlockSpec((depth, tile), lambda i, s: (0, s[i // tiles] * tiles + i % tiles)),
+                pl.BlockSpec((2 * HB, HB), lambda i, s: (0, 0)),
+            ],
+            out_specs=out_specs,
+        ),
+        out_shape=[jax.ShapeDtypeStruct((unit_blocks, tokens, HB), d) for d in dtypes],
+        compiler_params=pltpu.CompilerParams(vmem_limit_bytes=24 << 20),
+        cost_estimate=pl.CostEstimate(
+            flops=2 * tokens * depth * unit_width * count,
+            bytes_accessed=2 * depth * unit_width * count,
+            transcendentals=0,
+        ),
+        name="down_units",
+    )(jnp.stack(units), rows, down_weight, signs)
+
+
+def update_kernel(own_ref, a_ref, b_ref, c_ref, residual_ref, signs_ref, out_ref):
+    signs = signs_ref[...]
+    for j in range(own_ref.shape[0]):
+        summed = own_ref[j] + a_ref[j].astype(f32) + b_ref[j].astype(f32) + c_ref[j].astype(f32)
+        restored = split_dot(summed, signs) * (1.0 / math.sqrt(HB))
+        out_ref[j] = (residual_ref[j].astype(f32) + restored).astype(out_ref.dtype)
+
+
+def update(own, a, b, c, residual, signs):
+    return pl.pallas_call(
+        update_kernel,
+        out_shape=jax.ShapeDtypeStruct(residual.shape, residual.dtype),
+        compiler_params=pltpu.CompilerParams(vmem_limit_bytes=24 << 20),
+        name="update",
+    )(own, a, b, c, residual, signs)
+
+
+def query_kernel(info, units, *refs):
+    count, tiles, tile, first, last = (info[n] for n in ("count", "tiles", "tile", "first", "last"))
+    refs = list(refs)
+    stream = [refs.pop(0) for _ in range(count)]
+    gains = [refs.pop(0) for _ in range(count)]
+    weight_ref = refs.pop(0)
+    if not first:
+        acc_in, square_in = refs.pop(0), refs.pop(0)
+    if last:
+        cos_ref, sin_ref, out_ref, acc_ref, square_ref, factor = refs
+    else:
+        acc_ref, square_ref, factor = refs
+    step = pl.program_id(0)
+    blocks = stream[0].shape[0]
+    for k in range(count):
+
+        @pl.when(step == k * tiles)
+        def _(k=k):
+            squares = None
+            for j in range(blocks):
+                value = stream[k][j].astype(f32)
+                squares = value * value if squares is None else squares + value * value
+                factor[:, j * HB : (j + 1) * HB] = (value * gains[k][j : j + 1, :]).astype(bf16)
+            if k > 0:
+                square_ref[...] += squares
+            elif first:
+                square_ref[...] = squares
+            else:
+                square_ref[...] = square_in[...] + squares
+
+    product = lax.dot_general(
+        weight_ref[...], factor[...], (((1,), (1,)), ((), ())), preferred_element_type=f32
+    )
+    here = pl.ds(pl.multiple_of((step % tiles) * tile, tile), tile)
+
+    @pl.when(step < tiles)
+    def _():
+        if first:
+            acc_ref[here, :] = product
+        else:
+            acc_ref[here, :] = acc_in[here, :] + product
+
+    if count > 1:
+
+        @pl.when(step >= tiles)
+        def _():
+            acc_ref[here, :] += product
+
+    if last:
+
+        @pl.when(step >= (count - 1) * tiles)
+        def _():
+            mean_square = jnp.sum(square_ref[...].T, axis=0, keepdims=True) * (1.0 / info["width"])
+            root = lax.rsqrt(mean_square + eps_norm)
+            even = lax.broadcasted_iota(jnp.int32, (HEAD, HB), 0) % 2 == 0
+            for h in range(tile // HEAD):
+                rows = pl.ds(pl.multiple_of((step % tiles) * tile + h * HEAD, HEAD), HEAD)
+                value = acc_ref[rows, :] * root
+                up, down = pltpu.roll(value, HEAD - 1, 0), pltpu.roll(value, 1, 0)
+                other = jnp.where(even, up, down)
+                out_ref[h * HEAD : (h + 1) * HEAD, :] = (value * cos_ref[...] + other * sin_ref[...]).astype(out_ref.dtype)
+
+
+def query_units(streams, units, gain, query_weight, carried=None, tables=None):
+    count = len(streams)
+    blocks, tokens, _ = streams[0].shape
+    columns, width = query_weight.shape
+    unit_width = blocks * HB
+    tile = 256
+    tiles = columns // tile
+    first, last = carried is None, tables is not None
+    info = dict(count=count, tiles=tiles, tile=tile, first=first, last=last, width=width)
+    whole = lambda shape: pl.BlockSpec(shape, lambda i, s: (0,) * len(shape))
+    in_specs = [whole((blocks, tokens, HB))] * count
+    in_specs += [pl.BlockSpec((blocks, HB), functools.partial(lambda i, s, k: (s[k], 0), k=k)) for k in range(count)]
+    in_specs += [pl.BlockSpec((tile, unit_width), lambda i, s: (i % tiles, s[i // tiles]))]
+    args = [*streams, *([gain] * count), query_weight]
+    if not first:
+        in_specs += [whole((columns, tokens)), whole((tokens, HB))]
+        args += list(carried)
+    scratch = [pltpu.VMEM((tokens, unit_width), bf16)]
+    state = [((columns, tokens), f32), ((tokens, HB), f32)]
+    if last:
+        in_specs += [whole((HEAD, tokens))] * 2
+        args += list(tables)
+        out_specs = pl.BlockSpec((tile, tokens), lambda i, s: (jnp.maximum(i - (count - 1) * tiles, 0), 0))
+        out_shape = jax.ShapeDtypeStruct((columns, tokens), bf16)
+        scratch = [pltpu.VMEM(s, d) for s, d in state] + scratch
+    else:
+        out_specs = [whole(s) for s, _ in state]
+        out_shape = [jax.ShapeDtypeStruct(s, d) for s, d in state]
+    return pl.pallas_call(
+        functools.partial(query_kernel, info),
+        grid_spec=pltpu.PrefetchScalarGridSpec(
+            num_scalar_prefetch=1,
+            grid=(count * tiles,),
+            in_specs=in_specs,
+            out_specs=out_specs,
+            scratch_shapes=scratch,
+        ),
+        out_shape=out_shape,
+        compiler_params=pltpu.CompilerParams(vmem_limit_bytes=24 << 20),
+        cost_estimate=pl.CostEstimate(
+            flops=2 * tokens * columns * unit_width * count,
+            bytes_accessed=2 * columns * unit_width * count,
+            transcendentals=0,
+        ),
+        name="query_units",
+    )(jnp.stack(units), *args)
+
+
+def rotary_tables(positions):
+    row_ids = jnp.arange(HEAD, dtype=jnp.int32)
+    inv_freq = jnp.exp((row_ids // 2).astype(f32) * (-2.0 * math.log(rope_base) / HEAD))
+    angles = inv_freq[:, None] * positions[None, :]
+    sign = jnp.where(row_ids % 2 == 0, -1.0, 1.0).astype(f32)
+    return jnp.cos(angles), jnp.sin(angles) * sign[:, None]
+
+
+def line_pairs(pairs):
+    return [(2 * a + x, 2 * b + x) for a, b in pairs for x in range(2)]
+
+
+ACROSS = [(t, t ^ 1) for t in range(8)]
+TWINS = line_pairs([(0, 1), (1, 0), (2, 3), (3, 2)])
+MIDDLE = line_pairs([(1, 2), (2, 1)])
+INWARD = line_pairs([(0, 1), (3, 2)])
+OUTWARD = line_pairs([(1, 0), (2, 3)])
+
+
+def send(value, pairs):
+    return lax.ppermute(value.astype(bf16), "tensor", pairs)
+
+
+def local_eight(hidden, down_weight, residual, norm_gain, query_weight, prefix_len, seg_lengths):
+    place = lax.axis_index("tensor").astype(jnp.int32)
+    z, x = place // 2, place % 2
+    tokens = hidden.shape[2]
+    slot = [z, z ^ 1, jnp.where(z < 2, 2, 1), jnp.where(z < 2, 3, 0)]
+    mine = [2 * s + x for s in slot]
+    theirs = [2 * s + 1 - x for s in slot]
+    signs = hadamard_signs()
+    rows = hidden[0].T
+
+    def down(units, dtypes):
+        return down_units(rows, down_weight, signs, units, dtypes)
+
+    out3, = down([theirs[3]], [bf16])
+    got3 = send(out3, ACROSS)
+    own3, out2 = down([mine[3], theirs[2]], [f32, bf16])
+    got2 = send(out2, ACROSS)
+    own2, out1 = down([mine[2], theirs[1]], [f32, bf16])
+    got1 = send(out1, ACROSS)
+    own1, out0 = down([mine[1], theirs[0]], [f32, bf16])
+    got0 = send(out0, ACROSS)
+    own0, = down([mine[0]], [f32])
+
+    sum3 = own3 + got3.astype(f32)
+    sum3 = sum3 + send(sum3, INWARD).astype(f32)
+    sum2 = own2 + got2.astype(f32)
+    sum2 = sum2 + send(sum2, INWARD).astype(f32)
+    sum1 = own1 + got1.astype(f32) + send(sum3, MIDDLE).astype(f32)
+    from2 = send(sum2, MIDDLE)
+    from1 = send(sum1, TWINS)
+    updated = update(own0, got0, from2, from1, residual[0], signs)
+
+    gain = norm_gain.reshape(-1, HB)
+    tables = rotary_tables(positions_of(prefix_len[0], seg_lengths[0], tokens))
+    unit0 = updated
+    unit1 = send(unit0, TWINS)
+    inner2 = send(unit0, MIDDLE)
+    inner3 = send(unit1, MIDDLE)
+    unit2 = inner2 + send(inner2, OUTWARD)
+    unit3 = inner3 + send(inner3, OUTWARD)
+    side0 = send(unit0, ACROSS)
+    side1 = send(unit1, ACROSS)
+    side2 = send(unit2, ACROSS)
+    side3 = send(unit3, ACROSS)
+    state = query_units([unit0], [mine[0]], gain, query_weight)
+    state = query_units([side0, unit1], [theirs[0], mine[1]], gain, query_weight, state)
+    state = query_units([side1, unit2], [theirs[1], mine[2]], gain, query_weight, state)
+    state = query_units([side2, unit3], [theirs[2], mine[3]], gain, query_weight, state)
+    query_one = query_units([side3], [theirs[3]], gain, query_weight, state, tables)
+    return (updated[None], query_one[None])
+
+
 def solution(mesh):
     in_specs = (
         P(("groups", "replica"), "tensor", None),
@@ -123,4 +413,5 @@
         P(("groups", "replica"), "tensor", None, None),
         P(("groups", "replica"), "tensor", None),
     )
+    local = local_eight if mesh.shape["tensor"] == 8 else local_general
     return jax.shard_map(local, mesh=mesh, in_specs=in_specs, out_specs=out_specs, check_vma=False)

time: 249 us -> 126 us (0.51)
  waiting for transfers between devices: 96.5 us -> 16.1 us
  Pallas kernels: 0 us -> 61.1 us
  local copies, waits for them, and re-layouts: 73.5 us -> 14.8 us
  matrix products: 40 us -> 0 us
  starting transfers between devices: 12.2 us -> 28.9 us
  between operations: 14.8 us -> 1.73 us
  other arithmetic: 9.86 us -> 2.43 us
    reshape x1 -> x0, local copies, waits for them, and re-layouts: 71.9 us -> none  [local(): weight_parts = down_weight.reshape(down_weight.shape[0], blocks, HB)]
    pallas_call x0 -> x11, Pallas kernels: none -> 61.1 us  [the longest x5 44.1 us: down_units(): pl.pallas_call(functools.partial(down_kernel, dict(tiles=tiles, per_tile=...]
    all_to_all x2 -> x0, waiting for transfers between devices: 48.8 us -> none  [the longest x1 47.4 us: local(): lax.all_to_all(sent_codes, 'tensor', split_axis=0, concat_axis=0, tiled=T...]
    all_gather x1 -> x0, waiting for transfers between devices: 47.6 us -> none  [local(): gathered = lax.all_gather(updated, 'tensor', axis=0, tiled=True)]
    dot_general x4 -> x0, matrix products: 40 us -> none  [the longest x1 22.8 us: local(): jnp.einsum('fsc,fbh->sbch', hidden_parts, weight_parts, preferred_element...]
    ppermute x0 -> x18, starting transfers between devices: none -> 28.9 us  [send(): return lax.ppermute(value.astype(bf16), 'tensor', pairs)]
    ppermute x0 -> x18, waiting for transfers between devices: none -> 16.1 us  [send(): return lax.ppermute(value.astype(bf16), 'tensor', pairs)]
    unnamed x10 -> x25, local copies, waits for them, and re-layouts: 0.03 us -> 14.8 us
  transfers between devices with their start and end apart: 3 -> 18, of which waited for: 3 -> 4; matrix products, arithmetic and copies ran while one was open for 2% -> 2% of each run, Pallas kernels for 0% -> 41%
where the time goes in v1:
time: 126 us; the launch traced here: 125 us
  Pallas kernels  61.1 us (48%)
  starting transfers between devices  28.9 us (23%)
  waiting for transfers between devices  16.1 us (13%)
  local copies, waits for them, and re-layouts  14.8 us (12%)
  other arithmetic  2.43 us (2%)
  between operations  1.73 us (1%)
    pallas_call x5, Pallas kernels, down_units(): pl.pallas_call(functools.partial(down_kernel, dict(tiles=tiles, per_tile=...  44.1 us
    ppermute x18, starting transfers between devices, send(): return lax.ppermute(value.astype(bf16), 'tensor', pairs)  28.9 us
    ppermute x18, waiting for transfers between devices, send(): return lax.ppermute(value.astype(bf16), 'tensor', pairs)  16.1 us
    pallas_call x5, Pallas kernels, query_units(): pl.pallas_call(functools.partial(query_kernel, info), grid_spec=pltpu.Pre...  16 us
    unnamed x25, local copies, waits for them, and re-layouts  14.8 us
  transfers between devices with their start and end apart: 18, of which 4 were waited for; matrix products, arithmetic and copies ran while one was open for 2% of the time, Pallas kernels for 41%

profile of v1, /device:TPU:0, one launch (start us, length us, event | category | flops | bytes accessed | tf_op | source)
XLA Modules:
  0.0 125.0 jit_solution(13751224098002468760)
XLA Ops:
  0.6 0.0 copy-start.3
  0.7 1.5 %copy.11 = bf16[1,3584,128]{1,2,0:T(8,128)(2,1)S(1)} copy(bf16[1,3584,128]{2,1,0:T(8,128)(2,1)} %param.8) | data formatting | bytes 1835008 | tf_op args[0]
  2.1 0.0 copy-start.2
  2.2 0.8 copy-done.2
  3.0 5.4 %down_units.9 = bf16[8,128,128]{2,1,0:T(8,128)(2,1)S(1)} custom-call(s32[1]{0:T(128)} %bitcast.10.units, bf16[128,3584]{1,0:T(8,128)(2,1)S(1)} %bitcast.24, bf16[3584,8192]{1,0:T(8,128)(2,1)} %weight_ref.9, bf16[256,128]{1,0:T(8,128)(2,1)S(1)} %copy-done.2), custom_call_target="tpu_custom_call" | custom-call | flops 939524096 | bytes 7340032 | tf_op jit(solution)/shard_map/down_units/pallas_call | solution.py:176
  8.4 3.0 %collective-permute-start.5 = (bf16[8,128,128]{2,1,0:T(8,128)(2,1)S(1)}, bf16[8,128,128]{2,1,0:T(8,128)(2,1)S(1)}, u32[]{:S(2)}, u32[]{:S(2)}) collective-permute-start(bf16[8,128,128]{2,1,0:T(8,128)(2,1)S(1)} %down_units.9), channel_id=1, source_target_pairs={{0,2},{2,0},{4,6},{6,4},{8,10},{10,8},{12,14},{14,12},{1,3},{3,1},... | collective-permute-start | bytes 786440 | tf_op jit(solution)/shard_map/ppermute | solution.py:347
  11.4 0.1 pad_add_fusion.1.units
  11.5 10.7 %down_units.7 = (f32[8,128,128]{2,1,0:T(8,128)S(1)}, bf16[8,128,128]{2,1,0:T(8,128)(2,1)S(1)}) custom-call(s32[2]{0:T(128)S(1)} %pad_add_fusion.1.units, bf16[128,3584]{1,0:T(8,128)(2,1)S(1)} %bitcast.25, bf16[3584,8192]{1,0:T(8,128)(2,1)} %weight_ref.9, bf16[256,128]{1,0:T(8,128)(2,1)S(1)} %copy-done.3), custom_call_target="tpu_custom_call" | custom-call | flops 1879048192 | bytes 14680064 | tf_op jit(solution)/shard_map/down_units/pallas_call | solution.py:176
  22.2 0.1 collective-permute-start.4
  22.3 0.1 pad_add_fusion.2.units
  22.4 10.7 %down_units.8 = (f32[8,128,128]{2,1,0:T(8,128)S(1)}, bf16[8,128,128]{2,1,0:T(8,128)(2,1)S(1)}) custom-call(s32[2]{0:T(128)S(1)} %pad_add_fusion.2.units, bf16[128,3584]{1,0:T(8,128)(2,1)S(1)} %bitcast.26, bf16[3584,8192]{1,0:T(8,128)(2,1)} %weight_ref.9, bf16[256,128]{1,0:T(8,128)(2,1)S(1)} %copy-done.3), custom_call_target="tpu_custom_call" | custom-call | flops 1879048192 | bytes 14680064 | tf_op jit(solution)/shard_map/down_units/pallas_call | solution.py:176
  33.1 2.1 %collective-permute-start.1 = (bf16[8,128,128]{2,1,0:T(8,128)(2,1)S(1)}, bf16[8,128,128]{2,1,0:T(8,128)(2,1)S(1)}, u32[]{:S(2)}, u32[]{:S(2)}) collective-permute-start(bf16[8,128,128]{2,1,0:T(8,128)(2,1)S(1)} %get-tuple-element.18), channel_id=1, source_target_pairs={{0,2},{2,0},{4,6},{6,4},{8,10},{10,8},{12,14},{14,12},{1,3},{3,1},... | collective-permute-start | bytes 786440 | tf_op jit(solution)/shard_map/ppermute | solution.py:347
  35.1 0.1 fusion.1
  35.2 3.5 %collective-permute-start.6 = (bf16[8,128,128]{2,1,0:T(8,128)(2,1)S(1)}, bf16[8,128,128]{2,1,0:T(8,128)(2,1)S(1)}, u32[]{:S(2)}, u32[]{:S(2)}) collective-permute-start(bf16[8,128,128]{2,1,0:T(8,128)(2,1)S(1)} %fusion.1), channel_id=1, source_target_pairs={{0,4},{2,6},{12,8},{14,10},{1,5},{3,7},{13,9},{15,11},{16,20},{18,... | collective-permute-start | bytes 786440 | tf_op jit(solution)/shard_map/ppermute | solution.py:347
  38.7 0.1 pad_add_fusion.units
  38.8 2.1 %collective-permute-done.1 = bf16[8,128,128]{2,1,0:T(8,128)(2,1)S(1)} collective-permute-done((bf16[8,128,128]{2,1,0:T(8,128)(2,1)S(1)}, bf16[8,128,128]{2,1,0:T(8,128)(2,1)S(1)}, u32[]{:S(2)}, u32[]{:S(2)}) %collective-permute-start.1) | collective-permute-done | bytes 262176 | tf_op jit(solution)/shard_map/ppermute | solution.py:347
  40.9 0.1 fusion
  41.0 3.7 %collective-permute-start.2 = (bf16[8,128,128]{2,1,0:T(8,128)(2,1)S(1)}, bf16[8,128,128]{2,1,0:T(8,128)(2,1)S(1)}, u32[]{:S(2)}, u32[]{:S(2)}) collective-permute-start(bf16[8,128,128]{2,1,0:T(8,128)(2,1)S(1)} %fusion), channel_id=1, source_target_pairs={{0,4},{2,6},{12,8},{14,10},{1,5},{3,7},{13,9},{15,11},{16,20},{18,... | collective-permute-start | bytes 786440 | tf_op jit(solution)/shard_map/ppermute | solution.py:347
  44.7 0.0 collective-permute-done.6
  44.7 0.1 add_convert_fusion.1
  44.8 0.0 copy-start.6
  44.8 0.0 copy-start.7
  44.8 0.0 copy-start.4
  44.8 0.8 collective-permute-start.7
  45.7 10.7 %down_units.6 = (f32[8,128,128]{2,1,0:T(8,128)S(1)}, bf16[8,128,128]{2,1,0:T(8,128)(2,1)S(1)}) custom-call(s32[2]{0:T(128)S(1)} %pad_add_fusion.units, bf16[128,3584]{1,0:T(8,128)(2,1)S(1)} %bitcast.27, bf16[3584,8192]{1,0:T(8,128)(2,1)} %weight_ref.9, bf16[256,128]{1,0:T(8,128)(2,1)S(1)} %copy-done.3), custom_call_target="tpu_custom_call" | custom-call | flops 1879048192 | bytes 14680064 | tf_op jit(solution)/shard_map/down_units/pallas_call | solution.py:176
  56.4 1.6 %collective-permute-start = (bf16[8,128,128]{2,1,0:T(8,128)(2,1)S(1)}, bf16[8,128,128]{2,1,0:T(8,128)(2,1)S(1)}, u32[]{:S(2)}, u32[]{:S(2)}) collective-permute-start(bf16[8,128,128]{2,1,0:T(8,128)(2,1)S(1)} %get-tuple-element.16), channel_id=1, source_target_pairs={{0,2},{2,0},{4,6},{6,4},{8,10},{10,8},{12,14},{14,12},{1,3},{3,1},... | collective-permute-start | bytes 786440 | tf_op jit(solution)/shard_map/ppermute | solution.py:347
  57.9 0.0 collective-permute-done.2
  57.9 0.1 add_convert_fusion.2
  58.1 0.7 collective-permute-start.3
  58.7 0.0 collective-permute-done.4
  58.8 1.0 add_convert_fusion
  59.8 4.8 %collective-permute-start.8 = (bf16[8,128,128]{2,1,0:T(8,128)(2,1)S(1)}, bf16[8,128,128]{2,1,0:T(8,128)(2,1)S(1)}, u32[]{:S(2)}, u32[]{:S(2)}) collective-permute-start(bf16[8,128,128]{2,1,0:T(8,128)(2,1)S(1)} %add_convert_fusion), channel_id=1, source_target_pairs={{0,4},{2,6},{4,0},{6,2},{8,12},{10,14},{12,8},{14,10},{1,5},{3,7},... | collective-permute-start | bytes 786440 | tf_op jit(solution)/shard_map/ppermute | solution.py:347
  64.6 6.6 %down_units.5.own_ref = f32[8,128,128]{2,1,0:T(8,128)S(1)} custom-call(s32[1]{0:T(128)} %bitcast.units, bf16[128,3584]{1,0:T(8,128)(2,1)S(1)} %bitcast.28, bf16[3584,8192]{1,0:T(8,128)(2,1)} %weight_ref.9, bf16[256,128]{1,0:T(8,128)(2,1)S(1)} %copy-done.3), custom_call_target="tpu_custom_call" | custom-call | flops 939524096 | bytes 7340032 | tf_op jit(solution)/shard_map/down_units/pallas_call | solution.py:176
  71.2 0.0 collective-permute-done.3.b_ref
  71.2 1.0 update.1.refs_0_
  72.2 0.1 select_reduce_fusion.1
  72.3 0.1 select_reduce_fusion
  72.4 0.7 collective-permute-start.13
  73.1 5.7 %collective-permute-done.9.refs_1_ = bf16[8,128,128]{2,1,0:T(8,128)(2,1)S(1)} collective-permute-done((bf16[8,128,128]{2,1,0:T(8,128)(2,1)}, bf16[8,128,128]{2,1,0:T(8,128)(2,1)S(1)}, u32[]{:S(2)}, u32[]{:S(2)}) %collective-permute-start.9) | collective-permute-done | bytes 262176 | tf_op jit(solution)/shard_map/ppermute | solution.py:347
  78.8 0.7 collective-permute-start.10
  80.2 1.3 %collective-permute-start.14 = (bf16[8,128,128]{2,1,0:T(8,128)(2,1)S(1)}, bf16[8,128,128]{2,1,0:T(8,128)(2,1)S(1)}, u32[]{:S(2)}, u32[]{:S(2)}) collective-permute-start(bf16[8,128,128]{2,1,0:T(8,128)(2,1)S(1)} %collective-permute-done.13), channel_id=1, source_target_pairs={{4,0},{6,2},{8,12},{10,14},{5,1},{7,3},{9,13},{11,15},{20,16},{22,... | collective-permute-start | bytes 786440 | tf_op jit(solution)/shard_map/ppermute | solution.py:347
  81.5 1.3 %collective-permute-start.11 = (bf16[8,128,128]{2,1,0:T(8,128)(2,1)S(1)}, bf16[8,128,128]{2,1,0:T(8,128)(2,1)S(1)}, u32[]{:S(2)}, u32[]{:S(2)}) collective-permute-start(bf16[8,128,128]{2,1,0:T(8,128)(2,1)S(1)} %collective-permute-done.10), channel_id=1, source_target_pairs={{4,0},{6,2},{8,12},{10,14},{5,1},{7,3},{9,13},{11,15},{20,16},{22,... | collective-permute-start | bytes 786440 | tf_op jit(solution)/shard_map/ppermute | solution.py:347
  82.8 0.3 fusion.2
  83.1 1.8 %collective-permute-start.17 = (bf16[8,128,128]{2,1,0:T(8,128)(2,1)}, bf16[8,128,128]{2,1,0:T(8,128)(2,1)S(1)}, u32[]{:S(2)}, u32[]{:S(2)}) collective-permute-start(bf16[8,128,128]{2,1,0:T(8,128)(2,1)} %update.1.refs_0_), channel_id=1, source_target_pairs={{0,2},{2,0},{4,6},{6,4},{8,10},{10,8},{12,14},{14,12},{1,3},{3,1},... | collective-permute-start | bytes 786440 | tf_op jit(solution)/shard_map/ppermute | solution.py:347
  84.9 0.1 pad_add_fusion.5.units
  84.9 0.3 collective-permute-start.16
  85.3 6.9 %collective-permute-done.14 = bf16[8,128,128]{2,1,0:T(8,128)(2,1)S(1)} collective-permute-done((bf16[8,128,128]{2,1,0:T(8,128)(2,1)S(1)}, bf16[8,128,128]{2,1,0:T(8,128)(2,1)S(1)}, u32[]{:S(2)}, u32[]{:S(2)}) %collective-permute-start.14) | collective-permute-done | bytes 262176 | tf_op jit(solution)/shard_map/ppermute | solution.py:347
  92.1 0.1 add.97.refs_1_
  92.2 1.3 %collective-permute-start.15 = (bf16[8,128,128]{2,1,0:T(8,128)(2,1)S(1)}, bf16[8,128,128]{2,1,0:T(8,128)(2,1)S(1)}, u32[]{:S(2)}, u32[]{:S(2)}) collective-permute-start(bf16[8,128,128]{2,1,0:T(8,128)(2,1)S(1)} %add.97.refs_1_), channel_id=1, source_target_pairs={{0,2},{2,0},{4,6},{6,4},{8,10},{10,8},{12,14},{14,12},{1,3},{3,1},... | collective-permute-start | bytes 786440 | tf_op jit(solution)/shard_map/ppermute | solution.py:347
  93.5 0.1 pad_add_fusion.4.units
  93.6 1.3 %collective-permute-done.11 = bf16[8,128,128]{2,1,0:T(8,128)(2,1)S(1)} collective-permute-done((bf16[8,128,128]{2,1,0:T(8,128)(2,1)S(1)}, bf16[8,128,128]{2,1,0:T(8,128)(2,1)S(1)}, u32[]{:S(2)}, u32[]{:S(2)}) %collective-permute-start.11) | collective-permute-done | bytes 262176 | tf_op jit(solution)/shard_map/ppermute | solution.py:347
  94.9 0.1 add.96.refs_1_
  95.0 1.3 %collective-permute-start.12 = (bf16[8,128,128]{2,1,0:T(8,128)(2,1)S(1)}, bf16[8,128,128]{2,1,0:T(8,128)(2,1)S(1)}, u32[]{:S(2)}, u32[]{:S(2)}) collective-permute-start(bf16[8,128,128]{2,1,0:T(8,128)(2,1)S(1)} %add.96.refs_1_), channel_id=1, source_target_pairs={{0,2},{2,0},{4,6},{6,4},{8,10},{10,8},{12,14},{14,12},{1,3},{3,1},... | collective-permute-start | bytes 786440 | tf_op jit(solution)/shard_map/ppermute | solution.py:347
  96.3 0.1 pad_add_fusion.3.units
  96.4 5.8 %copy-done = bf16[1024,8192]{1,0:T(8,128)(2,1)S(1)} copy-done((bf16[1024,8192]{1,0:T(8,128)(2,1)S(1)}, bf16[1024,8192]{1,0:T(8,128)(2,1)}, u32[]{:S(2)}) %copy-start) | copy-done | bytes 16777240
  102.2 0.9 copy-done.5
  103.1 1.6 %query_units.5 = (f32[1024,128]{1,0:T(8,128)S(1)}, f32[128,128]{1,0:T(8,128)S(1)}) custom-call(s32[1]{0:T(128)} %bitcast.units, bf16[8,128,128]{2,1,0:T(8,128)(2,1)S(1)} %copy-done.5, f32[64,128]{1,0:T(8,128)S(1)} %bitcast.29, bf16[1024,8192]{1,0:T(8,128)(2,1)S(1)} %copy-done), custom_call_target="tpu_custom_call" | custom-call | flops 268435456 | bytes 2097152 | tf_op jit(solution)/shard_map/query_units/pallas_call | solution.py:307
  104.7 0.0 copy-start.1
  104.7 5.8 %copy-done.1 = bf16[1024,8192]{1,0:T(8,128)(2,1)S(1)} copy-done((bf16[1024,8192]{1,0:T(8,128)(2,1)S(1)}, bf16[1024,8192]{1,0:T(8,128)(2,1)}, u32[]{:S(2)}) %copy-start.1) | copy-done | bytes 16777240
  110.5 3.8 %query_units.6 = (f32[1024,128]{1,0:T(8,128)S(1)}, f32[128,128]{1,0:T(8,128)S(1)}) custom-call(s32[2]{0:T(128)S(1)} %pad_add_fusion.5.units, bf16[8,128,128]{2,1,0:T(8,128)(2,1)S(1)} %collective-permute-done.17.refs_0_, bf16[8,128,128]{2,1,0:T(8,128)(2,1)S(1)} %collective-permute-done.9.refs_1_, f32[64,128]{1,0:T(8,128)S(1)} %bitcast.30, ...), custom_call_target="tpu_custom_call" | custom-call | flops 536870912 | bytes 4194304 | tf_op jit(solution)/shard_map/query_units/pallas_call | solution.py:307
  114.3 0.0 slice-start.3
  114.3 3.8 %query_units.7 = (f32[1024,128]{1,0:T(8,128)S(1)}, f32[128,128]{1,0:T(8,128)S(1)}) custom-call(s32[2]{0:T(128)S(1)} %pad_add_fusion.4.units, bf16[8,128,128]{2,1,0:T(8,128)(2,1)S(1)} %collective-permute-done.16.refs_0_, bf16[8,128,128]{2,1,0:T(8,128)(2,1)S(1)} %add.97.refs_1_, f32[64,128]{1,0:T(8,128)S(1)} %bitcast.32, f32[64,128]{1,0:T(8,128)S(1)} %bitcast.33, ...), custom_call_target="tpu_custom_call" | custom-call | flops 536870912 | bytes 4194304 | tf_op jit(solution)/shard_map/query_units/pallas_call | solution.py:307
  118.2 3.8 %query_units.8 = (f32[1024,128]{1,0:T(8,128)S(1)}, f32[128,128]{1,0:T(8,128)S(1)}) custom-call(s32[2]{0:T(128)S(1)} %pad_add_fusion.3.units, bf16[8,128,128]{2,1,0:T(8,128)(2,1)S(1)} %collective-permute-done.15.refs_0_, bf16[8,128,128]{2,1,0:T(8,128)(2,1)S(1)} %add.96.refs_1_, f32[64,128]{1,0:T(8,128)S(1)} %bitcast.34, f32[64,128]{1,0:T(8,128)S(1)} %bitcast.35, ...), custom_call_target="tpu_custom_call" | custom-call | flops 536870912 | bytes 4194304 | tf_op jit(solution)/shard_map/query_units/pallas_call | solution.py:307
  122.0 3.0 %query_units.9 = bf16[1024,128]{1,0:T(8,128)(2,1)} custom-call(s32[1]{0:T(128)} %bitcast.10.units, bf16[8,128,128]{2,1,0:T(8,128)(2,1)S(1)} %collective-permute-done.12.refs_0_, f32[64,128]{1,0:T(8,128)S(1)} %bitcast.36, bf16[1024,8192]{1,0:T(8,128)(2,1)S(1)} %bitcast.23, f32[1024,128]{1,0:T(8,128)S(1)} %get-tuple-element.28.refs_3_, ...), custom_call_target="tpu_custom_call" | custom-call | flops 268435456 | bytes 2097152 | tf_op jit(solution)/shard_map/query_units/pallas_call | solution.py:307
  (28 shorter events, 0.1 us)
Async XLA Ops:
  0.6 10.8 %copy-start.3 = (bf16[256,128]{1,0:T(8,128)(2,1)S(1)}, bf16[256,128]{1,0:T(8,128)(2,1)}, u32[]{:S(2)}) copy-start(bf16[256,128]{1,0:T(8,128)(2,1)} %constant.70.signs_ref) | copy-start | bytes 196612
  2.1 0.8 copy-start.2
  8.4 26.8 %collective-permute-start.5 = (bf16[8,128,128]{2,1,0:T(8,128)(2,1)S(1)}, bf16[8,128,128]{2,1,0:T(8,128)(2,1)S(1)}, u32[]{:S(2)}, u32[]{:S(2)}) collective-permute-start(bf16[8,128,128]{2,1,0:T(8,128)(2,1)S(1)} %down_units.9), channel_id=1, source_target_pairs={{0,2},{2,0},{4,6},{6,4},{8,10},{10,8},{12,14},{14,12},{1,3},{3,1},... | collective-permute-start | bytes 786440 | tf_op jit(solution)/shard_map/ppermute | solution.py:347
  22.2 36.6 %collective-permute-start.4 = (bf16[8,128,128]{2,1,0:T(8,128)(2,1)S(1)}, bf16[8,128,128]{2,1,0:T(8,128)(2,1)}, u32[]{:S(2)}, u32[]{:S(2)}) collective-permute-start(bf16[8,128,128]{2,1,0:T(8,128)(2,1)S(1)} %get-tuple-element.20), channel_id=1, source_target_pairs={{0,2},{2,0},{4,6},{6,4},{8,10},{10,8},{12,14},{14,12},{1,3},{3,1},... | collective-permute-start | bytes 786440 | tf_op jit(solution)/shard_map/ppermute | solution.py:347
  33.1 7.8 %collective-permute-start.1 = (bf16[8,128,128]{2,1,0:T(8,128)(2,1)S(1)}, bf16[8,128,128]{2,1,0:T(8,128)(2,1)S(1)}, u32[]{:S(2)}, u32[]{:S(2)}) collective-permute-start(bf16[8,128,128]{2,1,0:T(8,128)(2,1)S(1)} %get-tuple-element.18), channel_id=1, source_target_pairs={{0,2},{2,0},{4,6},{6,4},{8,10},{10,8},{12,14},{14,12},{1,3},{3,1},... | collective-permute-start | bytes 786440 | tf_op jit(solution)/shard_map/ppermute | solution.py:347
  35.2 9.5 %collective-permute-start.6 = (bf16[8,128,128]{2,1,0:T(8,128)(2,1)S(1)}, bf16[8,128,128]{2,1,0:T(8,128)(2,1)S(1)}, u32[]{:S(2)}, u32[]{:S(2)}) collective-permute-start(bf16[8,128,128]{2,1,0:T(8,128)(2,1)S(1)} %fusion.1), channel_id=1, source_target_pairs={{0,4},{2,6},{12,8},{14,10},{1,5},{3,7},{13,9},{15,11},{16,20},{18,... | collective-permute-start | bytes 786440 | tf_op jit(solution)/shard_map/ppermute | solution.py:347
  41.0 17.0 %collective-permute-start.2 = (bf16[8,128,128]{2,1,0:T(8,128)(2,1)S(1)}, bf16[8,128,128]{2,1,0:T(8,128)(2,1)S(1)}, u32[]{:S(2)}, u32[]{:S(2)}) collective-permute-start(bf16[8,128,128]{2,1,0:T(8,128)(2,1)S(1)} %fusion), channel_id=1, source_target_pairs={{0,4},{2,6},{12,8},{14,10},{1,5},{3,7},{13,9},{15,11},{16,20},{18,... | collective-permute-start | bytes 786440 | tf_op jit(solution)/shard_map/ppermute | solution.py:347
  44.8 26.4 %copy-start.6 = (bf16[1,8,128,128]{3,2,1,0:T(8,128)(2,1)S(1)}, bf16[1,8,128,128]{3,2,1,0:T(8,128)(2,1)}, u32[]{:S(2)}) copy-start(bf16[1,8,128,128]{3,2,1,0:T(8,128)(2,1)} %param.10) | copy-start | bytes 786436
  44.8 27.4 %copy-start.7 = (s32[1,4]{1,0:T(1,128)S(1)}, s32[1,4]{1,0:T(1,128)}, u32[]{:S(2)}) copy-start(s32[1,4]{1,0:T(1,128)} %param.14) | copy-start | bytes 52
  44.8 51.6 %copy-start.4 = (f32[8192]{0:T(1024)S(1)}, f32[8192]{0:T(1024)}, u32[]{:S(2)}) copy-start(f32[8192]{0:T(1024)} %param.11) | copy-start | bytes 98308
  44.8 13.9 %collective-permute-start.7 = (bf16[8,128,128]{2,1,0:T(8,128)(2,1)S(1)}, bf16[8,128,128]{2,1,0:T(8,128)(2,1)S(1)}, u32[]{:S(2)}, u32[]{:S(2)}) collective-permute-start(bf16[8,128,128]{2,1,0:T(8,128)(2,1)S(1)} %add_convert_fusion.1), channel_id=1, source_target_pairs={{4,8},{6,10},{8,4},{10,6},{5,9},{7,11},{9,5},{11,7},{20,24},{22,26... | collective-permute-start | bytes 786440 | tf_op jit(solution)/shard_map/ppermute | solution.py:347
  56.4 14.8 %collective-permute-start = (bf16[8,128,128]{2,1,0:T(8,128)(2,1)S(1)}, bf16[8,128,128]{2,1,0:T(8,128)(2,1)S(1)}, u32[]{:S(2)}, u32[]{:S(2)}) collective-permute-start(bf16[8,128,128]{2,1,0:T(8,128)(2,1)S(1)} %get-tuple-element.16), channel_id=1, source_target_pairs={{0,2},{2,0},{4,6},{6,4},{8,10},{10,8},{12,14},{14,12},{1,3},{3,1},... | collective-permute-start | bytes 786440 | tf_op jit(solution)/shard_map/ppermute | solution.py:347
  58.1 13.1 %collective-permute-start.3 = (bf16[8,128,128]{2,1,0:T(8,128)(2,1)S(1)}, bf16[8,128,128]{2,1,0:T(8,128)(2,1)S(1)}, u32[]{:S(2)}, u32[]{:S(2)}) collective-permute-start(bf16[8,128,128]{2,1,0:T(8,128)(2,1)S(1)} %add_convert_fusion.2), channel_id=1, source_target_pairs={{4,8},{6,10},{8,4},{10,6},{5,9},{7,11},{9,5},{11,7},{20,24},{22,26... | collective-permute-start | bytes 786440 | tf_op jit(solution)/shard_map/ppermute | solution.py:347
  59.8 11.4 %collective-permute-start.8 = (bf16[8,128,128]{2,1,0:T(8,128)(2,1)S(1)}, bf16[8,128,128]{2,1,0:T(8,128)(2,1)S(1)}, u32[]{:S(2)}, u32[]{:S(2)}) collective-permute-start(bf16[8,128,128]{2,1,0:T(8,128)(2,1)S(1)} %add_convert_fusion), channel_id=1, source_target_pairs={{0,4},{2,6},{4,0},{6,2},{8,12},{10,14},{12,8},{14,10},{1,5},{3,7},... | collective-permute-start | bytes 786440 | tf_op jit(solution)/shard_map/ppermute | solution.py:347
  64.6 57.4 %slice-start = ((s8[16777216]{0:T(1024)(128)(4,1)}), s8[4194304]{0:T(1024)(128)(4,1)S(1)}, s32[]{:S(2)}) async-start(s8[16777216]{0:T(1024)(128)(4,1)} %bitcast.22), calls=%async_computation | async-start | bytes 8388608
  64.6 57.5 %slice-start.1 = ((s8[16777216]{0:T(1024)(128)(4,1)}), s8[4194304]{0:T(1024)(128)(4,1)S(1)}, s32[]{:S(2)}) async-start(s8[16777216]{0:T(1024)(128)(4,1)} %bitcast.22), calls=%async_computation.1 | async-start | bytes 8388608
  72.2 6.6 %collective-permute-start.9 = (bf16[8,128,128]{2,1,0:T(8,128)(2,1)}, bf16[8,128,128]{2,1,0:T(8,128)(2,1)S(1)}, u32[]{:S(2)}, u32[]{:S(2)}) collective-permute-start(bf16[8,128,128]{2,1,0:T(8,128)(2,1)} %update.1.refs_0_), channel_id=1, source_target_pairs={{0,4},{2,6},{4,0},{6,2},{8,12},{10,14},{12,8},{14,10},{1,5},{3,7},... | collective-permute-start | bytes 786440 | tf_op jit(solution)/shard_map/ppermute | solution.py:347
  72.4 7.8 %collective-permute-start.13 = (bf16[8,128,128]{2,1,0:T(8,128)(2,1)}, bf16[8,128,128]{2,1,0:T(8,128)(2,1)S(1)}, u32[]{:S(2)}, u32[]{:S(2)}) collective-permute-start(bf16[8,128,128]{2,1,0:T(8,128)(2,1)} %update.1.refs_0_), channel_id=1, source_target_pairs={{4,8},{6,10},{8,4},{10,6},{5,9},{7,11},{9,5},{11,7},{20,24},{22,26... | collective-permute-start | bytes 786440 | tf_op jit(solution)/shard_map/ppermute | solution.py:347
  78.8 2.7 %collective-permute-start.10 = (bf16[8,128,128]{2,1,0:T(8,128)(2,1)S(1)}, bf16[8,128,128]{2,1,0:T(8,128)(2,1)S(1)}, u32[]{:S(2)}, u32[]{:S(2)}) collective-permute-start(bf16[8,128,128]{2,1,0:T(8,128)(2,1)S(1)} %collective-permute-done.9.refs_1_), channel_id=1, source_target_pairs={{4,8},{6,10},{8,4},{10,6},{5,9},{7,11},{9,5},{11,7},{20,24},{22,26... | collective-permute-start | bytes 786440 | tf_op jit(solution)/shard_map/ppermute | solution.py:347
  80.2 12.0 %collective-permute-start.14 = (bf16[8,128,128]{2,1,0:T(8,128)(2,1)S(1)}, bf16[8,128,128]{2,1,0:T(8,128)(2,1)S(1)}, u32[]{:S(2)}, u32[]{:S(2)}) collective-permute-start(bf16[8,128,128]{2,1,0:T(8,128)(2,1)S(1)} %collective-permute-done.13), channel_id=1, source_target_pairs={{4,0},{6,2},{8,12},{10,14},{5,1},{7,3},{9,13},{11,15},{20,16},{22,... | collective-permute-start | bytes 786440 | tf_op jit(solution)/shard_map/ppermute | solution.py:347
  81.5 13.4 %collective-permute-start.11 = (bf16[8,128,128]{2,1,0:T(8,128)(2,1)S(1)}, bf16[8,128,128]{2,1,0:T(8,128)(2,1)S(1)}, u32[]{:S(2)}, u32[]{:S(2)}) collective-permute-start(bf16[8,128,128]{2,1,0:T(8,128)(2,1)S(1)} %collective-permute-done.10), channel_id=1, source_target_pairs={{4,0},{6,2},{8,12},{10,14},{5,1},{7,3},{9,13},{11,15},{20,16},{22,... | collective-permute-start | bytes 786440 | tf_op jit(solution)/shard_map/ppermute | solution.py:347
  83.1 21.6 %collective-permute-start.17 = (bf16[8,128,128]{2,1,0:T(8,128)(2,1)}, bf16[8,128,128]{2,1,0:T(8,128)(2,1)S(1)}, u32[]{:S(2)}, u32[]{:S(2)}) collective-permute-start(bf16[8,128,128]{2,1,0:T(8,128)(2,1)} %update.1.refs_0_), channel_id=1, source_target_pairs={{0,2},{2,0},{4,6},{6,4},{8,10},{10,8},{12,14},{14,12},{1,3},{3,1},... | collective-permute-start | bytes 786440 | tf_op jit(solution)/shard_map/ppermute | solution.py:347
  84.9 29.4 %collective-permute-start.16 = (bf16[8,128,128]{2,1,0:T(8,128)(2,1)S(1)}, bf16[8,128,128]{2,1,0:T(8,128)(2,1)S(1)}, u32[]{:S(2)}, u32[]{:S(2)}) collective-permute-start(bf16[8,128,128]{2,1,0:T(8,128)(2,1)S(1)} %collective-permute-done.9.refs_1_), channel_id=1, source_target_pairs={{0,2},{2,0},{4,6},{6,4},{8,10},{10,8},{12,14},{14,12},{1,3},{3,1},... | collective-permute-start | bytes 786440 | tf_op jit(solution)/shard_map/ppermute | solution.py:347
  92.2 26.0 %collective-permute-start.15 = (bf16[8,128,128]{2,1,0:T(8,128)(2,1)S(1)}, bf16[8,128,128]{2,1,0:T(8,128)(2,1)S(1)}, u32[]{:S(2)}, u32[]{:S(2)}) collective-permute-start(bf16[8,128,128]{2,1,0:T(8,128)(2,1)S(1)} %add.97.refs_1_), channel_id=1, source_target_pairs={{0,2},{2,0},{4,6},{6,4},{8,10},{10,8},{12,14},{14,12},{1,3},{3,1},... | collective-permute-start | bytes 786440 | tf_op jit(solution)/shard_map/ppermute | solution.py:347
  95.0 27.0 %collective-permute-start.12 = (bf16[8,128,128]{2,1,0:T(8,128)(2,1)S(1)}, bf16[8,128,128]{2,1,0:T(8,128)(2,1)S(1)}, u32[]{:S(2)}, u32[]{:S(2)}) collective-permute-start(bf16[8,128,128]{2,1,0:T(8,128)(2,1)S(1)} %add.96.refs_1_), channel_id=1, source_target_pairs={{0,2},{2,0},{4,6},{6,4},{8,10},{10,8},{12,14},{14,12},{1,3},{3,1},... | collective-permute-start | bytes 786440 | tf_op jit(solution)/shard_map/ppermute | solution.py:347
  96.4 5.8 %copy-start = (bf16[1024,8192]{1,0:T(8,128)(2,1)S(1)}, bf16[1024,8192]{1,0:T(8,128)(2,1)}, u32[]{:S(2)}) copy-start(bf16[1024,8192]{1,0:T(8,128)(2,1)} %refs_2_.3) | copy-start | bytes 50331652
  102.2 0.9 copy-start.5
  103.1 18.9 %slice-start.2 = ((s8[16777216]{0:T(1024)(128)(4,1)}), s8[4194304]{0:T(1024)(128)(4,1)S(1)}, s32[]{:S(2)}) async-start(s8[16777216]{0:T(1024)(128)(4,1)} %bitcast.22), calls=%async_computation.2 | async-start | bytes 8388608
  104.7 5.8 %copy-start.1 = (bf16[1024,8192]{1,0:T(8,128)(2,1)S(1)}, bf16[1024,8192]{1,0:T(8,128)(2,1)}, u32[]{:S(2)}) copy-start(bf16[1024,8192]{1,0:T(8,128)(2,1)} %refs_2_.3) | copy-start | bytes 50331652
  114.3 7.7 %slice-start.3 = ((s8[16777216]{0:T(1024)(128)(4,1)}), s8[4194304]{0:T(1024)(128)(4,1)S(1)}, s32[]{:S(2)}) async-start(s8[16777216]{0:T(1024)(128)(4,1)} %bitcast.22), calls=%async_computation.3 | async-start | bytes 8388608

commit v2 on v0

--- a/solution.py
+++ b/solution.py
@@ -1,8 +1,11 @@
+import functools
 import math
 
 import jax
 import jax.numpy as jnp
 from jax import lax
+from jax.experimental import pallas as pl
+from jax.experimental.pallas import tpu as pltpu
 from jax.sharding import PartitionSpec as P
 
 HEAD = 128
@@ -14,6 +17,9 @@
 code_top = 448.0
 least_normal = 0.015625
 rope_base = 500000.0
+
+bf16 = jnp.bfloat16
+f32 = jnp.float32
 
 
 def hadamard_table(order_size):
@@ -25,6 +31,15 @@
         parity = parity + jnp.bitwise_and(jnp.right_shift(common, shift_bits), 1)
     sign_table = (1 - 2 * (parity % 2)).astype(jnp.float32)
     return sign_table / math.sqrt(order_size)
+
+
+def hadamard_signs():
+    row_ids = lax.broadcasted_iota(jnp.int32, (2 * HB, HB), 0)
+    col_ids = lax.broadcasted_iota(jnp.int32, (2 * HB, HB), 1)
+    common = jnp.bitwise_and(row_ids, col_ids)
+    for shift_bits in (4, 2, 1):
+        common = jnp.bitwise_xor(common, jnp.right_shift(common, shift_bits))
+    return (1 - 2 * jnp.bitwise_and(common, 1)).astype(f32).astype(bf16)
 
 
 def grid_code(scaled):
@@ -64,7 +79,7 @@
     return rotated_pairs.reshape(projected.shape)
 
 
-def local(hidden, down_weight, residual, norm_gain, query_weight, prefix_len, seg_lengths):
+def local_general(hidden, down_weight, residual, norm_gain, query_weight, prefix_len, seg_lengths):
     members = lax.axis_size("tensor")
     span_len = hidden.shape[2]
     model_width = down_weight.shape[1]
@@ -74,11 +89,10 @@
     item_total = splits * blocks
     per_device = item_total // members
     hadamard = hadamard_table(HB)
-    hidden_parts = hidden[0].reshape(hidden.shape[1], splits, piece_len)
-    weight_parts = down_weight.reshape(down_weight.shape[0], blocks, HB)
-    partial_value = jnp.einsum(
-        "fsc,fbh->sbch", hidden_parts, weight_parts, preferred_element_type=jnp.float32
+    partial_value = lax.dot_general(
+        hidden[0], down_weight, (((0,), (0,)), ((), ())), preferred_element_type=jnp.float32
     )
+    partial_value = partial_value.reshape(splits, piece_len, blocks, HB).transpose(0, 2, 1, 3)
     rotated = jnp.einsum("sbch,hk->sbck", partial_value, hadamard, precision=lax.Precision.HIGHEST)
     block_scale = (jnp.max(jnp.abs(rotated), axis=3, keepdims=True) + eps_scale) / code_top
     block_code = grid_code(rotated / block_scale).astype(jnp.bfloat16)
@@ -109,6 +123,309 @@
     return (updated[None], query_one[None])
 
 
+def split_dot(value, signs):
+    high = value.astype(bf16)
+    low = (value - high.astype(f32)).astype(bf16)
+    return jnp.dot(jnp.concatenate([high, low], axis=1), signs, preferred_element_type=f32)
+
+
+def coded(total, signs):
+    for j in range(total.shape[1] // HB):
+        rotated = split_dot(total[:, j * HB : (j + 1) * HB], signs)
+        top = jnp.max(jnp.abs(rotated), axis=1, keepdims=True) * (1.0 / math.sqrt(HB)) + eps_scale
+        scaled = rotated * ((code_top / math.sqrt(HB)) / top)
+        anchor = jnp.maximum(jnp.abs(scaled), least_normal) * (2.0**20 - 4.0)
+        code = (scaled + anchor) - anchor
+        yield code * (top * (1.0 / code_top))
+
+
+def down_kernel(count, first, chunk, units, *refs):
+    if first:
+        rows_ref, weight_ref, out, turned, signs_out, held, sems, held_rows, row_sem = refs
+        outs = [out]
+    else:
+        rows_ref, weight_ref, signs_ref, *outs, held, sems = refs
+    depth, width = held.shape[1:]
+    chunks = depth // chunk
+
+    def fetch(k, c):
+        here = pl.ds(c * chunk, chunk)
+        columns = pl.ds(pl.multiple_of(units[k] * width, width), width)
+        return pltpu.make_async_copy(weight_ref.at[here, columns], held.at[k, here], sems.at[k, c])
+
+    if first:
+        bring = pltpu.make_async_copy(rows_ref, held_rows, row_sem)
+        bring.start()
+    for k in range(count):
+        for c in range(chunks):
+            fetch(k, c).start()
+    if first:
+        signs = hadamard_signs()
+        signs_out[...] = signs
+        bring.wait()
+    else:
+        signs = signs_ref[...]
+    for k in range(count):
+        total = None
+        for c in range(chunks):
+            here = slice(c * chunk, (c + 1) * chunk)
+            if first:
+                rows = held_rows[here, :].T
+                turned[:, here] = rows
+            else:
+                rows = rows_ref[:, here]
+            fetch(k, c).wait()
+            product = jnp.dot(rows, held[k, here, :], preferred_element_type=f32)
+            total = product if total is None else total + product
+        for j, value in enumerate(coded(total, signs)):
+            outs[k][j] = value.astype(outs[k].dtype)
+
+
+def down_units(rows, down_weight, signs, units, dtypes):
+    count = len(dtypes)
+    first = signs is None
+    tokens, depth = rows.shape[::-1] if first else rows.shape
+    unit_width = down_weight.shape[1] // 8
+    chunk = 512 if depth % 512 == 0 else depth
+    vmem = pl.BlockSpec(memory_space=pltpu.VMEM)
+    hbm = pl.BlockSpec(memory_space=pltpu.HBM)
+    out_shape = [jax.ShapeDtypeStruct((unit_width // HB, tokens, HB), d) for d in dtypes]
+    scratch = [
+        pltpu.VMEM((count, depth, unit_width), bf16),
+        pltpu.SemaphoreType.DMA((count, depth // chunk)),
+    ]
+    if first:
+        out_shape.append(jax.ShapeDtypeStruct((tokens, depth), bf16))
+        out_shape.append(jax.ShapeDtypeStruct((2 * HB, HB), bf16))
+        scratch += [pltpu.VMEM((depth, tokens), bf16), pltpu.SemaphoreType.DMA]
+        args, in_specs = (rows, down_weight), [hbm, hbm]
+    else:
+        args, in_specs = (rows, down_weight, signs), [vmem, hbm, vmem]
+    return pl.pallas_call(
+        functools.partial(down_kernel, count, first, chunk),
+        in_specs=[pl.BlockSpec(memory_space=pltpu.SMEM), *in_specs],
+        out_specs=[vmem] * len(out_shape),
+        out_shape=out_shape,
+        scratch_shapes=scratch,
+        compiler_params=pltpu.CompilerParams(vmem_limit_bytes=(48 if first else 32) << 20),
+        cost_estimate=pl.CostEstimate(
+            flops=2 * tokens * depth * unit_width * count,
+            bytes_accessed=2 * depth * unit_width * count,
+            transcendentals=0,
+        ),
+        name="down_units",
+    )(jnp.stack(units), *args)
+
+
+def update_kernel(own_ref, a_ref, b_ref, c_ref, residual_ref, signs_ref, out_ref, turned_ref):
+    signs = signs_ref[...]
+    for j in range(own_ref.shape[0]):
+        summed = own_ref[j] + a_ref[j].astype(f32) + b_ref[j].astype(f32) + c_ref[j].astype(f32)
+        restored = split_dot(summed, signs) * (1.0 / math.sqrt(HB))
+        value = (residual_ref[j].astype(f32) + restored).astype(out_ref.dtype)
+        out_ref[j] = value
+        turned_ref[j] = value.T
+
+
+def update(own, a, b, c, residual, signs):
+    vmem = pl.BlockSpec(memory_space=pltpu.VMEM)
+    blocks, tokens, _ = residual.shape
+    return pl.pallas_call(
+        update_kernel,
+        in_specs=[vmem] * 6,
+        out_specs=[vmem, vmem],
+        out_shape=[
+            jax.ShapeDtypeStruct(residual.shape, residual.dtype),
+            jax.ShapeDtypeStruct((blocks, HB, tokens), residual.dtype),
+        ],
+        compiler_params=pltpu.CompilerParams(vmem_limit_bytes=24 << 20),
+        name="update",
+    )(own, a, b, c, residual, signs)
+
+
+def query_kernel(info, units, *refs):
+    count, chunk, first, last = (info[n] for n in ("count", "chunk", "first", "last"))
+    refs = list(refs)
+    streams = [refs.pop(0) for _ in range(count)]
+    gain_ref, weight_ref = refs.pop(0), refs.pop(0)
+    if not first:
+        acc_in, square_in = refs.pop(0), refs.pop(0)
+    if last:
+        cos_ref, sin_ref, out_ref, held, sems = refs
+    else:
+        acc_ref, square_ref, held, sems = refs
+    blocks, _, tokens = streams[0].shape
+    columns, width = held.shape[1:]
+    chunks = columns // chunk
+
+    def fetch(k, c):
+        here = pl.ds(c * chunk, chunk)
+        place = pl.ds(pl.multiple_of(units[k] * width, width), width)
+        return pltpu.make_async_copy(weight_ref.at[here, place], held.at[k, here], sems.at[k, c])
+
+    for c in range(chunks):
+        for k in range(count):
+            fetch(k, c).start()
+    squares = None if first else square_in[...]
+    factors = []
+    for k in range(count):
+        parts = []
+        gains = gain_ref[pl.ds(pl.multiple_of(units[k] * blocks, blocks), blocks), :].T
+        for j in range(blocks):
+            value = streams[k][j].astype(f32)
+            squares = value * value if squares is None else squares + value * value
+            parts.append((value * gains[:, j : j + 1]).astype(bf16))
+        factors.append(jnp.concatenate(parts, axis=0))
+    if last:
+        mean_square = jnp.sum(squares, axis=0, keepdims=True) * (1.0 / info["width"])
+        root = lax.rsqrt(mean_square + eps_norm)
+        even = lax.broadcasted_iota(jnp.int32, (HEAD, tokens), 0) % 2 == 0
+    else:
+        square_ref[...] = squares
+    for c in range(chunks):
+        here = slice(c * chunk, (c + 1) * chunk)
+        total = None if first else acc_in[here, :]
+        for k in range(count):
+            fetch(k, c).wait()
+            product = jnp.dot(held[k, here, :], factors[k], preferred_element_type=f32)
+            total = product if total is None else total + product
+        if not last:
+            acc_ref[here, :] = total
+            continue
+        for h in range(chunk // HEAD):
+            value = total[h * HEAD : (h + 1) * HEAD, :] * root
+            other = jnp.where(even, pltpu.roll(value, HEAD - 1, 0), pltpu.roll(value, 1, 0))
+            rotated = value * cos_ref[...] + other * sin_ref[...]
+            out_ref[c * chunk + h * HEAD : c * chunk + (h + 1) * HEAD, :] = rotated.astype(out_ref.dtype)
+
+
+def query_units(streams, units, gain, query_weight, carried=None, tables=None):
+    count = len(streams)
+    blocks, _, tokens = streams[0].shape
+    columns, width = query_weight.shape
+    unit_width = blocks * HB
+    chunk = 256
+    first, last = carried is None, tables is not None
+    info = dict(count=count, chunk=chunk, first=first, last=last, width=width)
+    vmem = pl.BlockSpec(memory_space=pltpu.VMEM)
+    args = [jnp.stack(units), *streams, gain, query_weight, *(carried or ()), *(tables or ())]
+    in_specs = [pl.BlockSpec(memory_space=pltpu.SMEM)] + [vmem] * (len(args) - 1)
+    in_specs[count + 2] = pl.BlockSpec(memory_space=pltpu.HBM)
+    if last:
+        out_specs, out_shape = vmem, jax.ShapeDtypeStruct((columns, tokens), bf16)
+    else:
+        out_specs = [vmem, vmem]
+        out_shape = [jax.ShapeDtypeStruct((columns, tokens), f32), jax.ShapeDtypeStruct((HB, tokens), f32)]
+    return pl.pallas_call(
+        functools.partial(query_kernel, info),
+        in_specs=in_specs,
+        out_specs=out_specs,
+        out_shape=out_shape,
+        scratch_shapes=[
+            pltpu.VMEM((count, columns, unit_width), bf16),
+            pltpu.SemaphoreType.DMA((count, columns // chunk)),
+        ],
+        compiler_params=pltpu.CompilerParams(vmem_limit_bytes=50 << 20),
+        cost_estimate=pl.CostEstimate(
+            flops=2 * tokens * columns * unit_width * count,
+            bytes_accessed=2 * columns * unit_width * count,
+            transcendentals=0,
+        ),
+        name="query_units",
+    )(*args)
+
+
+def rotary_tables(positions):
+    row_ids = jnp.arange(HEAD, dtype=jnp.int32)
+    inv_freq = jnp.exp((row_ids // 2).astype(f32) * (-2.0 * math.log(rope_base) / HEAD))
+    angles = inv_freq[:, None] * positions[None, :]
+    sign = jnp.where(row_ids % 2 == 0, -1.0, 1.0).astype(f32)
+    return jnp.cos(angles), jnp.sin(angles) * sign[:, None]
+
+
+def pairs_of(partner):
+    found = []
+    for z in range(4):
+        for x in range(2):
+            for core in range(2):
+                pz, px, pcore = partner(z, x, core)
+                found.append(((2 * z + x) * 2 + core, (2 * pz + px) * 2 + pcore))
+    return found
+
+
+ACROSS = pairs_of(lambda z, x, core: (z, 1 - x, core))
+TWINS = pairs_of(lambda z, x, core: (z ^ 1, x, core))
+MIDDLE = pairs_of(lambda z, x, core: (3 - z, x, core) if z in (1, 2) else (z, x, 1 - core))
+
+
+def after(*values):
+    return lax.optimization_barrier(values)
+
+
+def send(value, pairs):
+    return lax.ppermute(value.astype(bf16), ("tensor", "replica"), pairs)
+
+
+def local_eight(hidden, down_weight, residual, norm_gain, query_weight, prefix_len, seg_lengths):
+    place = lax.axis_index("tensor").astype(jnp.int32)
+    z, x = place // 2, place % 2
+    tokens = hidden.shape[2]
+    slot = [z, z ^ 1, jnp.where(z < 2, 2, 1), jnp.where(z < 2, 3, 0)]
+    mine = [2 * s + x for s in slot]
+    theirs = [2 * s + 1 - x for s in slot]
+    inner = (z == 1) | (z == 2)
+
+    def down(units, dtypes, rows):
+        return down_units(rows, down_weight, signs, units, dtypes)
+
+    def only(here, value):
+        return jnp.where(here, value, jnp.zeros_like(value))
+
+    out3, rows, signs = down_units(hidden[0], down_weight, None, [theirs[3]], [bf16])
+    got3 = send(out3, ACROSS)
+    own3, out2 = down([mine[3], theirs[2]], [f32, bf16], rows)
+    got2 = send(out2, ACROSS)
+    part3, rows = after((own3 + got3).astype(bf16), rows)
+    add3 = only(inner, send(part3, TWINS))
+    own2, out1 = down([mine[2], theirs[1]], [f32, bf16], rows)
+    got1 = send(out1, ACROSS)
+    part2 = (own2 + got2).astype(bf16)
+    add2 = only(inner, send(part2, TWINS))
+    part3 = (own3 + got3 + add3).astype(bf16)
+    part2, part3, rows = after(part2, part3, rows)
+    add1 = only(inner, send(part3, MIDDLE))
+    own1, out0 = down([mine[1], theirs[0]], [f32, bf16], rows)
+    got0 = send(out0, ACROSS)
+    part1 = (own1 + got1 + add1).astype(bf16)
+    part2 = only(inner, (own2 + got2 + add2).astype(bf16))
+    part1, part2, rows = after(part1, part2, rows)
+    from1 = send(part1, TWINS)
+    from2 = send(part2, MIDDLE)
+    own0, = down([mine[0]], [f32], rows)
+    updated, unit0 = update(own0, got0, from2, from1, residual[0], signs)
+
+    gain = norm_gain.reshape(-1, HB)
+    tables = rotary_tables(positions_of(prefix_len[0], seg_lengths[0], tokens))
+    unit1 = send(unit0, TWINS)
+    inner2 = send(unit0, MIDDLE)
+    side0 = send(unit0, ACROSS)
+    state = query_units([unit0], [mine[0]], gain, query_weight)
+    unit1, state = after(unit1, state)
+    inner3 = send(unit1, MIDDLE)
+    unit2 = jnp.where(inner, inner2, send(inner2, TWINS))
+    side1 = send(unit1, ACROSS)
+    state = query_units([side0, unit1], [theirs[0], mine[1]], gain, query_weight, state)
+    unit2, inner3, state = after(unit2, inner3, state)
+    unit3 = jnp.where(inner, inner3, send(inner3, TWINS))
+    side2 = send(unit2, ACROSS)
+    state = query_units([side1, unit2], [theirs[1], mine[2]], gain, query_weight, state)
+    unit3, state = after(unit3, state)
+    side3 = send(unit3, ACROSS)
+    state = query_units([side2, unit3], [theirs[2], mine[3]], gain, query_weight, state)
+    query_one = query_units([side3], [theirs[3]], gain, query_weight, state, tables)
+    return (updated[None], query_one[None])
+
+
 def solution(mesh):
     in_specs = (
         P(("groups", "replica"), "tensor", None),
@@ -123,4 +440,5 @@
         P(("groups", "replica"), "tensor", None, None),
         P(("groups", "replica"), "tensor", None),
     )
+    local = local_eight if mesh.shape["tensor"] == 8 and mesh.shape["replica"] == 2 else local_general
     return jax.shard_map(local, mesh=mesh, in_specs=in_specs, out_specs=out_specs, check_vma=False)

time: 249 us -> 80.5 us (0.32)
  waiting for transfers between devices: 96.5 us -> 4.11 us
  local copies, waits for them, and re-layouts: 73.5 us -> 1.19 us
  Pallas kernels: 0 us -> 46.4 us
  matrix products: 40 us -> 0 us
  starting transfers between devices: 12.2 us -> 25.5 us
  between operations: 14.8 us -> 1.71 us
  other arithmetic: 9.86 us -> 1.46 us
    reshape x1 -> x0, local copies, waits for them, and re-layouts: 71.9 us -> none  [local(): weight_parts = down_weight.reshape(down_weight.shape[0], blocks, HB)]
    all_to_all x2 -> x0, waiting for transfers between devices: 48.8 us -> none  [the longest x1 47.4 us: local(): lax.all_to_all(sent_codes, 'tensor', split_axis=0, concat_axis=0, tiled=T...]
    all_gather x1 -> x0, waiting for transfers between devices: 47.6 us -> none  [local(): gathered = lax.all_gather(updated, 'tensor', axis=0, tiled=True)]
    pallas_call x0 -> x11, Pallas kernels: none -> 46.4 us  [the longest x5 27.9 us: down_units(): pl.pallas_call(functools.partial(down_kernel, count, first, chunk), in_sp...]
    dot_general x4 -> x0, matrix products: 40 us -> none  [the longest x1 22.8 us: local(): jnp.einsum('fsc,fbh->sbch', hidden_parts, weight_parts, preferred_element...]
    ppermute x0 -> x18, starting transfers between devices: none -> 25.5 us  [send(): return lax.ppermute(value.astype(bf16), ('tensor', 'replica'), pairs)]
    all_to_all x2 -> x0, starting transfers between devices: 12 us -> none  [the longest x1 7.26 us: local(): lax.all_to_all(sent_scales.astype(jnp.bfloat16), 'tensor', split_axis=0,...]
    convert_element_type x3 -> x4, other arithmetic: 5.79 us -> 0.34 us  [the longest x1 0.12 us: local_eight(): part1 = (own1 + got1 + add1).astype(bf16)]
  transfers between devices with their start and end apart: 3 -> 18, of which waited for: 3 -> 5; matrix products, arithmetic and copies ran while one was open for 2% -> 2% of each run, Pallas kernels for 0% -> 48%
where the time goes in v2:
time: 80.5 us; the launch traced here: 80.3 us
  Pallas kernels  46.4 us (58%)
  starting transfers between devices  25.5 us (32%)
  waiting for transfers between devices  4.11 us (5%)
  between operations  1.71 us (2%)
  other arithmetic  1.46 us (2%)
  local copies, waits for them, and re-layouts  1.19 us (1%)
    pallas_call x5, Pallas kernels, down_units(): pl.pallas_call(functools.partial(down_kernel, count, first, chunk), in_sp...  27.9 us
    ppermute x18, starting transfers between devices, send(): return lax.ppermute(value.astype(bf16), ('tensor', 'replica'), pairs)  25.5 us
    pallas_call x5, Pallas kernels, query_units(): pl.pallas_call(functools.partial(query_kernel, info), in_specs=in_specs,...  17.4 us
    ppermute x18, waiting for transfers between devices, send(): return lax.ppermute(value.astype(bf16), ('tensor', 'replica'), pairs)  4.11 us
  transfers between devices with their start and end apart: 18, of which 5 were waited for; matrix products, arithmetic and copies ran while one was open for 2% of the time, Pallas kernels for 48%

profile of v2, /device:TPU:0, one launch (start us, length us, event | category | flops | bytes accessed | tf_op | source)
XLA Modules:
  0.0 80.3 jit_solution(601608831118069100)
XLA Ops:
  0.7 1.2 %copy-done = bf16[1,3584,128]{2,1,0:T(8,128)(2,1)S(1)} copy-done((bf16[1,3584,128]{2,1,0:T(8,128)(2,1)S(1)}, bf16[1,3584,128]{2,1,0:T(8,128)(2,1)}, u32[]{:S(2)}) %copy-start) | copy-done | bytes 917528
  1.8 4.1 %down_units.5 = (bf16[8,128,128]{2,1,0:T(8,128)(2,1)S(1)}, bf16[128,3584]{1,0:T(8,128)(2,1)S(1)}, bf16[256,128]{1,0:T(8,128)(2,1)S(1)}) custom-call(s32[1]{0:T(128)} %bitcast.7.units, bf16[3584,128]{1,0:T(8,128)(2,1)S(1)} %bitcast.20, bf16[3584,8192]{1,0:T(8,128)(2,1)} %refs_1_.9), custom_call_target="tpu_custom_call" | custom-call | flops 939524096 | bytes 7340032 | tf_op jit(solution)/shard_map/down_units/pallas_call | solution.py:204
  5.9 3.0 %collective-permute-start = (bf16[8,128,128]{2,1,0:T(8,128)(2,1)S(1)}, bf16[8,128,128]{2,1,0:T(8,128)(2,1)S(1)}, u32[]{:S(2)}, u32[]{:S(2)}) collective-permute-start(bf16[8,128,128]{2,1,0:T(8,128)(2,1)S(1)} %get-tuple-element.41), channel_id=1, source_target_pairs={{0,2},{1,3},{2,0},{3,1},{4,6},{5,7},{6,4},{7,5},{8,10},{9,11},{10,... | collective-permute-start | bytes 786440 | tf_op jit(solution)/shard_map/ppermute | solution.py:366
  8.9 0.1 pad_add_fusion.2.units
  9.0 6.6 %down_units.6 = (f32[8,128,128]{2,1,0:T(8,128)S(1)}, bf16[8,128,128]{2,1,0:T(8,128)(2,1)S(1)}) custom-call(s32[2]{0:T(128)S(1)} %pad_add_fusion.2.units, bf16[128,3584]{1,0:T(8,128)(2,1)S(1)} %get-tuple-element.50.refs_0_, bf16[3584,8192]{1,0:T(8,128)(2,1)} %refs_1_.9, bf16[256,128]{1,0:T(8,128)(2,1)S(1)} %get-tuple-element.39.refs_2_.signs_ref), custom_call_target="tpu_custom_call" | custom-call | flops 1879048192 | bytes 14680064 | tf_op jit(solution)/shard_map/down_units/pallas_call | solution.py:204
  15.6 0.1 collective-permute-start.1
  15.7 0.1 pad_add_fusion.units
  15.8 0.1 pad_add_fusion.1.units
  15.9 0.0 collective-permute-done
  15.9 0.1 fusion
  15.9 2.2 %collective-permute-start.2 = (bf16[8,128,128]{2,1,0:T(8,128)(2,1)S(1)}, bf16[8,128,128]{2,1,0:T(8,128)(2,1)S(1)}, u32[]{:S(2)}, u32[]{:S(2)}) collective-permute-start(bf16[8,128,128]{2,1,0:T(8,128)(2,1)S(1)} %fusion), channel_id=1, source_target_pairs={{0,4},{1,5},{2,6},{3,7},{4,0},{5,1},{6,2},{7,3},{8,12},{9,13},{10,... | collective-permute-start | bytes 786440 | tf_op jit(solution)/shard_map/ppermute | solution.py:366
  18.1 6.6 %down_units.7 = (f32[8,128,128]{2,1,0:T(8,128)S(1)}, bf16[8,128,128]{2,1,0:T(8,128)(2,1)S(1)}) custom-call(s32[2]{0:T(128)S(1)} %pad_add_fusion.1.units, bf16[128,3584]{1,0:T(8,128)(2,1)S(1)} %get-tuple-element.50.refs_0_, bf16[3584,8192]{1,0:T(8,128)(2,1)} %refs_1_.9, bf16[256,128]{1,0:T(8,128)(2,1)S(1)} %get-tuple-element.39.refs_2_.signs_ref), custom_call_target="tpu_custom_call" | custom-call | flops 1879048192 | bytes 14680064 | tf_op jit(solution)/shard_map/down_units/pallas_call | solution.py:204
  24.7 0.0 collective-permute-done.1
  24.7 0.1 fusion.1
  24.7 0.4 collective-permute-start.5
  25.2 1.6 %collective-permute-start.3 = (bf16[8,128,128]{2,1,0:T(8,128)(2,1)S(1)}, bf16[8,128,128]{2,1,0:T(8,128)(2,1)S(1)}, u32[]{:S(2)}, u32[]{:S(2)}) collective-permute-start(bf16[8,128,128]{2,1,0:T(8,128)(2,1)S(1)} %get-tuple-element.48), channel_id=1, source_target_pairs={{0,2},{1,3},{2,0},{3,1},{4,6},{5,7},{6,4},{7,5},{8,10},{9,11},{10,... | collective-permute-start | bytes 786440 | tf_op jit(solution)/shard_map/ppermute | solution.py:366
  26.8 0.0 collective-permute-done.2
  26.8 0.1 add_convert_fusion.2
  26.9 0.0 copy-start.2
  26.9 0.0 copy-start.3
  26.9 0.0 copy-start.1
  26.9 0.1 collective-permute-start.4
  27.0 6.8 %down_units.8 = (f32[8,128,128]{2,1,0:T(8,128)S(1)}, bf16[8,128,128]{2,1,0:T(8,128)(2,1)S(1)}) custom-call(s32[2]{0:T(128)S(1)} %pad_add_fusion.units, bf16[128,3584]{1,0:T(8,128)(2,1)S(1)} %get-tuple-element.50.refs_0_, bf16[3584,8192]{1,0:T(8,128)(2,1)} %refs_1_.9, bf16[256,128]{1,0:T(8,128)(2,1)S(1)} %get-tuple-element.39.refs_2_.signs_ref), custom_call_target="tpu_custom_call" | custom-call | flops 1879048192 | bytes 14680064 | tf_op jit(solution)/shard_map/down_units/pallas_call | solution.py:204
  33.8 0.5 collective-permute-start.6
  34.3 0.0 collective-permute-done.5
  34.3 0.1 fusion.2
  34.4 0.0 collective-permute-done.3
  34.4 0.0 collective-permute-done.4
  34.4 0.1 add_convert_fusion.1
  34.5 0.3 collective-permute-start.7
  34.8 3.5 %collective-permute-start.8 = (bf16[8,128,128]{2,1,0:T(8,128)(2,1)S(1)}, bf16[8,128,128]{2,1,0:T(8,128)(2,1)S(1)}, u32[]{:S(2)}, u32[]{:S(2)}) collective-permute-start(bf16[8,128,128]{2,1,0:T(8,128)(2,1)S(1)} %add_convert_fusion.1), channel_id=1, source_target_pairs={{0,4},{1,5},{2,6},{3,7},{4,0},{5,1},{6,2},{7,3},{8,12},{9,13},{10,... | collective-permute-start | bytes 786440 | tf_op jit(solution)/shard_map/ppermute | solution.py:366
  38.3 3.9 %down_units.9.own_ref = f32[8,128,128]{2,1,0:T(8,128)S(1)} custom-call(s32[1]{0:T(128)} %bitcast.units, bf16[128,3584]{1,0:T(8,128)(2,1)S(1)} %get-tuple-element.50.refs_0_, bf16[3584,8192]{1,0:T(8,128)(2,1)} %refs_1_.9, bf16[256,128]{1,0:T(8,128)(2,1)S(1)} %get-tuple-element.39.refs_2_.signs_ref), custom_call_target="tpu_custom_call" | custom-call | flops 939524096 | bytes 7340032 | tf_op jit(solution)/shard_map/down_units/pallas_call | solution.py:204
  42.2 0.4 collective-permute-done.6.a_ref
  42.5 0.0 collective-permute-done.7.b_ref
  42.5 0.8 collective-permute-done.8.c_ref
  43.3 1.0 %update.1 = (bf16[8,128,128]{2,1,0:T(8,128)(2,1)}, bf16[8,128,128]{2,1,0:T(8,128)(2,1)S(1)}) custom-call(f32[8,128,128]{2,1,0:T(8,128)S(1)} %down_units.9.own_ref, bf16[8,128,128]{2,1,0:T(8,128)(2,1)S(1)} %collective-permute-done.6.a_ref, bf16[8,128,128]{2,1,0:T(8,128)(2,1)S(1)} %collective-permute-done.7.b_ref, ...), custom_call_target="tpu_custom_call" | custom-call | tf_op jit(solution)/shard_map/update/pallas_call | solution.py:233
  44.3 0.0 collective-permute-start.9
  44.3 0.1 pad_add_fusion.3.units
  44.4 0.1 select_reduce_fusion.1
  44.5 1.6 %collective-permute-start.13 = (bf16[8,128,128]{2,1,0:T(8,128)(2,1)S(1)}, bf16[8,128,128]{2,1,0:T(8,128)(2,1)S(1)}, u32[]{:S(2)}, u32[]{:S(2)}) collective-permute-start(bf16[8,128,128]{2,1,0:T(8,128)(2,1)S(1)} %get-tuple-element.55.refs_0_), channel_id=1, source_target_pairs={{0,2},{1,3},{2,0},{3,1},{4,6},{5,7},{6,4},{7,5},{8,10},{9,11},{10,... | collective-permute-start | bytes 786440 | tf_op jit(solution)/shard_map/ppermute | solution.py:366
  46.1 3.0 %collective-permute-start.11 = (bf16[8,128,128]{2,1,0:T(8,128)(2,1)S(1)}, bf16[8,128,128]{2,1,0:T(8,128)(2,1)S(1)}, u32[]{:S(2)}, u32[]{:S(2)}) collective-permute-start(bf16[8,128,128]{2,1,0:T(8,128)(2,1)S(1)} %get-tuple-element.55.refs_0_), channel_id=1, source_target_pairs={{0,4},{1,5},{2,6},{3,7},{4,0},{5,1},{6,2},{7,3},{8,12},{9,13},{10,... | collective-permute-start | bytes 786440 | tf_op jit(solution)/shard_map/ppermute | solution.py:366
  49.1 0.1 pad_add_fusion.4.units
  49.8 0.0 collective-permute-done.9
  49.8 2.6 %collective-permute-start.10 = (bf16[8,128,128]{2,1,0:T(8,128)(2,1)S(1)}, bf16[8,128,128]{2,1,0:T(8,128)(2,1)S(1)}, u32[]{:S(2)}, u32[]{:S(2)}) collective-permute-start(bf16[8,128,128]{2,1,0:T(8,128)(2,1)S(1)} %collective-permute-done.9), channel_id=1, source_target_pairs={{0,4},{1,5},{2,6},{3,7},{4,0},{5,1},{6,2},{7,3},{8,12},{9,13},{10,... | collective-permute-start | bytes 786440 | tf_op jit(solution)/shard_map/ppermute | solution.py:366
  52.4 0.1 pad_add_fusion.5.units
  52.5 0.1 select_reduce_fusion
  52.5 2.2 %query_units.5 = (f32[1024,128]{1,0:T(8,128)S(1)}, f32[128,128]{1,0:T(8,128)S(1)}) custom-call(s32[1]{0:T(128)} %bitcast.units, bf16[8,128,128]{2,1,0:T(8,128)(2,1)S(1)} %get-tuple-element.55.refs_0_, f32[64,128]{1,0:T(8,128)S(1)} %bitcast.21, bf16[1024,8192]{1,0:T(8,128)(2,1)} %refs_2_.3), custom_call_target="tpu_custom_call" | custom-call | flops 268435456 | bytes 2097152 | tf_op jit(solution)/shard_map/query_units/pallas_call | solution.py:319
  54.8 1.5 %collective-permute-done.11.refs_1_ = bf16[8,128,128]{2,1,0:T(8,128)(2,1)S(1)} collective-permute-done((bf16[8,128,128]{2,1,0:T(8,128)(2,1)S(1)}, bf16[8,128,128]{2,1,0:T(8,128)(2,1)S(1)}, u32[]{:S(2)}, u32[]{:S(2)}) %collective-permute-start.11) | collective-permute-done | bytes 262176 | tf_op jit(solution)/shard_map/ppermute | solution.py:366
  56.3 0.5 collective-permute-start.15
  56.8 0.0 collective-permute-start.12
  56.8 0.0 collective-permute-done.13.refs_0_
  56.8 4.1 %query_units.6 = (f32[1024,128]{1,0:T(8,128)S(1)}, f32[128,128]{1,0:T(8,128)S(1)}) custom-call(s32[2]{0:T(128)S(1)} %pad_add_fusion.3.units, bf16[8,128,128]{2,1,0:T(8,128)(2,1)S(1)} %collective-permute-done.13.refs_0_, bf16[8,128,128]{2,1,0:T(8,128)(2,1)S(1)} %collective-permute-done.11.refs_1_, f32[64,128]{1,0:T(8,128)S(1)} %bitcast.22, ...), custom_call_target="tpu_custom_call" | custom-call | flops 536870912 | bytes 4194304 | tf_op jit(solution)/shard_map/query_units/pallas_call | solution.py:319
  60.9 0.0 collective-permute-done.10
  61.0 0.0 collective-permute-done.12
  61.0 3.5 %collective-permute-start.14 = (bf16[8,128,128]{2,1,0:T(8,128)(2,1)S(1)}, bf16[8,128,128]{2,1,0:T(8,128)(2,1)S(1)}, u32[]{:S(2)}, u32[]{:S(2)}) collective-permute-start(bf16[8,128,128]{2,1,0:T(8,128)(2,1)S(1)} %collective-permute-done.12), channel_id=1, source_target_pairs={{0,4},{1,5},{2,6},{3,7},{4,0},{5,1},{6,2},{7,3},{8,12},{9,13},{10,... | collective-permute-start | bytes 786440 | tf_op jit(solution)/shard_map/ppermute | solution.py:366
  64.5 2.0 %collective-permute-start.17 = (bf16[8,128,128]{2,1,0:T(8,128)(2,1)S(1)}, bf16[8,128,128]{2,1,0:T(8,128)(2,1)S(1)}, u32[]{:S(2)}, u32[]{:S(2)}) collective-permute-start(bf16[8,128,128]{2,1,0:T(8,128)(2,1)S(1)} %broadcast_select_fusion.refs_1_), channel_id=1, source_target_pairs={{0,2},{1,3},{2,0},{3,1},{4,6},{5,7},{6,4},{7,5},{8,10},{9,11},{10,... | collective-permute-start | bytes 786440 | tf_op jit(solution)/shard_map/ppermute | solution.py:366
  66.6 0.0 collective-permute-done.15.refs_0_
  66.6 4.1 %query_units.7 = (f32[1024,128]{1,0:T(8,128)S(1)}, f32[128,128]{1,0:T(8,128)S(1)}) custom-call(s32[2]{0:T(128)S(1)} %pad_add_fusion.4.units, bf16[8,128,128]{2,1,0:T(8,128)(2,1)S(1)} %collective-permute-done.15.refs_0_, bf16[8,128,128]{2,1,0:T(8,128)(2,1)S(1)} %broadcast_select_fusion.refs_1_, f32[64,128]{1,0:T(8,128)S(1)} %bitcast.23, ...), custom_call_target="tpu_custom_call" | custom-call | flops 536870912 | bytes 4194304 | tf_op jit(solution)/shard_map/query_units/pallas_call | solution.py:319
  70.7 0.7 collective-permute-start.16
  71.4 0.3 fusion.3
  71.7 0.1 collective-permute-done.17.refs_0_
  71.7 4.1 %query_units.8 = (f32[1024,128]{1,0:T(8,128)S(1)}, f32[128,128]{1,0:T(8,128)S(1)}) custom-call(s32[2]{0:T(128)S(1)} %pad_add_fusion.5.units, bf16[8,128,128]{2,1,0:T(8,128)(2,1)S(1)} %collective-permute-done.17.refs_0_, bf16[8,128,128]{2,1,0:T(8,128)(2,1)S(1)} %broadcast_select_fusion.1.refs_1_, f32[64,128]{1,0:T(8,128)S(1)} %bitcast.24, ...), custom_call_target="tpu_custom_call" | custom-call | flops 536870912 | bytes 4194304 | tf_op jit(solution)/shard_map/query_units/pallas_call | solution.py:319
  75.8 1.3 %collective-permute-done.16.refs_0_ = bf16[8,128,128]{2,1,0:T(8,128)(2,1)S(1)} collective-permute-done((bf16[8,128,128]{2,1,0:T(8,128)(2,1)S(1)}, bf16[8,128,128]{2,1,0:T(8,128)(2,1)S(1)}, u32[]{:S(2)}, u32[]{:S(2)}) %collective-permute-start.16) | collective-permute-done | bytes 262176 | tf_op jit(solution)/shard_map/ppermute | solution.py:366
  77.2 3.0 %query_units.9 = bf16[1024,128]{1,0:T(8,128)(2,1)} custom-call(s32[1]{0:T(128)} %bitcast.7.units, bf16[8,128,128]{2,1,0:T(8,128)(2,1)S(1)} %collective-permute-done.16.refs_0_, f32[64,128]{1,0:T(8,128)S(1)} %bitcast.25, bf16[1024,8192]{1,0:T(8,128)(2,1)} %refs_2_.3, f32[1024,128]{1,0:T(8,128)S(1)} %get-tuple-element.72.refs_3_, ...), custom_call_target="tpu_custom_call" | custom-call | flops 268435456 | bytes 2097152 | tf_op jit(solution)/shard_map/query_units/pallas_call | solution.py:319
  (10 shorter events, 0.1 us)
Async XLA Ops:
  0.7 1.2 %copy-start = (bf16[1,3584,128]{2,1,0:T(8,128)(2,1)S(1)}, bf16[1,3584,128]{2,1,0:T(8,128)(2,1)}, u32[]{:S(2)}) copy-start(bf16[1,3584,128]{2,1,0:T(8,128)(2,1)} %param.7) | copy-start | bytes 2752516
  5.9 9.9 %collective-permute-start = (bf16[8,128,128]{2,1,0:T(8,128)(2,1)S(1)}, bf16[8,128,128]{2,1,0:T(8,128)(2,1)S(1)}, u32[]{:S(2)}, u32[]{:S(2)}) collective-permute-start(bf16[8,128,128]{2,1,0:T(8,128)(2,1)S(1)} %get-tuple-element.41), channel_id=1, source_target_pairs={{0,2},{1,3},{2,0},{3,1},{4,6},{5,7},{6,4},{7,5},{8,10},{9,11},{10,... | collective-permute-start | bytes 786440 | tf_op jit(solution)/shard_map/ppermute | solution.py:366
  15.6 9.1 %collective-permute-start.1 = (bf16[8,128,128]{2,1,0:T(8,128)(2,1)S(1)}, bf16[8,128,128]{2,1,0:T(8,128)(2,1)S(1)}, u32[]{:S(2)}, u32[]{:S(2)}) collective-permute-start(bf16[8,128,128]{2,1,0:T(8,128)(2,1)S(1)} %get-tuple-element.44), channel_id=1, source_target_pairs={{0,2},{1,3},{2,0},{3,1},{4,6},{5,7},{6,4},{7,5},{8,10},{9,11},{10,... | collective-permute-start | bytes 786440 | tf_op jit(solution)/shard_map/ppermute | solution.py:366
  15.9 10.8 %collective-permute-start.2 = (bf16[8,128,128]{2,1,0:T(8,128)(2,1)S(1)}, bf16[8,128,128]{2,1,0:T(8,128)(2,1)S(1)}, u32[]{:S(2)}, u32[]{:S(2)}) collective-permute-start(bf16[8,128,128]{2,1,0:T(8,128)(2,1)S(1)} %fusion), channel_id=1, source_target_pairs={{0,4},{1,5},{2,6},{3,7},{4,0},{5,1},{6,2},{7,3},{8,12},{9,13},{10,... | collective-permute-start | bytes 786440 | tf_op jit(solution)/shard_map/ppermute | solution.py:366
  24.7 9.5 %collective-permute-start.5 = (bf16[8,128,128]{2,1,0:T(8,128)(2,1)S(1)}, bf16[8,128,128]{2,1,0:T(8,128)(2,1)S(1)}, u32[]{:S(2)}, u32[]{:S(2)}) collective-permute-start(bf16[8,128,128]{2,1,0:T(8,128)(2,1)S(1)} %fusion.1), channel_id=1, source_target_pairs={{0,4},{1,5},{2,6},{3,7},{4,0},{5,1},{6,2},{7,3},{8,12},{9,13},{10,... | collective-permute-start | bytes 786440 | tf_op jit(solution)/shard_map/ppermute | solution.py:366
  25.2 9.2 %collective-permute-start.3 = (bf16[8,128,128]{2,1,0:T(8,128)(2,1)S(1)}, bf16[8,128,128]{2,1,0:T(8,128)(2,1)S(1)}, u32[]{:S(2)}, u32[]{:S(2)}) collective-permute-start(bf16[8,128,128]{2,1,0:T(8,128)(2,1)S(1)} %get-tuple-element.48), channel_id=1, source_target_pairs={{0,2},{1,3},{2,0},{3,1},{4,6},{5,7},{6,4},{7,5},{8,10},{9,11},{10,... | collective-permute-start | bytes 786440 | tf_op jit(solution)/shard_map/ppermute | solution.py:366
  26.9 16.5 %copy-start.2 = (bf16[1,8,128,128]{3,2,1,0:T(8,128)(2,1)S(1)}, bf16[1,8,128,128]{3,2,1,0:T(8,128)(2,1)}, u32[]{:S(2)}) copy-start(bf16[1,8,128,128]{3,2,1,0:T(8,128)(2,1)} %param.9) | copy-start | bytes 786436
  26.9 17.5 %copy-start.3 = (s32[1,4]{1,0:T(1,128)S(1)}, s32[1,4]{1,0:T(1,128)}, u32[]{:S(2)}) copy-start(s32[1,4]{1,0:T(1,128)} %param.13) | copy-start | bytes 52
  26.9 25.7 %copy-start.1 = (f32[8192]{0:T(1024)S(1)}, f32[8192]{0:T(1024)}, u32[]{:S(2)}) copy-start(f32[8192]{0:T(1024)} %param.10) | copy-start | bytes 98308
  26.9 7.5 %collective-permute-start.4 = (bf16[8,128,128]{2,1,0:T(8,128)(2,1)S(1)}, bf16[8,128,128]{2,1,0:T(8,128)(2,1)S(1)}, u32[]{:S(2)}, u32[]{:S(2)}) collective-permute-start(bf16[8,128,128]{2,1,0:T(8,128)(2,1)S(1)} %add_convert_fusion.2), channel_id=1, source_target_pairs={{0,1},{1,0},{2,3},{3,2},{4,8},{5,9},{6,10},{7,11},{8,4},{9,5},{10,... | collective-permute-start | bytes 786440 | tf_op jit(solution)/shard_map/ppermute | solution.py:366
  33.8 8.8 %collective-permute-start.6 = (bf16[8,128,128]{2,1,0:T(8,128)(2,1)S(1)}, bf16[8,128,128]{2,1,0:T(8,128)(2,1)S(1)}, u32[]{:S(2)}, u32[]{:S(2)}) collective-permute-start(bf16[8,128,128]{2,1,0:T(8,128)(2,1)S(1)} %get-tuple-element.51), channel_id=1, source_target_pairs={{0,2},{1,3},{2,0},{3,1},{4,6},{5,7},{6,4},{7,5},{8,10},{9,11},{10,... | collective-permute-start | bytes 786440 | tf_op jit(solution)/shard_map/ppermute | solution.py:366
  34.5 8.0 %collective-permute-start.7 = (bf16[8,128,128]{2,1,0:T(8,128)(2,1)S(1)}, bf16[8,128,128]{2,1,0:T(8,128)(2,1)S(1)}, u32[]{:S(2)}, u32[]{:S(2)}) collective-permute-start(bf16[8,128,128]{2,1,0:T(8,128)(2,1)S(1)} %fusion.2), channel_id=1, source_target_pairs={{0,1},{1,0},{2,3},{3,2},{4,8},{5,9},{6,10},{7,11},{8,4},{9,5},{10,... | collective-permute-start | bytes 786440 | tf_op jit(solution)/shard_map/ppermute | solution.py:366
  34.8 8.5 %collective-permute-start.8 = (bf16[8,128,128]{2,1,0:T(8,128)(2,1)S(1)}, bf16[8,128,128]{2,1,0:T(8,128)(2,1)S(1)}, u32[]{:S(2)}, u32[]{:S(2)}) collective-permute-start(bf16[8,128,128]{2,1,0:T(8,128)(2,1)S(1)} %add_convert_fusion.1), channel_id=1, source_target_pairs={{0,4},{1,5},{2,6},{3,7},{4,0},{5,1},{6,2},{7,3},{8,12},{9,13},{10,... | collective-permute-start | bytes 786440 | tf_op jit(solution)/shard_map/ppermute | solution.py:366
  44.3 5.5 %collective-permute-start.9 = (bf16[8,128,128]{2,1,0:T(8,128)(2,1)S(1)}, bf16[8,128,128]{2,1,0:T(8,128)(2,1)S(1)}, u32[]{:S(2)}, u32[]{:S(2)}) collective-permute-start(bf16[8,128,128]{2,1,0:T(8,128)(2,1)S(1)} %get-tuple-element.55.refs_0_), channel_id=1, source_target_pairs={{0,1},{1,0},{2,3},{3,2},{4,8},{5,9},{6,10},{7,11},{8,4},{9,5},{10,... | collective-permute-start | bytes 786440 | tf_op jit(solution)/shard_map/ppermute | solution.py:366
  44.5 12.3 %collective-permute-start.13 = (bf16[8,128,128]{2,1,0:T(8,128)(2,1)S(1)}, bf16[8,128,128]{2,1,0:T(8,128)(2,1)S(1)}, u32[]{:S(2)}, u32[]{:S(2)}) collective-permute-start(bf16[8,128,128]{2,1,0:T(8,128)(2,1)S(1)} %get-tuple-element.55.refs_0_), channel_id=1, source_target_pairs={{0,2},{1,3},{2,0},{3,1},{4,6},{5,7},{6,4},{7,5},{8,10},{9,11},{10,... | collective-permute-start | bytes 786440 | tf_op jit(solution)/shard_map/ppermute | solution.py:366
  46.1 10.2 %collective-permute-start.11 = (bf16[8,128,128]{2,1,0:T(8,128)(2,1)S(1)}, bf16[8,128,128]{2,1,0:T(8,128)(2,1)S(1)}, u32[]{:S(2)}, u32[]{:S(2)}) collective-permute-start(bf16[8,128,128]{2,1,0:T(8,128)(2,1)S(1)} %get-tuple-element.55.refs_0_), channel_id=1, source_target_pairs={{0,4},{1,5},{2,6},{3,7},{4,0},{5,1},{6,2},{7,3},{8,12},{9,13},{10,... | collective-permute-start | bytes 786440 | tf_op jit(solution)/shard_map/ppermute | solution.py:366
  49.8 11.1 %collective-permute-start.10 = (bf16[8,128,128]{2,1,0:T(8,128)(2,1)S(1)}, bf16[8,128,128]{2,1,0:T(8,128)(2,1)S(1)}, u32[]{:S(2)}, u32[]{:S(2)}) collective-permute-start(bf16[8,128,128]{2,1,0:T(8,128)(2,1)S(1)} %collective-permute-done.9), channel_id=1, source_target_pairs={{0,4},{1,5},{2,6},{3,7},{4,0},{5,1},{6,2},{7,3},{8,12},{9,13},{10,... | collective-permute-start | bytes 786440 | tf_op jit(solution)/shard_map/ppermute | solution.py:366
  56.3 10.3 %collective-permute-start.15 = (bf16[8,128,128]{2,1,0:T(8,128)(2,1)S(1)}, bf16[8,128,128]{2,1,0:T(8,128)(2,1)S(1)}, u32[]{:S(2)}, u32[]{:S(2)}) collective-permute-start(bf16[8,128,128]{2,1,0:T(8,128)(2,1)S(1)} %collective-permute-done.11.refs_1_), channel_id=1, source_target_pairs={{0,2},{1,3},{2,0},{3,1},{4,6},{5,7},{6,4},{7,5},{8,10},{9,11},{10,... | collective-permute-start | bytes 786440 | tf_op jit(solution)/shard_map/ppermute | solution.py:366
  56.8 4.2 %collective-permute-start.12 = (bf16[8,128,128]{2,1,0:T(8,128)(2,1)S(1)}, bf16[8,128,128]{2,1,0:T(8,128)(2,1)S(1)}, u32[]{:S(2)}, u32[]{:S(2)}) collective-permute-start(bf16[8,128,128]{2,1,0:T(8,128)(2,1)S(1)} %collective-permute-done.11.refs_1_), channel_id=1, source_target_pairs={{0,1},{1,0},{2,3},{3,2},{4,8},{5,9},{6,10},{7,11},{8,4},{9,5},{10,... | collective-permute-start | bytes 786440 | tf_op jit(solution)/shard_map/ppermute | solution.py:366
  61.0 9.7 %collective-permute-start.14 = (bf16[8,128,128]{2,1,0:T(8,128)(2,1)S(1)}, bf16[8,128,128]{2,1,0:T(8,128)(2,1)S(1)}, u32[]{:S(2)}, u32[]{:S(2)}) collective-permute-start(bf16[8,128,128]{2,1,0:T(8,128)(2,1)S(1)} %collective-permute-done.12), channel_id=1, source_target_pairs={{0,4},{1,5},{2,6},{3,7},{4,0},{5,1},{6,2},{7,3},{8,12},{9,13},{10,... | collective-permute-start | bytes 786440 | tf_op jit(solution)/shard_map/ppermute | solution.py:366
  64.5 7.2 %collective-permute-start.17 = (bf16[8,128,128]{2,1,0:T(8,128)(2,1)S(1)}, bf16[8,128,128]{2,1,0:T(8,128)(2,1)S(1)}, u32[]{:S(2)}, u32[]{:S(2)}) collective-permute-start(bf16[8,128,128]{2,1,0:T(8,128)(2,1)S(1)} %broadcast_select_fusion.refs_1_), channel_id=1, source_target_pairs={{0,2},{1,3},{2,0},{3,1},{4,6},{5,7},{6,4},{7,5},{8,10},{9,11},{10,... | collective-permute-start | bytes 786440 | tf_op jit(solution)/shard_map/ppermute | solution.py:366
  70.7 6.4 %collective-permute-start.16 = (bf16[8,128,128]{2,1,0:T(8,128)(2,1)S(1)}, bf16[8,128,128]{2,1,0:T(8,128)(2,1)S(1)}, u32[]{:S(2)}, u32[]{:S(2)}) collective-permute-start(bf16[8,128,128]{2,1,0:T(8,128)(2,1)S(1)} %broadcast_select_fusion.1.refs_1_), channel_id=1, source_target_pairs={{0,2},{1,3},{2,0},{3,1},{4,6},{5,7},{6,4},{7,5},{8,10},{9,11},{10,... | collective-permute-start | bytes 786440 | tf_op jit(solution)/shard_map/ppermute | solution.py:366

commit v3 on v2

--- a/solution.py
+++ b/solution.py
@@ -139,7 +139,21 @@
         yield code * (top * (1.0 / code_top))
 
 
-def down_kernel(count, first, chunk, units, *refs):
+def next_fetches(weight_ref, units, places, outs, sems):
+    width = outs[0].shape[1]
+    return [
+        pltpu.make_async_copy(
+            weight_ref.at[:, pl.ds(pl.multiple_of(units[p] * width, width), width)], out, sems.at[k]
+        )
+        for k, (p, out) in enumerate(zip(places, outs))
+    ]
+
+
+def down_kernel(count, first, later, chunk, units, *refs):
+    if later:
+        *refs, ahead, held, sems, ahead_sems = refs
+        query_ref, *refs = refs
+        refs = [*refs, held, sems]
     if first:
         rows_ref, weight_ref, out, turned, signs_out, held, sems, held_rows, row_sem = refs
         outs = [out]
@@ -159,6 +173,9 @@
     for k in range(count):
         for c in range(chunks):
             fetch(k, c).start()
+    coming = next_fetches(query_ref, units, [count], [ahead], ahead_sems) if later else []
+    for copy in coming:
+        copy.start()
     if first:
         signs = hadamard_signs()
         signs_out[...] = signs
@@ -179,9 +196,11 @@
             total = product if total is None else total + product
         for j, value in enumerate(coded(total, signs)):
             outs[k][j] = value.astype(outs[k].dtype)
-
-
-def down_units(rows, down_weight, signs, units, dtypes):
+    for copy in coming:
+        copy.wait()
+
+
+def down_units(rows, down_weight, signs, units, dtypes, query_weight=None, later=None):
     count = len(dtypes)
     first = signs is None
     tokens, depth = rows.shape[::-1] if first else rows.shape
@@ -201,13 +220,18 @@
         args, in_specs = (rows, down_weight), [hbm, hbm]
     else:
         args, in_specs = (rows, down_weight, signs), [vmem, hbm, vmem]
+    if later is not None:
+        args, in_specs = (query_weight, *args), [hbm, *in_specs]
+        units = [*units, later]
+        out_shape.append(jax.ShapeDtypeStruct((query_weight.shape[0], unit_width), bf16))
+        scratch.append(pltpu.SemaphoreType.DMA((1,)))
     return pl.pallas_call(
-        functools.partial(down_kernel, count, first, chunk),
+        functools.partial(down_kernel, count, first, later is not None, chunk),
         in_specs=[pl.BlockSpec(memory_space=pltpu.SMEM), *in_specs],
         out_specs=[vmem] * len(out_shape),
         out_shape=out_shape,
         scratch_shapes=scratch,
-        compiler_params=pltpu.CompilerParams(vmem_limit_bytes=(48 if first else 32) << 20),
+        compiler_params=pltpu.CompilerParams(vmem_limit_bytes=(48 if first or later is not None else 32) << 20),
         cost_estimate=pl.CostEstimate(
             flops=2 * tokens * depth * unit_width * count,
             bytes_accessed=2 * depth * unit_width * count,
@@ -217,22 +241,25 @@
     )(jnp.stack(units), *args)
 
 
-def update_kernel(own_ref, a_ref, b_ref, c_ref, residual_ref, signs_ref, out_ref, turned_ref):
+def update_kernel(own_ref, *refs):
+    *terms, residual_ref, signs_ref, out_ref, turned_ref = refs
     signs = signs_ref[...]
     for j in range(own_ref.shape[0]):
-        summed = own_ref[j] + a_ref[j].astype(f32) + b_ref[j].astype(f32) + c_ref[j].astype(f32)
+        summed = own_ref[j]
+        for term in terms:
+            summed = summed + term[j].astype(f32)
         restored = split_dot(summed, signs) * (1.0 / math.sqrt(HB))
         value = (residual_ref[j].astype(f32) + restored).astype(out_ref.dtype)
         out_ref[j] = value
         turned_ref[j] = value.T
 
 
-def update(own, a, b, c, residual, signs):
+def update(own, terms, residual, signs):
     vmem = pl.BlockSpec(memory_space=pltpu.VMEM)
     blocks, tokens, _ = residual.shape
     return pl.pallas_call(
         update_kernel,
-        in_specs=[vmem] * 6,
+        in_specs=[vmem] * (len(terms) + 3),
         out_specs=[vmem, vmem],
         out_shape=[
             jax.ShapeDtypeStruct(residual.shape, residual.dtype),
@@ -240,32 +267,29 @@
         ],
         compiler_params=pltpu.CompilerParams(vmem_limit_bytes=24 << 20),
         name="update",
-    )(own, a, b, c, residual, signs)
+    )(own, *terms, residual, signs)
 
 
 def query_kernel(info, units, *refs):
-    count, chunk, first, last = (info[n] for n in ("count", "chunk", "first", "last"))
+    count, chunk, first, last, following = (info[n] for n in ("count", "chunk", "first", "last", "following"))
     refs = list(refs)
     streams = [refs.pop(0) for _ in range(count)]
-    gain_ref, weight_ref = refs.pop(0), refs.pop(0)
+    gain_ref = refs.pop(0)
+    now = [refs.pop(0) for _ in range(count)]
+    if not last:
+        weight_ref = refs.pop(0)
     if not first:
         acc_in, square_in = refs.pop(0), refs.pop(0)
     if last:
-        cos_ref, sin_ref, out_ref, held, sems = refs
-    else:
-        acc_ref, square_ref, held, sems = refs
+        cos_ref, sin_ref, out_ref = refs
+    else:
+        acc_ref, square_ref, *ahead, sems = refs
+        coming = next_fetches(weight_ref, units, range(count, count + following), ahead, sems)
+        for copy in coming:
+            copy.start()
     blocks, _, tokens = streams[0].shape
-    columns, width = held.shape[1:]
-    chunks = columns // chunk
-
-    def fetch(k, c):
-        here = pl.ds(c * chunk, chunk)
-        place = pl.ds(pl.multiple_of(units[k] * width, width), width)
-        return pltpu.make_async_copy(weight_ref.at[here, place], held.at[k, here], sems.at[k, c])
-
-    for c in range(chunks):
-        for k in range(count):
-            fetch(k, c).start()
+    width = blocks * HB
+    chunks = now[0].shape[0] // chunk
     squares = None if first else square_in[...]
     factors = []
     for k in range(count):
@@ -286,8 +310,7 @@
         here = slice(c * chunk, (c + 1) * chunk)
         total = None if first else acc_in[here, :]
         for k in range(count):
-            fetch(k, c).wait()
-            product = jnp.dot(held[k, here, :], factors[k], preferred_element_type=f32)
+            product = jnp.dot(now[k][here, :], factors[k], preferred_element_type=f32)
             total = product if total is None else total + product
         if not last:
             acc_ref[here, :] = total
@@ -297,42 +320,48 @@
             other = jnp.where(even, pltpu.roll(value, HEAD - 1, 0), pltpu.roll(value, 1, 0))
             rotated = value * cos_ref[...] + other * sin_ref[...]
             out_ref[c * chunk + h * HEAD : c * chunk + (h + 1) * HEAD, :] = rotated.astype(out_ref.dtype)
-
-
-def query_units(streams, units, gain, query_weight, carried=None, tables=None):
-    count = len(streams)
+    if not last:
+        for copy in coming:
+            copy.wait()
+
+
+def query_units(streams, units, later, gain, query_weight, ahead, carried=None, tables=None):
+    count, following = len(streams), len(later)
     blocks, _, tokens = streams[0].shape
     columns, width = query_weight.shape
     unit_width = blocks * HB
-    chunk = 256
     first, last = carried is None, tables is not None
-    info = dict(count=count, chunk=chunk, first=first, last=last, width=width)
+    info = dict(count=count, chunk=512, first=first, last=last, following=following, width=width)
     vmem = pl.BlockSpec(memory_space=pltpu.VMEM)
-    args = [jnp.stack(units), *streams, gain, query_weight, *(carried or ()), *(tables or ())]
-    in_specs = [pl.BlockSpec(memory_space=pltpu.SMEM)] + [vmem] * (len(args) - 1)
-    in_specs[count + 2] = pl.BlockSpec(memory_space=pltpu.HBM)
+    args = [jnp.stack([*units, *later]), *streams, gain, *ahead]
+    in_specs = [pl.BlockSpec(memory_space=pltpu.SMEM)] + [vmem] * (2 * count + 1)
+    if not last:
+        args.append(query_weight)
+        in_specs.append(pl.BlockSpec(memory_space=pltpu.HBM))
+    rest = [*(carried or ()), *(tables or ())]
     if last:
-        out_specs, out_shape = vmem, jax.ShapeDtypeStruct((columns, tokens), bf16)
-    else:
-        out_specs = [vmem, vmem]
-        out_shape = [jax.ShapeDtypeStruct((columns, tokens), f32), jax.ShapeDtypeStruct((HB, tokens), f32)]
+        out_shape, scratch = [jax.ShapeDtypeStruct((columns, tokens), bf16)], []
+    else:
+        out_shape = [
+            jax.ShapeDtypeStruct((columns, tokens), f32),
+            jax.ShapeDtypeStruct((HB, tokens), f32),
+        ]
+        out_shape += [jax.ShapeDtypeStruct((columns, unit_width), bf16)] * following
+        scratch = [pltpu.SemaphoreType.DMA((following,))]
     return pl.pallas_call(
         functools.partial(query_kernel, info),
-        in_specs=in_specs,
-        out_specs=out_specs,
+        in_specs=in_specs + [vmem] * len(rest),
+        out_specs=[vmem] * len(out_shape),
         out_shape=out_shape,
-        scratch_shapes=[
-            pltpu.VMEM((count, columns, unit_width), bf16),
-            pltpu.SemaphoreType.DMA((count, columns // chunk)),
-        ],
-        compiler_params=pltpu.CompilerParams(vmem_limit_bytes=50 << 20),
+        scratch_shapes=scratch,
+        compiler_params=pltpu.CompilerParams(vmem_limit_bytes=42 << 20),
         cost_estimate=pl.CostEstimate(
             flops=2 * tokens * columns * unit_width * count,
             bytes_accessed=2 * columns * unit_width * count,
             transcendentals=0,
         ),
         name="query_units",
-    )(*args)
+    )(*args, *rest)
 
 
 def rotary_tables(positions):
@@ -401,28 +430,33 @@
     part1, part2, rows = after(part1, part2, rows)
     from1 = send(part1, TWINS)
     from2 = send(part2, MIDDLE)
-    own0, = down([mine[0]], [f32], rows)
-    updated, unit0 = update(own0, got0, from2, from1, residual[0], signs)
+    own0, *ahead = down_units(rows, down_weight, signs, [mine[0]], [f32], query_weight, mine[0])
+    updated, unit0 = update(own0, [got0, from2, from1], residual[0], signs)
 
     gain = norm_gain.reshape(-1, HB)
     tables = rotary_tables(positions_of(prefix_len[0], seg_lengths[0], tokens))
+
+    def query(streams, units, later, ahead, state=None):
+        acc, square, *ahead = query_units(streams, units, later, gain, query_weight, ahead, state)
+        return (acc, square), ahead
+
+    side0 = send(unit0, ACROSS)
     unit1 = send(unit0, TWINS)
     inner2 = send(unit0, MIDDLE)
-    side0 = send(unit0, ACROSS)
-    state = query_units([unit0], [mine[0]], gain, query_weight)
+    state, ahead = query([unit0], [mine[0]], [theirs[0], mine[1]], ahead)
     unit1, state = after(unit1, state)
+    side1 = send(unit1, ACROSS)
     inner3 = send(unit1, MIDDLE)
     unit2 = jnp.where(inner, inner2, send(inner2, TWINS))
-    side1 = send(unit1, ACROSS)
-    state = query_units([side0, unit1], [theirs[0], mine[1]], gain, query_weight, state)
-    unit2, inner3, state = after(unit2, inner3, state)
+    state, ahead = query([side0, unit1], [theirs[0], mine[1]], [theirs[1], mine[2]], ahead, state)
+    inner3, state = after(inner3, state)
     unit3 = jnp.where(inner, inner3, send(inner3, TWINS))
     side2 = send(unit2, ACROSS)
-    state = query_units([side1, unit2], [theirs[1], mine[2]], gain, query_weight, state)
+    state, ahead = query([side1, unit2], [theirs[1], mine[2]], [theirs[2], mine[3]], ahead, state)
     unit3, state = after(unit3, state)
     side3 = send(unit3, ACROSS)
-    state = query_units([side2, unit3], [theirs[2], mine[3]], gain, query_weight, state)
-    query_one = query_units([side3], [theirs[3]], gain, query_weight, state, tables)
+    state, ahead = query([side2, unit3], [theirs[2], mine[3]], [theirs[3]], ahead, state)
+    query_one, = query_units([side3], [theirs[3]], [], gain, query_weight, ahead, state, tables)
     return (updated[None], query_one[None])
 
 

time: 80.5 us -> 77.3 us (0.960)
  starting transfers between devices: 25.5 us -> 22.6 us
    ppermute x18, starting transfers between devices: 25.5 us -> 22.6 us  [send(): return lax.ppermute(value.astype(bf16), ('tensor', 'replica'), pairs)]
  transfers between devices with their start and end apart: 18 -> 18, of which waited for: 5 -> 5; matrix products, arithmetic and copies ran while one was open for 2% -> 2% of each run, Pallas kernels for 48% -> 52%
where the time goes in v3:
time: 77.3 us; the launch traced here: 77.1 us
  Pallas kernels  46.6 us (60%)
  starting transfers between devices  22.6 us (29%)
  waiting for transfers between devices  3.47 us (4%)
  other arithmetic  1.67 us (2%)
  between operations  1.55 us (2%)
  local copies, waits for them, and re-layouts  1.19 us (2%)
    pallas_call x5, Pallas kernels, down_units(): pl.pallas_call(functools.partial(down_kernel, count, first, later is not...  28.5 us
    ppermute x18, starting transfers between devices, send(): return lax.ppermute(value.astype(bf16), ('tensor', 'replica'), pairs)  22.6 us
    pallas_call x5, Pallas kernels, query_units(): pl.pallas_call(functools.partial(query_kernel, info), in_specs=in_specs +...  17.1 us
    ppermute x18, waiting for transfers between devices, send(): return lax.ppermute(value.astype(bf16), ('tensor', 'replica'), pairs)  3.47 us
  transfers between devices with their start and end apart: 18, of which 5 were waited for; matrix products, arithmetic and copies ran while one was open for 2% of the time, Pallas kernels for 52%

profile of v3, /device:TPU:0, one launch (start us, length us, event | category | flops | bytes accessed | tf_op | source)
XLA Modules:
  0.0 77.1 jit_solution(9244433005482643962)
XLA Ops:
  0.7 1.2 %copy-done = bf16[1,3584,128]{2,1,0:T(8,128)(2,1)S(1)} copy-done((bf16[1,3584,128]{2,1,0:T(8,128)(2,1)S(1)}, bf16[1,3584,128]{2,1,0:T(8,128)(2,1)}, u32[]{:S(2)}) %copy-start) | copy-done | bytes 917528
  1.8 4.1 %down_units.5 = (bf16[8,128,128]{2,1,0:T(8,128)(2,1)S(1)}, bf16[128,3584]{1,0:T(8,128)(2,1)S(1)}, bf16[256,128]{1,0:T(8,128)(2,1)S(1)}) custom-call(s32[1]{0:T(128)} %bitcast.7.units, bf16[3584,128]{1,0:T(8,128)(2,1)S(1)} %bitcast.20, bf16[3584,8192]{1,0:T(8,128)(2,1)} %refs_2_.1), custom_call_target="tpu_custom_call" | custom-call | flops 939524096 | bytes 7340032 | tf_op jit(solution)/shard_map/down_units/pallas_call | solution.py:228
  5.9 3.0 %collective-permute-start = (bf16[8,128,128]{2,1,0:T(8,128)(2,1)S(1)}, bf16[8,128,128]{2,1,0:T(8,128)(2,1)S(1)}, u32[]{:S(2)}, u32[]{:S(2)}) collective-permute-start(bf16[8,128,128]{2,1,0:T(8,128)(2,1)S(1)} %get-tuple-element.49), channel_id=1, source_target_pairs={{0,2},{1,3},{2,0},{3,1},{4,6},{5,7},{6,4},{7,5},{8,10},{9,11},{10,... | collective-permute-start | bytes 786440 | tf_op jit(solution)/shard_map/ppermute | solution.py:395
  8.9 0.1 pad_add_fusion.3.units
  9.0 6.6 %down_units.6 = (f32[8,128,128]{2,1,0:T(8,128)S(1)}, bf16[8,128,128]{2,1,0:T(8,128)(2,1)S(1)}) custom-call(s32[2]{0:T(128)S(1)} %pad_add_fusion.3.units, bf16[128,3584]{1,0:T(8,128)(2,1)S(1)} %get-tuple-element.58.refs_0_.refs_1_, bf16[3584,8192]{1,0:T(8,128)(2,1)} %refs_2_.1, bf16[256,128]{1,0:T(8,128)(2,1)S(1)} %get-tuple-element.47.refs_2_.refs_3_.refs_4_), custom_call_target="tpu_custom_call" | custom-call | flops 1879048192 | bytes 14680064 | tf_op jit(solution)/shard_map/down_units/pallas_call | solution.py:228
  15.6 0.1 collective-permute-start.1
  15.7 0.1 pad_add_fusion.units
  15.8 0.1 pad_add_fusion.1.units
  15.9 0.1 pad_add_fusion.4.units
  15.9 0.1 pad_add_fusion.2.units
  16.0 0.0 collective-permute-done
  16.0 0.1 fusion
  16.1 2.2 %collective-permute-start.2 = (bf16[8,128,128]{2,1,0:T(8,128)(2,1)S(1)}, bf16[8,128,128]{2,1,0:T(8,128)(2,1)S(1)}, u32[]{:S(2)}, u32[]{:S(2)}) collective-permute-start(bf16[8,128,128]{2,1,0:T(8,128)(2,1)S(1)} %fusion), channel_id=1, source_target_pairs={{0,4},{1,5},{2,6},{3,7},{4,0},{5,1},{6,2},{7,3},{8,12},{9,13},{10,... | collective-permute-start | bytes 786440 | tf_op jit(solution)/shard_map/ppermute | solution.py:395
  18.3 6.6 %down_units.7 = (f32[8,128,128]{2,1,0:T(8,128)S(1)}, bf16[8,128,128]{2,1,0:T(8,128)(2,1)S(1)}) custom-call(s32[2]{0:T(128)S(1)} %pad_add_fusion.2.units, bf16[128,3584]{1,0:T(8,128)(2,1)S(1)} %get-tuple-element.58.refs_0_.refs_1_, bf16[3584,8192]{1,0:T(8,128)(2,1)} %refs_2_.1, bf16[256,128]{1,0:T(8,128)(2,1)S(1)} %get-tuple-element.47.refs_2_.refs_3_.refs_4_), custom_call_target="tpu_custom_call" | custom-call | flops 1879048192 | bytes 14680064 | tf_op jit(solution)/shard_map/down_units/pallas_call | solution.py:228
  24.9 0.0 collective-permute-done.1
  24.9 0.1 fusion.1
  25.0 0.2 collective-permute-start.5
  25.2 1.8 %collective-permute-start.3 = (bf16[8,128,128]{2,1,0:T(8,128)(2,1)S(1)}, bf16[8,128,128]{2,1,0:T(8,128)(2,1)S(1)}, u32[]{:S(2)}, u32[]{:S(2)}) collective-permute-start(bf16[8,128,128]{2,1,0:T(8,128)(2,1)S(1)} %get-tuple-element.56), channel_id=1, source_target_pairs={{0,2},{1,3},{2,0},{3,1},{4,6},{5,7},{6,4},{7,5},{8,10},{9,11},{10,... | collective-permute-start | bytes 786440 | tf_op jit(solution)/shard_map/ppermute | solution.py:395
  26.9 0.0 collective-permute-done.2
  27.0 0.1 add_convert_fusion.2
  27.1 0.1 collective-permute-start.4
  27.1 6.8 %down_units.8 = (f32[8,128,128]{2,1,0:T(8,128)S(1)}, bf16[8,128,128]{2,1,0:T(8,128)(2,1)S(1)}) custom-call(s32[2]{0:T(128)S(1)} %pad_add_fusion.1.units, bf16[128,3584]{1,0:T(8,128)(2,1)S(1)} %get-tuple-element.58.refs_0_.refs_1_, bf16[3584,8192]{1,0:T(8,128)(2,1)} %refs_2_.1, bf16[256,128]{1,0:T(8,128)(2,1)S(1)} %get-tuple-element.47.refs_2_.refs_3_.refs_4_), custom_call_target="tpu_custom_call" | custom-call | flops 1879048192 | bytes 14680064 | tf_op jit(solution)/shard_map/down_units/pallas_call | solution.py:228
  33.9 0.0 copy-start.3
  33.9 0.3 collective-permute-start.6
  34.3 0.0 collective-permute-done.5
  34.3 0.1 fusion.2
  34.4 0.0 collective-permute-done.3
  34.4 0.0 collective-permute-done.4
  34.4 0.1 add_convert_fusion.1
  34.5 0.3 collective-permute-start.7
  34.9 3.6 %collective-permute-start.8 = (bf16[8,128,128]{2,1,0:T(8,128)(2,1)S(1)}, bf16[8,128,128]{2,1,0:T(8,128)(2,1)S(1)}, u32[]{:S(2)}, u32[]{:S(2)}) collective-permute-start(bf16[8,128,128]{2,1,0:T(8,128)(2,1)S(1)} %add_convert_fusion.1), channel_id=1, source_target_pairs={{0,4},{1,5},{2,6},{3,7},{4,0},{5,1},{6,2},{7,3},{8,12},{9,13},{10,... | collective-permute-start | bytes 786440 | tf_op jit(solution)/shard_map/ppermute | solution.py:395
  38.5 0.1 pad_add_fusion.5.units
  38.6 0.1 select_reduce_fusion.1
  38.7 4.4 %down_units.9 = (f32[8,128,128]{2,1,0:T(8,128)S(1)}, bf16[1024,1024]{1,0:T(8,128)(2,1)S(1)}) custom-call(s32[2]{0:T(128)S(1)} %pad_add_fusion.units, bf16[1024,8192]{1,0:T(8,128)(2,1)} %refs_5_.5, bf16[128,3584]{1,0:T(8,128)(2,1)S(1)} %get-tuple-element.58.refs_0_.refs_1_, bf16[3584,8192]{1,0:T(8,128)(2,1)} %refs_2_.1, ...), custom_call_target="tpu_custom_call" | custom-call | flops 939524096 | bytes 7340032 | tf_op jit(solution)/shard_map/down_units/pallas_call | solution.py:228
  43.1 0.0 collective-permute-done.6.refs_0_
  43.1 0.0 collective-permute-done.7.refs_1_
  43.1 0.2 collective-permute-done.8.refs_2_
  43.3 1.0 %update.1 = (bf16[8,128,128]{2,1,0:T(8,128)(2,1)}, bf16[8,128,128]{2,1,0:T(8,128)(2,1)S(1)}) custom-call(f32[8,128,128]{2,1,0:T(8,128)S(1)} %get-tuple-element.59.own_ref, bf16[8,128,128]{2,1,0:T(8,128)(2,1)S(1)} %collective-permute-done.6.refs_0_, bf16[8,128,128]{2,1,0:T(8,128)(2,1)S(1)} %collective-permute-done.7.refs_1_, ...), custom_call_target="tpu_custom_call" | custom-call | tf_op jit(solution)/shard_map/update/pallas_call | solution.py:260
  44.4 0.0 collective-permute-start.14
  44.4 3.2 %collective-permute-start.9 = (bf16[8,128,128]{2,1,0:T(8,128)(2,1)S(1)}, bf16[8,128,128]{2,1,0:T(8,128)(2,1)S(1)}, u32[]{:S(2)}, u32[]{:S(2)}) collective-permute-start(bf16[8,128,128]{2,1,0:T(8,128)(2,1)S(1)} %get-tuple-element.64.refs_0_), channel_id=1, source_target_pairs={{0,4},{1,5},{2,6},{3,7},{4,0},{5,1},{6,2},{7,3},{8,12},{9,13},{10,... | collective-permute-start | bytes 786440 | tf_op jit(solution)/shard_map/ppermute | solution.py:395
  47.6 0.1 pad_add_fusion.6.units
  47.7 0.1 select_reduce_fusion
  47.8 1.6 %collective-permute-start.11 = (bf16[8,128,128]{2,1,0:T(8,128)(2,1)S(1)}, bf16[8,128,128]{2,1,0:T(8,128)(2,1)S(1)}, u32[]{:S(2)}, u32[]{:S(2)}) collective-permute-start(bf16[8,128,128]{2,1,0:T(8,128)(2,1)S(1)} %get-tuple-element.64.refs_0_), channel_id=1, source_target_pairs={{0,2},{1,3},{2,0},{3,1},{4,6},{5,7},{6,4},{7,5},{8,10},{9,11},{10,... | collective-permute-start | bytes 786440 | tf_op jit(solution)/shard_map/ppermute | solution.py:395
  49.3 0.1 pad_add_fusion.7.units
  50.1 3.5 %query_units.5 = (f32[1024,128]{1,0:T(8,128)S(1)}, f32[128,128]{1,0:T(8,128)S(1)}, bf16[1024,1024]{1,0:T(8,128)(2,1)S(1)}, bf16[1024,1024]{1,0:T(8,128)(2,1)S(1)}) custom-call(s32[3]{0:T(128)S(1)} %pad_add_fusion.4.units, bf16[8,128,128]{2,1,0:T(8,128)(2,1)S(1)} %get-tuple-element.64.refs_0_, f32[64,128]{1,0:T(8,128)S(1)} %bitcast.21, ...), custom_call_target="tpu_custom_call" | custom-call | flops 268435456 | bytes 2097152 | tf_op jit(solution)/shard_map/query_units/pallas_call | solution.py:351
  53.6 0.0 collective-permute-done.9.refs_1_
  53.6 0.1 collective-permute-start.10
  53.7 0.0 collective-permute-done.14
  53.7 2.6 %collective-permute-start.15 = (bf16[8,128,128]{2,1,0:T(8,128)(2,1)S(1)}, bf16[8,128,128]{2,1,0:T(8,128)(2,1)S(1)}, u32[]{:S(2)}, u32[]{:S(2)}) collective-permute-start(bf16[8,128,128]{2,1,0:T(8,128)(2,1)S(1)} %collective-permute-done.14), channel_id=1, source_target_pairs={{0,4},{1,5},{2,6},{3,7},{4,0},{5,1},{6,2},{7,3},{8,12},{9,13},{10,... | collective-permute-start | bytes 786440 | tf_op jit(solution)/shard_map/ppermute | solution.py:395
  56.4 1.5 %collective-permute-start.13 = (bf16[8,128,128]{2,1,0:T(8,128)(2,1)S(1)}, bf16[8,128,128]{2,1,0:T(8,128)(2,1)S(1)}, u32[]{:S(2)}, u32[]{:S(2)}) collective-permute-start(bf16[8,128,128]{2,1,0:T(8,128)(2,1)S(1)} %collective-permute-done.9.refs_1_), channel_id=1, source_target_pairs={{0,2},{1,3},{2,0},{3,1},{4,6},{5,7},{6,4},{7,5},{8,10},{9,11},{10,... | collective-permute-start | bytes 786440 | tf_op jit(solution)/shard_map/ppermute | solution.py:395
  57.9 0.0 collective-permute-done.11.refs_0_
  57.9 4.2 %query_units.6 = (f32[1024,128]{1,0:T(8,128)S(1)}, f32[128,128]{1,0:T(8,128)S(1)}, bf16[1024,1024]{1,0:T(8,128)(2,1)S(1)}, bf16[1024,1024]{1,0:T(8,128)(2,1)S(1)}) custom-call(s32[4]{0:T(128)S(1)} %pad_add_fusion.5.units, bf16[8,128,128]{2,1,0:T(8,128)(2,1)S(1)} %collective-permute-done.11.refs_0_, bf16[8,128,128]{2,1,0:T(8,128)(2,1)S(1)} %collective-permute-done.9.refs_1_, ...), custom_call_target="tpu_custom_call" | custom-call | flops 536870912 | bytes 4194304 | tf_op jit(solution)/shard_map/query_units/pallas_call | solution.py:351
  62.0 0.1 collective-permute-start.12
  62.2 0.2 collective-permute-done.15
  62.5 1.3 %collective-permute-start.17 = (bf16[8,128,128]{2,1,0:T(8,128)(2,1)S(1)}, bf16[8,128,128]{2,1,0:T(8,128)(2,1)S(1)}, u32[]{:S(2)}, u32[]{:S(2)}) collective-permute-start(bf16[8,128,128]{2,1,0:T(8,128)(2,1)S(1)} %broadcast_select_fusion.1.refs_1_), channel_id=1, source_target_pairs={{0,2},{1,3},{2,0},{3,1},{4,6},{5,7},{6,4},{7,5},{8,10},{9,11},{10,... | collective-permute-start | bytes 786440 | tf_op jit(solution)/shard_map/ppermute | solution.py:395
  63.8 0.0 collective-permute-done.13.refs_0_
  63.8 4.2 %query_units.7 = (f32[1024,128]{1,0:T(8,128)S(1)}, f32[128,128]{1,0:T(8,128)S(1)}, bf16[1024,1024]{1,0:T(8,128)(2,1)S(1)}, bf16[1024,1024]{1,0:T(8,128)(2,1)S(1)}) custom-call(s32[4]{0:T(128)S(1)} %pad_add_fusion.6.units, bf16[8,128,128]{2,1,0:T(8,128)(2,1)S(1)} %collective-permute-done.13.refs_0_, bf16[8,128,128]{2,1,0:T(8,128)(2,1)S(1)} %broadcast_select_fusion.1.refs_1_, ...), custom_call_target="tpu_custom_call" | custom-call | flops 536870912 | bytes 4194304 | tf_op jit(solution)/shard_map/query_units/pallas_call | solution.py:351
  68.0 0.9 %collective-permute-done.12 = bf16[8,128,128]{2,1,0:T(8,128)(2,1)S(1)} collective-permute-done((bf16[8,128,128]{2,1,0:T(8,128)(2,1)S(1)}, bf16[8,128,128]{2,1,0:T(8,128)(2,1)S(1)}, u32[]{:S(2)}, u32[]{:S(2)}) %collective-permute-start.12) | collective-permute-done | bytes 262176 | tf_op jit(solution)/shard_map/ppermute | solution.py:395
  68.9 0.6 collective-permute-start.16
  69.5 0.3 fusion.3
  69.8 0.5 collective-permute-done.17.refs_0_
  70.3 3.5 %query_units.8 = (f32[1024,128]{1,0:T(8,128)S(1)}, f32[128,128]{1,0:T(8,128)S(1)}, bf16[1024,1024]{1,0:T(8,128)(2,1)S(1)}) custom-call(s32[3]{0:T(128)S(1)} %pad_add_fusion.7.units, bf16[8,128,128]{2,1,0:T(8,128)(2,1)S(1)} %collective-permute-done.17.refs_0_, bf16[8,128,128]{2,1,0:T(8,128)(2,1)S(1)} %broadcast_select_fusion.refs_1_, f32[64,128]{1,0:T(8,128)S(1)} %bitcast.24, ...), custom_call_target="tpu_custom_call" | custom-call | flops 536870912 | bytes 4194304 | tf_op jit(solution)/shard_map/query_units/pallas_call | solution.py:351
  73.8 1.6 %collective-permute-done.16.refs_0_ = bf16[8,128,128]{2,1,0:T(8,128)(2,1)S(1)} collective-permute-done((bf16[8,128,128]{2,1,0:T(8,128)(2,1)S(1)}, bf16[8,128,128]{2,1,0:T(8,128)(2,1)S(1)}, u32[]{:S(2)}, u32[]{:S(2)}) %collective-permute-start.16) | collective-permute-done | bytes 262176 | tf_op jit(solution)/shard_map/ppermute | solution.py:395
  75.4 1.7 %query_units.9 = bf16[1024,128]{1,0:T(8,128)(2,1)} custom-call(s32[1]{0:T(128)} %bitcast.7.units, bf16[8,128,128]{2,1,0:T(8,128)(2,1)S(1)} %collective-permute-done.16.refs_0_, f32[64,128]{1,0:T(8,128)S(1)} %bitcast.25, bf16[1024,1024]{1,0:T(8,128)(2,1)S(1)} %get-tuple-element.87.refs_2_, f32[1024,128]{1,0:T(8,128)S(1)} %get-tuple-element.88.refs_3_, ...), custom_call_target="tpu_custom_call" | custom-call | flops 268435456 | bytes 2097152 | tf_op jit(solution)/shard_map/query_units/pallas_call | solution.py:351
  (12 shorter events, 0.1 us)
Async XLA Ops:
  0.7 1.2 %copy-start = (bf16[1,3584,128]{2,1,0:T(8,128)(2,1)S(1)}, bf16[1,3584,128]{2,1,0:T(8,128)(2,1)}, u32[]{:S(2)}) copy-start(bf16[1,3584,128]{2,1,0:T(8,128)(2,1)} %param.7) | copy-start | bytes 2752516
  5.9 10.1 %collective-permute-start = (bf16[8,128,128]{2,1,0:T(8,128)(2,1)S(1)}, bf16[8,128,128]{2,1,0:T(8,128)(2,1)S(1)}, u32[]{:S(2)}, u32[]{:S(2)}) collective-permute-start(bf16[8,128,128]{2,1,0:T(8,128)(2,1)S(1)} %get-tuple-element.49), channel_id=1, source_target_pairs={{0,2},{1,3},{2,0},{3,1},{4,6},{5,7},{6,4},{7,5},{8,10},{9,11},{10,... | collective-permute-start | bytes 786440 | tf_op jit(solution)/shard_map/ppermute | solution.py:395
  15.6 9.3 %collective-permute-start.1 = (bf16[8,128,128]{2,1,0:T(8,128)(2,1)S(1)}, bf16[8,128,128]{2,1,0:T(8,128)(2,1)S(1)}, u32[]{:S(2)}, u32[]{:S(2)}) collective-permute-start(bf16[8,128,128]{2,1,0:T(8,128)(2,1)S(1)} %get-tuple-element.52), channel_id=1, source_target_pairs={{0,2},{1,3},{2,0},{3,1},{4,6},{5,7},{6,4},{7,5},{8,10},{9,11},{10,... | collective-permute-start | bytes 786440 | tf_op jit(solution)/shard_map/ppermute | solution.py:395
  16.1 10.8 %collective-permute-start.2 = (bf16[8,128,128]{2,1,0:T(8,128)(2,1)S(1)}, bf16[8,128,128]{2,1,0:T(8,128)(2,1)S(1)}, u32[]{:S(2)}, u32[]{:S(2)}) collective-permute-start(bf16[8,128,128]{2,1,0:T(8,128)(2,1)S(1)} %fusion), channel_id=1, source_target_pairs={{0,4},{1,5},{2,6},{3,7},{4,0},{5,1},{6,2},{7,3},{8,12},{9,13},{10,... | collective-permute-start | bytes 786440 | tf_op jit(solution)/shard_map/ppermute | solution.py:395
  25.0 9.3 %collective-permute-start.5 = (bf16[8,128,128]{2,1,0:T(8,128)(2,1)S(1)}, bf16[8,128,128]{2,1,0:T(8,128)(2,1)S(1)}, u32[]{:S(2)}, u32[]{:S(2)}) collective-permute-start(bf16[8,128,128]{2,1,0:T(8,128)(2,1)S(1)} %fusion.1), channel_id=1, source_target_pairs={{0,4},{1,5},{2,6},{3,7},{4,0},{5,1},{6,2},{7,3},{8,12},{9,13},{10,... | collective-permute-start | bytes 786440 | tf_op jit(solution)/shard_map/ppermute | solution.py:395
  25.2 9.2 %collective-permute-start.3 = (bf16[8,128,128]{2,1,0:T(8,128)(2,1)S(1)}, bf16[8,128,128]{2,1,0:T(8,128)(2,1)S(1)}, u32[]{:S(2)}, u32[]{:S(2)}) collective-permute-start(bf16[8,128,128]{2,1,0:T(8,128)(2,1)S(1)} %get-tuple-element.56), channel_id=1, source_target_pairs={{0,2},{1,3},{2,0},{3,1},{4,6},{5,7},{6,4},{7,5},{8,10},{9,11},{10,... | collective-permute-start | bytes 786440 | tf_op jit(solution)/shard_map/ppermute | solution.py:395
  27.1 7.3 %collective-permute-start.4 = (bf16[8,128,128]{2,1,0:T(8,128)(2,1)S(1)}, bf16[8,128,128]{2,1,0:T(8,128)(2,1)S(1)}, u32[]{:S(2)}, u32[]{:S(2)}) collective-permute-start(bf16[8,128,128]{2,1,0:T(8,128)(2,1)S(1)} %add_convert_fusion.2), channel_id=1, source_target_pairs={{0,1},{1,0},{2,3},{3,2},{4,8},{5,9},{6,10},{7,11},{8,4},{9,5},{10,... | collective-permute-start | bytes 786440 | tf_op jit(solution)/shard_map/ppermute | solution.py:395
  33.9 4.6 %copy-start.3 = (s32[1,4]{1,0:T(1,128)S(1)}, s32[1,4]{1,0:T(1,128)}, u32[]{:S(2)}) copy-start(s32[1,4]{1,0:T(1,128)} %param.13) | copy-start | bytes 52
  33.9 9.2 %collective-permute-start.6 = (bf16[8,128,128]{2,1,0:T(8,128)(2,1)S(1)}, bf16[8,128,128]{2,1,0:T(8,128)(2,1)S(1)}, u32[]{:S(2)}, u32[]{:S(2)}) collective-permute-start(bf16[8,128,128]{2,1,0:T(8,128)(2,1)S(1)} %get-tuple-element.60), channel_id=1, source_target_pairs={{0,2},{1,3},{2,0},{3,1},{4,6},{5,7},{6,4},{7,5},{8,10},{9,11},{10,... | collective-permute-start | bytes 786440 | tf_op jit(solution)/shard_map/ppermute | solution.py:395
  34.5 8.6 %collective-permute-start.7 = (bf16[8,128,128]{2,1,0:T(8,128)(2,1)S(1)}, bf16[8,128,128]{2,1,0:T(8,128)(2,1)S(1)}, u32[]{:S(2)}, u32[]{:S(2)}) collective-permute-start(bf16[8,128,128]{2,1,0:T(8,128)(2,1)S(1)} %fusion.2), channel_id=1, source_target_pairs={{0,1},{1,0},{2,3},{3,2},{4,8},{5,9},{6,10},{7,11},{8,4},{9,5},{10,... | collective-permute-start | bytes 786440 | tf_op jit(solution)/shard_map/ppermute | solution.py:395
  34.9 8.5 %collective-permute-start.8 = (bf16[8,128,128]{2,1,0:T(8,128)(2,1)S(1)}, bf16[8,128,128]{2,1,0:T(8,128)(2,1)S(1)}, u32[]{:S(2)}, u32[]{:S(2)}) collective-permute-start(bf16[8,128,128]{2,1,0:T(8,128)(2,1)S(1)} %add_convert_fusion.1), channel_id=1, source_target_pairs={{0,4},{1,5},{2,6},{3,7},{4,0},{5,1},{6,2},{7,3},{8,12},{9,13},{10,... | collective-permute-start | bytes 786440 | tf_op jit(solution)/shard_map/ppermute | solution.py:395
  38.7 4.7 %copy-start.2 = (bf16[1,8,128,128]{3,2,1,0:T(8,128)(2,1)S(1)}, bf16[1,8,128,128]{3,2,1,0:T(8,128)(2,1)}, u32[]{:S(2)}) copy-start(bf16[1,8,128,128]{3,2,1,0:T(8,128)(2,1)} %param.9) | copy-start | bytes 786436
  38.7 11.4 %copy-start.1 = (f32[8192]{0:T(1024)S(1)}, f32[8192]{0:T(1024)}, u32[]{:S(2)}) copy-start(f32[8192]{0:T(1024)} %param.10) | copy-start | bytes 98308
  44.4 9.3 %collective-permute-start.14 = (bf16[8,128,128]{2,1,0:T(8,128)(2,1)S(1)}, bf16[8,128,128]{2,1,0:T(8,128)(2,1)S(1)}, u32[]{:S(2)}, u32[]{:S(2)}) collective-permute-start(bf16[8,128,128]{2,1,0:T(8,128)(2,1)S(1)} %get-tuple-element.64.refs_0_), channel_id=1, source_target_pairs={{0,1},{1,0},{2,3},{3,2},{4,8},{5,9},{6,10},{7,11},{8,4},{9,5},{10,... | collective-permute-start | bytes 786440 | tf_op jit(solution)/shard_map/ppermute | solution.py:395
  44.4 9.2 %collective-permute-start.9 = (bf16[8,128,128]{2,1,0:T(8,128)(2,1)S(1)}, bf16[8,128,128]{2,1,0:T(8,128)(2,1)S(1)}, u32[]{:S(2)}, u32[]{:S(2)}) collective-permute-start(bf16[8,128,128]{2,1,0:T(8,128)(2,1)S(1)} %get-tuple-element.64.refs_0_), channel_id=1, source_target_pairs={{0,4},{1,5},{2,6},{3,7},{4,0},{5,1},{6,2},{7,3},{8,12},{9,13},{10,... | collective-permute-start | bytes 786440 | tf_op jit(solution)/shard_map/ppermute | solution.py:395
  47.8 10.1 %collective-permute-start.11 = (bf16[8,128,128]{2,1,0:T(8,128)(2,1)S(1)}, bf16[8,128,128]{2,1,0:T(8,128)(2,1)S(1)}, u32[]{:S(2)}, u32[]{:S(2)}) collective-permute-start(bf16[8,128,128]{2,1,0:T(8,128)(2,1)S(1)} %get-tuple-element.64.refs_0_), channel_id=1, source_target_pairs={{0,2},{1,3},{2,0},{3,1},{4,6},{5,7},{6,4},{7,5},{8,10},{9,11},{10,... | collective-permute-start | bytes 786440 | tf_op jit(solution)/shard_map/ppermute | solution.py:395
  53.6 8.4 %collective-permute-start.10 = (bf16[8,128,128]{2,1,0:T(8,128)(2,1)S(1)}, bf16[8,128,128]{2,1,0:T(8,128)(2,1)S(1)}, u32[]{:S(2)}, u32[]{:S(2)}) collective-permute-start(bf16[8,128,128]{2,1,0:T(8,128)(2,1)S(1)} %collective-permute-done.9.refs_1_), channel_id=1, source_target_pairs={{0,1},{1,0},{2,3},{3,2},{4,8},{5,9},{6,10},{7,11},{8,4},{9,5},{10,... | collective-permute-start | bytes 786440 | tf_op jit(solution)/shard_map/ppermute | solution.py:395
  53.7 8.7 %collective-permute-start.15 = (bf16[8,128,128]{2,1,0:T(8,128)(2,1)S(1)}, bf16[8,128,128]{2,1,0:T(8,128)(2,1)S(1)}, u32[]{:S(2)}, u32[]{:S(2)}) collective-permute-start(bf16[8,128,128]{2,1,0:T(8,128)(2,1)S(1)} %collective-permute-done.14), channel_id=1, source_target_pairs={{0,4},{1,5},{2,6},{3,7},{4,0},{5,1},{6,2},{7,3},{8,12},{9,13},{10,... | collective-permute-start | bytes 786440 | tf_op jit(solution)/shard_map/ppermute | solution.py:395
  56.4 7.5 %collective-permute-start.13 = (bf16[8,128,128]{2,1,0:T(8,128)(2,1)S(1)}, bf16[8,128,128]{2,1,0:T(8,128)(2,1)S(1)}, u32[]{:S(2)}, u32[]{:S(2)}) collective-permute-start(bf16[8,128,128]{2,1,0:T(8,128)(2,1)S(1)} %collective-permute-done.9.refs_1_), channel_id=1, source_target_pairs={{0,2},{1,3},{2,0},{3,1},{4,6},{5,7},{6,4},{7,5},{8,10},{9,11},{10,... | collective-permute-start | bytes 786440 | tf_op jit(solution)/shard_map/ppermute | solution.py:395
  62.0 6.8 %collective-permute-start.12 = (bf16[8,128,128]{2,1,0:T(8,128)(2,1)S(1)}, bf16[8,128,128]{2,1,0:T(8,128)(2,1)S(1)}, u32[]{:S(2)}, u32[]{:S(2)}) collective-permute-start(bf16[8,128,128]{2,1,0:T(8,128)(2,1)S(1)} %collective-permute-done.10), channel_id=1, source_target_pairs={{0,4},{1,5},{2,6},{3,7},{4,0},{5,1},{6,2},{7,3},{8,12},{9,13},{10,... | collective-permute-start | bytes 786440 | tf_op jit(solution)/shard_map/ppermute | solution.py:395
  62.5 7.8 %collective-permute-start.17 = (bf16[8,128,128]{2,1,0:T(8,128)(2,1)S(1)}, bf16[8,128,128]{2,1,0:T(8,128)(2,1)S(1)}, u32[]{:S(2)}, u32[]{:S(2)}) collective-permute-start(bf16[8,128,128]{2,1,0:T(8,128)(2,1)S(1)} %broadcast_select_fusion.1.refs_1_), channel_id=1, source_target_pairs={{0,2},{1,3},{2,0},{3,1},{4,6},{5,7},{6,4},{7,5},{8,10},{9,11},{10,... | collective-permute-start | bytes 786440 | tf_op jit(solution)/shard_map/ppermute | solution.py:395
  68.9 6.5 %collective-permute-start.16 = (bf16[8,128,128]{2,1,0:T(8,128)(2,1)S(1)}, bf16[8,128,128]{2,1,0:T(8,128)(2,1)S(1)}, u32[]{:S(2)}, u32[]{:S(2)}) collective-permute-start(bf16[8,128,128]{2,1,0:T(8,128)(2,1)S(1)} %broadcast_select_fusion.refs_1_), channel_id=1, source_target_pairs={{0,2},{1,3},{2,0},{3,1},{4,6},{5,7},{6,4},{7,5},{8,10},{9,11},{10,... | collective-permute-start | bytes 786440 | tf_op jit(solution)/shard_map/ppermute | solution.py:395

commit v4 on v3

--- a/solution.py
+++ b/solution.py
@@ -151,9 +151,9 @@
 
 def down_kernel(count, first, later, chunk, units, *refs):
     if later:
-        *refs, ahead, held, sems, ahead_sems = refs
-        query_ref, *refs = refs
-        refs = [*refs, held, sems]
+        query_ref, *refs, held, sems, ahead_sems = refs
+        ahead = refs[-later:]
+        refs = [*refs[:-later], held, sems]
     if first:
         rows_ref, weight_ref, out, turned, signs_out, held, sems, held_rows, row_sem = refs
         outs = [out]
@@ -173,7 +173,7 @@
     for k in range(count):
         for c in range(chunks):
             fetch(k, c).start()
-    coming = next_fetches(query_ref, units, [count], [ahead], ahead_sems) if later else []
+    coming = next_fetches(query_ref, units, range(count, count + later), ahead, ahead_sems) if later else []
     for copy in coming:
         copy.start()
     if first:
@@ -200,7 +200,7 @@
         copy.wait()
 
 
-def down_units(rows, down_weight, signs, units, dtypes, query_weight=None, later=None):
+def down_units(rows, down_weight, signs, units, dtypes, query_weight=None, later=()):
     count = len(dtypes)
     first = signs is None
     tokens, depth = rows.shape[::-1] if first else rows.shape
@@ -220,18 +220,18 @@
         args, in_specs = (rows, down_weight), [hbm, hbm]
     else:
         args, in_specs = (rows, down_weight, signs), [vmem, hbm, vmem]
-    if later is not None:
+    if later:
         args, in_specs = (query_weight, *args), [hbm, *in_specs]
-        units = [*units, later]
-        out_shape.append(jax.ShapeDtypeStruct((query_weight.shape[0], unit_width), bf16))
-        scratch.append(pltpu.SemaphoreType.DMA((1,)))
+        units = [*units, *later]
+        out_shape += [jax.ShapeDtypeStruct((query_weight.shape[0], unit_width), bf16)] * len(later)
+        scratch.append(pltpu.SemaphoreType.DMA((len(later),)))
     return pl.pallas_call(
-        functools.partial(down_kernel, count, first, later is not None, chunk),
+        functools.partial(down_kernel, count, first, len(later), chunk),
         in_specs=[pl.BlockSpec(memory_space=pltpu.SMEM), *in_specs],
         out_specs=[vmem] * len(out_shape),
         out_shape=out_shape,
         scratch_shapes=scratch,
-        compiler_params=pltpu.CompilerParams(vmem_limit_bytes=(48 if first or later is not None else 32) << 20),
+        compiler_params=pltpu.CompilerParams(vmem_limit_bytes=(48 if first or later else 32) << 20),
         cost_estimate=pl.CostEstimate(
             flops=2 * tokens * depth * unit_width * count,
             bytes_accessed=2 * depth * unit_width * count,
@@ -430,11 +430,12 @@
     part1, part2, rows = after(part1, part2, rows)
     from1 = send(part1, TWINS)
     from2 = send(part2, MIDDLE)
-    own0, *ahead = down_units(rows, down_weight, signs, [mine[0]], [f32], query_weight, mine[0])
+    early = [mine[0], theirs[0]]
+    own0, ahead0, held = down_units(rows, down_weight, signs, [mine[0]], [f32], query_weight, early)
+    from2, got0, _ = after(from2, got0, from1)
     updated, unit0 = update(own0, [got0, from2, from1], residual[0], signs)
 
     gain = norm_gain.reshape(-1, HB)
-    tables = rotary_tables(positions_of(prefix_len[0], seg_lengths[0], tokens))
 
     def query(streams, units, later, ahead, state=None):
         acc, square, *ahead = query_units(streams, units, later, gain, query_weight, ahead, state)
@@ -443,17 +444,20 @@
     side0 = send(unit0, ACROSS)
     unit1 = send(unit0, TWINS)
     inner2 = send(unit0, MIDDLE)
-    state, ahead = query([unit0], [mine[0]], [theirs[0], mine[1]], ahead)
+    state, ahead = query([unit0], [mine[0]], [mine[1]], [ahead0])
     unit1, state = after(unit1, state)
+    inner2, _ = after(inner2, unit1)
     side1 = send(unit1, ACROSS)
     inner3 = send(unit1, MIDDLE)
     unit2 = jnp.where(inner, inner2, send(inner2, TWINS))
-    state, ahead = query([side0, unit1], [theirs[0], mine[1]], [theirs[1], mine[2]], ahead, state)
+    state, ahead = query([side0, unit1], [theirs[0], mine[1]], [theirs[1], mine[2]], [held, *ahead], state)
     inner3, state = after(inner3, state)
     unit3 = jnp.where(inner, inner3, send(inner3, TWINS))
     side2 = send(unit2, ACROSS)
     state, ahead = query([side1, unit2], [theirs[1], mine[2]], [theirs[2], mine[3]], ahead, state)
     unit3, state = after(unit3, state)
+    prefix, lengths, _ = after(prefix_len[0], seg_lengths[0], unit3)
+    tables = rotary_tables(positions_of(prefix, lengths, tokens))
     side3 = send(unit3, ACROSS)
     state, ahead = query([side2, unit3], [theirs[2], mine[3]], [theirs[3]], ahead, state)
     query_one, = query_units([side3], [theirs[3]], [], gain, query_weight, ahead, state, tables)

time: 77.3 us -> 75.5 us (0.977)
  waiting for transfers between devices: 3.47 us -> 2.5 us
    ppermute x18, waiting for transfers between devices: 3.47 us -> 2.5 us  [send(): return lax.ppermute(value.astype(bf16), ('tensor', 'replica'), pairs)]
    pallas_call x5, Pallas kernels: 17.1 us -> 16.2 us  [query_units(): pl.pallas_call(functools.partial(query_kernel, info), in_specs=in_specs +...]
  transfers between devices with their start and end apart: 18 -> 18, of which waited for: 5 -> 3; matrix products, arithmetic and copies ran while one was open for 2% -> 2% of each run, Pallas kernels for 52% -> 53%
where the time goes in v4:
time: 75.5 us; the launch traced here: 75.3 us
  Pallas kernels  46.3 us (61%)
  starting transfers between devices  22.1 us (29%)
  waiting for transfers between devices  2.5 us (3%)
  other arithmetic  1.62 us (2%)
  between operations  1.55 us (2%)
  local copies, waits for them, and re-layouts  1.19 us (2%)
    pallas_call x5, Pallas kernels, down_units(): pl.pallas_call(functools.partial(down_kernel, count, first, len(later), c...  29.1 us
    ppermute x18, starting transfers between devices, send(): return lax.ppermute(value.astype(bf16), ('tensor', 'replica'), pairs)  22.1 us
    pallas_call x5, Pallas kernels, query_units(): pl.pallas_call(functools.partial(query_kernel, info), in_specs=in_specs +...  16.2 us
    ppermute x18, waiting for transfers between devices, send(): return lax.ppermute(value.astype(bf16), ('tensor', 'replica'), pairs)  2.5 us
  transfers between devices with their start and end apart: 18, of which 3 were waited for; matrix products, arithmetic and copies ran while one was open for 2% of the time, Pallas kernels for 53%

profile of v4, /device:TPU:0, one launch (start us, length us, event | category | flops | bytes accessed | tf_op | source)
XLA Modules:
  0.0 75.3 jit_solution(10757632692947900004)
XLA Ops:
  0.7 1.2 %copy-done = bf16[1,3584,128]{2,1,0:T(8,128)(2,1)S(1)} copy-done((bf16[1,3584,128]{2,1,0:T(8,128)(2,1)S(1)}, bf16[1,3584,128]{2,1,0:T(8,128)(2,1)}, u32[]{:S(2)}) %copy-start) | copy-done | bytes 917528
  1.8 4.1 %down_units.5 = (bf16[8,128,128]{2,1,0:T(8,128)(2,1)S(1)}, bf16[128,3584]{1,0:T(8,128)(2,1)S(1)}, bf16[256,128]{1,0:T(8,128)(2,1)S(1)}) custom-call(s32[1]{0:T(128)} %bitcast.7.units, bf16[3584,128]{1,0:T(8,128)(2,1)S(1)} %bitcast.20, bf16[3584,8192]{1,0:T(8,128)(2,1)} %refs_2_.1), custom_call_target="tpu_custom_call" | custom-call | flops 939524096 | bytes 7340032 | tf_op jit(solution)/shard_map/down_units/pallas_call | solution.py:228
  5.9 3.0 %collective-permute-start = (bf16[8,128,128]{2,1,0:T(8,128)(2,1)S(1)}, bf16[8,128,128]{2,1,0:T(8,128)(2,1)S(1)}, u32[]{:S(2)}, u32[]{:S(2)}) collective-permute-start(bf16[8,128,128]{2,1,0:T(8,128)(2,1)S(1)} %get-tuple-element.54), channel_id=1, source_target_pairs={{0,2},{1,3},{2,0},{3,1},{4,6},{5,7},{6,4},{7,5},{8,10},{9,11},{10,... | collective-permute-start | bytes 786440 | tf_op jit(solution)/shard_map/ppermute | solution.py:395
  8.9 0.1 pad_add_fusion.3.units
  9.0 6.6 %down_units.6 = (f32[8,128,128]{2,1,0:T(8,128)S(1)}, bf16[8,128,128]{2,1,0:T(8,128)(2,1)S(1)}) custom-call(s32[2]{0:T(128)S(1)} %pad_add_fusion.3.units, bf16[128,3584]{1,0:T(8,128)(2,1)S(1)} %get-tuple-element.63.refs_0_.refs_1_, bf16[3584,8192]{1,0:T(8,128)(2,1)} %refs_2_.1, bf16[256,128]{1,0:T(8,128)(2,1)S(1)} %get-tuple-element.52.refs_2_.refs_3_.refs_4_), custom_call_target="tpu_custom_call" | custom-call | flops 1879048192 | bytes 14680064 | tf_op jit(solution)/shard_map/down_units/pallas_call | solution.py:228
  15.6 0.1 collective-permute-start.1
  15.7 0.1 pad_add_fusion.2.units
  15.8 0.1 pad_add_fusion.1.units
  15.9 0.0 collective-permute-done
  15.9 0.1 fusion
  15.9 2.2 %collective-permute-start.2 = (bf16[8,128,128]{2,1,0:T(8,128)(2,1)S(1)}, bf16[8,128,128]{2,1,0:T(8,128)(2,1)S(1)}, u32[]{:S(2)}, u32[]{:S(2)}) collective-permute-start(bf16[8,128,128]{2,1,0:T(8,128)(2,1)S(1)} %fusion), channel_id=1, source_target_pairs={{0,4},{1,5},{2,6},{3,7},{4,0},{5,1},{6,2},{7,3},{8,12},{9,13},{10,... | collective-permute-start | bytes 786440 | tf_op jit(solution)/shard_map/ppermute | solution.py:395
  18.1 6.6 %down_units.7 = (f32[8,128,128]{2,1,0:T(8,128)S(1)}, bf16[8,128,128]{2,1,0:T(8,128)(2,1)S(1)}) custom-call(s32[2]{0:T(128)S(1)} %pad_add_fusion.2.units, bf16[128,3584]{1,0:T(8,128)(2,1)S(1)} %get-tuple-element.63.refs_0_.refs_1_, bf16[3584,8192]{1,0:T(8,128)(2,1)} %refs_2_.1, bf16[256,128]{1,0:T(8,128)(2,1)S(1)} %get-tuple-element.52.refs_2_.refs_3_.refs_4_), custom_call_target="tpu_custom_call" | custom-call | flops 1879048192 | bytes 14680064 | tf_op jit(solution)/shard_map/down_units/pallas_call | solution.py:228
  24.7 0.0 collective-permute-done.1
  24.7 0.1 fusion.1
  24.7 0.4 collective-permute-start.5
  25.2 1.6 %collective-permute-start.3 = (bf16[8,128,128]{2,1,0:T(8,128)(2,1)S(1)}, bf16[8,128,128]{2,1,0:T(8,128)(2,1)S(1)}, u32[]{:S(2)}, u32[]{:S(2)}) collective-permute-start(bf16[8,128,128]{2,1,0:T(8,128)(2,1)S(1)} %get-tuple-element.61), channel_id=1, source_target_pairs={{0,2},{1,3},{2,0},{3,1},{4,6},{5,7},{6,4},{7,5},{8,10},{9,11},{10,... | collective-permute-start | bytes 786440 | tf_op jit(solution)/shard_map/ppermute | solution.py:395
  26.8 0.0 collective-permute-done.2
  26.8 0.1 add_convert_fusion.2
  26.9 0.1 collective-permute-start.4
  26.9 6.8 %down_units.8 = (f32[8,128,128]{2,1,0:T(8,128)S(1)}, bf16[8,128,128]{2,1,0:T(8,128)(2,1)S(1)}) custom-call(s32[2]{0:T(128)S(1)} %pad_add_fusion.1.units, bf16[128,3584]{1,0:T(8,128)(2,1)S(1)} %get-tuple-element.63.refs_0_.refs_1_, bf16[3584,8192]{1,0:T(8,128)(2,1)} %refs_2_.1, bf16[256,128]{1,0:T(8,128)(2,1)S(1)} %get-tuple-element.52.refs_2_.refs_3_.refs_4_), custom_call_target="tpu_custom_call" | custom-call | flops 1879048192 | bytes 14680064 | tf_op jit(solution)/shard_map/down_units/pallas_call | solution.py:228
  33.7 0.5 collective-permute-start.7
  34.2 0.0 collective-permute-done.5
  34.2 0.1 fusion.2
  34.4 0.0 collective-permute-done.3
  34.4 0.0 collective-permute-done.4
  34.4 0.1 add_convert_fusion.1
  34.5 0.3 collective-permute-start.6
  34.8 3.5 %collective-permute-start.8 = (bf16[8,128,128]{2,1,0:T(8,128)(2,1)S(1)}, bf16[8,128,128]{2,1,0:T(8,128)(2,1)S(1)}, u32[]{:S(2)}, u32[]{:S(2)}) collective-permute-start(bf16[8,128,128]{2,1,0:T(8,128)(2,1)S(1)} %add_convert_fusion.1), channel_id=1, source_target_pairs={{0,4},{1,5},{2,6},{3,7},{4,0},{5,1},{6,2},{7,3},{8,12},{9,13},{10,... | collective-permute-start | bytes 786440 | tf_op jit(solution)/shard_map/ppermute | solution.py:395
  38.3 0.1 pad_add_fusion.units
  38.3 5.0 %down_units.9 = (f32[8,128,128]{2,1,0:T(8,128)S(1)}, bf16[1024,1024]{1,0:T(8,128)(2,1)S(1)}, bf16[1024,1024]{1,0:T(8,128)(2,1)S(1)}) custom-call(s32[3]{0:T(128)S(1)} %pad_add_fusion.units, bf16[1024,8192]{1,0:T(8,128)(2,1)} %refs_5_.5, bf16[128,3584]{1,0:T(8,128)(2,1)S(1)} %get-tuple-element.63.refs_0_.refs_1_, bf16[3584,8192]{1,0:T(8,128)(2,1)} %refs_2_.1, ...), custom_call_target="tpu_custom_call" | custom-call | flops 939524096 | bytes 7340032 | tf_op jit(solution)/shard_map/down_units/pallas_call | solution.py:228
  43.4 0.0 collective-permute-done.7.refs_0_
  43.4 0.0 collective-permute-done.6.refs_1_
  43.4 0.0 collective-permute-done.8.refs_2_
  43.4 1.0 %update.1 = (bf16[8,128,128]{2,1,0:T(8,128)(2,1)}, bf16[8,128,128]{2,1,0:T(8,128)(2,1)S(1)}) custom-call(f32[8,128,128]{2,1,0:T(8,128)S(1)} %get-tuple-element.64.own_ref, bf16[8,128,128]{2,1,0:T(8,128)(2,1)S(1)} %collective-permute-done.7.refs_0_, bf16[8,128,128]{2,1,0:T(8,128)(2,1)S(1)} %collective-permute-done.6.refs_1_, ...), custom_call_target="tpu_custom_call" | custom-call | tf_op jit(solution)/shard_map/update/pallas_call | solution.py:260
  44.5 1.2 %collective-permute-start.9 = (bf16[8,128,128]{2,1,0:T(8,128)(2,1)S(1)}, bf16[8,128,128]{2,1,0:T(8,128)(2,1)S(1)}, u32[]{:S(2)}, u32[]{:S(2)}) collective-permute-start(bf16[8,128,128]{2,1,0:T(8,128)(2,1)S(1)} %get-tuple-element.71.refs_0_), channel_id=1, source_target_pairs={{0,4},{1,5},{2,6},{3,7},{4,0},{5,1},{6,2},{7,3},{8,12},{9,13},{10,... | collective-permute-start | bytes 786440 | tf_op jit(solution)/shard_map/ppermute | solution.py:395
  45.7 0.0 collective-permute-start.14
  45.7 0.1 pad_add_fusion.4.units
  45.7 0.1 pad_add_fusion.5.units
  45.8 1.5 %collective-permute-start.11 = (bf16[8,128,128]{2,1,0:T(8,128)(2,1)S(1)}, bf16[8,128,128]{2,1,0:T(8,128)(2,1)S(1)}, u32[]{:S(2)}, u32[]{:S(2)}) collective-permute-start(bf16[8,128,128]{2,1,0:T(8,128)(2,1)S(1)} %get-tuple-element.71.refs_0_), channel_id=1, source_target_pairs={{0,2},{1,3},{2,0},{3,1},{4,6},{5,7},{6,4},{7,5},{8,10},{9,11},{10,... | collective-permute-start | bytes 786440 | tf_op jit(solution)/shard_map/ppermute | solution.py:395
  47.3 0.1 pad_add_fusion.6.units
  48.1 2.7 %query_units.5 = (f32[1024,128]{1,0:T(8,128)S(1)}, f32[128,128]{1,0:T(8,128)S(1)}, bf16[1024,1024]{1,0:T(8,128)(2,1)S(1)}) custom-call(s32[2]{0:T(128)S(1)} %pad_add_fusion.4.units, bf16[8,128,128]{2,1,0:T(8,128)(2,1)S(1)} %get-tuple-element.71.refs_0_, f32[64,128]{1,0:T(8,128)S(1)} %bitcast.21, bf16[1024,1024]{1,0:T(8,128)(2,1)S(1)} %get-tuple-element.72.refs_2_, ...), custom_call_target="tpu_custom_call" | custom-call | flops 268435456 | bytes 2097152 | tf_op jit(solution)/shard_map/query_units/pallas_call | solution.py:351
  50.8 0.7 collective-permute-done.9.refs_1_
  51.5 0.0 collective-permute-start.10
  51.5 0.0 collective-permute-done.14
  51.5 3.4 %collective-permute-start.15 = (bf16[8,128,128]{2,1,0:T(8,128)(2,1)S(1)}, bf16[8,128,128]{2,1,0:T(8,128)(2,1)S(1)}, u32[]{:S(2)}, u32[]{:S(2)}) collective-permute-start(bf16[8,128,128]{2,1,0:T(8,128)(2,1)S(1)} %collective-permute-done.14), channel_id=1, source_target_pairs={{0,4},{1,5},{2,6},{3,7},{4,0},{5,1},{6,2},{7,3},{8,12},{9,13},{10,... | collective-permute-start | bytes 786440 | tf_op jit(solution)/shard_map/ppermute | solution.py:395
  54.9 0.1 pad_add_fusion.7.units
  55.0 1.5 %collective-permute-start.13 = (bf16[8,128,128]{2,1,0:T(8,128)(2,1)S(1)}, bf16[8,128,128]{2,1,0:T(8,128)(2,1)S(1)}, u32[]{:S(2)}, u32[]{:S(2)}) collective-permute-start(bf16[8,128,128]{2,1,0:T(8,128)(2,1)S(1)} %collective-permute-done.9.refs_1_), channel_id=1, source_target_pairs={{0,2},{1,3},{2,0},{3,1},{4,6},{5,7},{6,4},{7,5},{8,10},{9,11},{10,... | collective-permute-start | bytes 786440 | tf_op jit(solution)/shard_map/ppermute | solution.py:395
  56.5 0.0 collective-permute-done.11.refs_0_
  56.5 4.2 %query_units.6 = (f32[1024,128]{1,0:T(8,128)S(1)}, f32[128,128]{1,0:T(8,128)S(1)}, bf16[1024,1024]{1,0:T(8,128)(2,1)S(1)}, bf16[1024,1024]{1,0:T(8,128)(2,1)S(1)}) custom-call(s32[4]{0:T(128)S(1)} %pad_add_fusion.5.units, bf16[8,128,128]{2,1,0:T(8,128)(2,1)S(1)} %collective-permute-done.11.refs_0_, bf16[8,128,128]{2,1,0:T(8,128)(2,1)S(1)} %collective-permute-done.9.refs_1_, ...), custom_call_target="tpu_custom_call" | custom-call | flops 536870912 | bytes 4194304 | tf_op jit(solution)/shard_map/query_units/pallas_call | solution.py:351
  60.7 0.0 collective-permute-done.10
  60.7 0.3 collective-permute-start.12
  61.0 0.0 collective-permute-done.15
  61.0 1.4 %collective-permute-start.17 = (bf16[8,128,128]{2,1,0:T(8,128)(2,1)S(1)}, bf16[8,128,128]{2,1,0:T(8,128)(2,1)S(1)}, u32[]{:S(2)}, u32[]{:S(2)}) collective-permute-start(bf16[8,128,128]{2,1,0:T(8,128)(2,1)S(1)} %broadcast_select_fusion.1.refs_1_), channel_id=1, source_target_pairs={{0,2},{1,3},{2,0},{3,1},{4,6},{5,7},{6,4},{7,5},{8,10},{9,11},{10,... | collective-permute-start | bytes 786440 | tf_op jit(solution)/shard_map/ppermute | solution.py:395
  62.4 0.0 collective-permute-done.13.refs_0_
  62.4 4.2 %query_units.7 = (f32[1024,128]{1,0:T(8,128)S(1)}, f32[128,128]{1,0:T(8,128)S(1)}, bf16[1024,1024]{1,0:T(8,128)(2,1)S(1)}, bf16[1024,1024]{1,0:T(8,128)(2,1)S(1)}) custom-call(s32[4]{0:T(128)S(1)} %pad_add_fusion.6.units, bf16[8,128,128]{2,1,0:T(8,128)(2,1)S(1)} %collective-permute-done.13.refs_0_, bf16[8,128,128]{2,1,0:T(8,128)(2,1)S(1)} %broadcast_select_fusion.1.refs_1_, ...), custom_call_target="tpu_custom_call" | custom-call | flops 536870912 | bytes 4194304 | tf_op jit(solution)/shard_map/query_units/pallas_call | solution.py:351
  66.6 0.6 collective-permute-done.12
  67.2 1.2 %collective-permute-start.16 = (bf16[8,128,128]{2,1,0:T(8,128)(2,1)S(1)}, bf16[8,128,128]{2,1,0:T(8,128)(2,1)S(1)}, u32[]{:S(2)}, u32[]{:S(2)}) collective-permute-start(bf16[8,128,128]{2,1,0:T(8,128)(2,1)S(1)} %broadcast_select_fusion.refs_1_), channel_id=1, source_target_pairs={{0,2},{1,3},{2,0},{3,1},{4,6},{5,7},{6,4},{7,5},{8,10},{9,11},{10,... | collective-permute-start | bytes 786440 | tf_op jit(solution)/shard_map/ppermute | solution.py:395
  68.3 0.1 select_reduce_fusion.1
  68.4 0.1 select_reduce_fusion
  68.5 0.0 collective-permute-done.17.refs_0_
  68.5 3.5 %query_units.8 = (f32[1024,128]{1,0:T(8,128)S(1)}, f32[128,128]{1,0:T(8,128)S(1)}, bf16[1024,1024]{1,0:T(8,128)(2,1)S(1)}) custom-call(s32[3]{0:T(128)S(1)} %pad_add_fusion.7.units, bf16[8,128,128]{2,1,0:T(8,128)(2,1)S(1)} %collective-permute-done.17.refs_0_, bf16[8,128,128]{2,1,0:T(8,128)(2,1)S(1)} %broadcast_select_fusion.refs_1_, f32[64,128]{1,0:T(8,128)S(1)} %bitcast.24, ...), custom_call_target="tpu_custom_call" | custom-call | flops 536870912 | bytes 4194304 | tf_op jit(solution)/shard_map/query_units/pallas_call | solution.py:351
  72.1 0.3 fusion.3
  72.4 1.2 %collective-permute-done.16.refs_0_ = bf16[8,128,128]{2,1,0:T(8,128)(2,1)S(1)} collective-permute-done((bf16[8,128,128]{2,1,0:T(8,128)(2,1)S(1)}, bf16[8,128,128]{2,1,0:T(8,128)(2,1)S(1)}, u32[]{:S(2)}, u32[]{:S(2)}) %collective-permute-start.16) | collective-permute-done | bytes 262176 | tf_op jit(solution)/shard_map/ppermute | solution.py:395
  73.6 1.7 %query_units.9 = bf16[1024,128]{1,0:T(8,128)(2,1)} custom-call(s32[1]{0:T(128)} %bitcast.7.units, bf16[8,128,128]{2,1,0:T(8,128)(2,1)S(1)} %collective-permute-done.16.refs_0_, f32[64,128]{1,0:T(8,128)S(1)} %bitcast.25, bf16[1024,1024]{1,0:T(8,128)(2,1)S(1)} %get-tuple-element.95.refs_2_, f32[1024,128]{1,0:T(8,128)S(1)} %get-tuple-element.96.refs_3_, ...), custom_call_target="tpu_custom_call" | custom-call | flops 268435456 | bytes 2097152 | tf_op jit(solution)/shard_map/query_units/pallas_call | solution.py:351
  (12 shorter events, 0.1 us)
Async XLA Ops:
  0.7 1.2 %copy-start = (bf16[1,3584,128]{2,1,0:T(8,128)(2,1)S(1)}, bf16[1,3584,128]{2,1,0:T(8,128)(2,1)}, u32[]{:S(2)}) copy-start(bf16[1,3584,128]{2,1,0:T(8,128)(2,1)} %param.7) | copy-start | bytes 2752516
  5.9 9.9 %collective-permute-start = (bf16[8,128,128]{2,1,0:T(8,128)(2,1)S(1)}, bf16[8,128,128]{2,1,0:T(8,128)(2,1)S(1)}, u32[]{:S(2)}, u32[]{:S(2)}) collective-permute-start(bf16[8,128,128]{2,1,0:T(8,128)(2,1)S(1)} %get-tuple-element.54), channel_id=1, source_target_pairs={{0,2},{1,3},{2,0},{3,1},{4,6},{5,7},{6,4},{7,5},{8,10},{9,11},{10,... | collective-permute-start | bytes 786440 | tf_op jit(solution)/shard_map/ppermute | solution.py:395
  15.6 9.1 %collective-permute-start.1 = (bf16[8,128,128]{2,1,0:T(8,128)(2,1)S(1)}, bf16[8,128,128]{2,1,0:T(8,128)(2,1)S(1)}, u32[]{:S(2)}, u32[]{:S(2)}) collective-permute-start(bf16[8,128,128]{2,1,0:T(8,128)(2,1)S(1)} %get-tuple-element.57), channel_id=1, source_target_pairs={{0,2},{1,3},{2,0},{3,1},{4,6},{5,7},{6,4},{7,5},{8,10},{9,11},{10,... | collective-permute-start | bytes 786440 | tf_op jit(solution)/shard_map/ppermute | solution.py:395
  15.9 10.8 %collective-permute-start.2 = (bf16[8,128,128]{2,1,0:T(8,128)(2,1)S(1)}, bf16[8,128,128]{2,1,0:T(8,128)(2,1)S(1)}, u32[]{:S(2)}, u32[]{:S(2)}) collective-permute-start(bf16[8,128,128]{2,1,0:T(8,128)(2,1)S(1)} %fusion), channel_id=1, source_target_pairs={{0,4},{1,5},{2,6},{3,7},{4,0},{5,1},{6,2},{7,3},{8,12},{9,13},{10,... | collective-permute-start | bytes 786440 | tf_op jit(solution)/shard_map/ppermute | solution.py:395
  24.7 9.5 %collective-permute-start.5 = (bf16[8,128,128]{2,1,0:T(8,128)(2,1)S(1)}, bf16[8,128,128]{2,1,0:T(8,128)(2,1)S(1)}, u32[]{:S(2)}, u32[]{:S(2)}) collective-permute-start(bf16[8,128,128]{2,1,0:T(8,128)(2,1)S(1)} %fusion.1), channel_id=1, source_target_pairs={{0,4},{1,5},{2,6},{3,7},{4,0},{5,1},{6,2},{7,3},{8,12},{9,13},{10,... | collective-permute-start | bytes 786440 | tf_op jit(solution)/shard_map/ppermute | solution.py:395
  25.2 9.2 %collective-permute-start.3 = (bf16[8,128,128]{2,1,0:T(8,128)(2,1)S(1)}, bf16[8,128,128]{2,1,0:T(8,128)(2,1)S(1)}, u32[]{:S(2)}, u32[]{:S(2)}) collective-permute-start(bf16[8,128,128]{2,1,0:T(8,128)(2,1)S(1)} %get-tuple-element.61), channel_id=1, source_target_pairs={{0,2},{1,3},{2,0},{3,1},{4,6},{5,7},{6,4},{7,5},{8,10},{9,11},{10,... | collective-permute-start | bytes 786440 | tf_op jit(solution)/shard_map/ppermute | solution.py:395
  26.9 7.5 %collective-permute-start.4 = (bf16[8,128,128]{2,1,0:T(8,128)(2,1)S(1)}, bf16[8,128,128]{2,1,0:T(8,128)(2,1)S(1)}, u32[]{:S(2)}, u32[]{:S(2)}) collective-permute-start(bf16[8,128,128]{2,1,0:T(8,128)(2,1)S(1)} %add_convert_fusion.2), channel_id=1, source_target_pairs={{0,1},{1,0},{2,3},{3,2},{4,8},{5,9},{6,10},{7,11},{8,4},{9,5},{10,... | collective-permute-start | bytes 786440 | tf_op jit(solution)/shard_map/ppermute | solution.py:395
  33.7 9.7 %collective-permute-start.7 = (bf16[8,128,128]{2,1,0:T(8,128)(2,1)S(1)}, bf16[8,128,128]{2,1,0:T(8,128)(2,1)S(1)}, u32[]{:S(2)}, u32[]{:S(2)}) collective-permute-start(bf16[8,128,128]{2,1,0:T(8,128)(2,1)S(1)} %get-tuple-element.66), channel_id=1, source_target_pairs={{0,2},{1,3},{2,0},{3,1},{4,6},{5,7},{6,4},{7,5},{8,10},{9,11},{10,... | collective-permute-start | bytes 786440 | tf_op jit(solution)/shard_map/ppermute | solution.py:395
  34.5 8.9 %collective-permute-start.6 = (bf16[8,128,128]{2,1,0:T(8,128)(2,1)S(1)}, bf16[8,128,128]{2,1,0:T(8,128)(2,1)S(1)}, u32[]{:S(2)}, u32[]{:S(2)}) collective-permute-start(bf16[8,128,128]{2,1,0:T(8,128)(2,1)S(1)} %fusion.2), channel_id=1, source_target_pairs={{0,1},{1,0},{2,3},{3,2},{4,8},{5,9},{6,10},{7,11},{8,4},{9,5},{10,... | collective-permute-start | bytes 786440 | tf_op jit(solution)/shard_map/ppermute | solution.py:395
  34.8 8.6 %collective-permute-start.8 = (bf16[8,128,128]{2,1,0:T(8,128)(2,1)S(1)}, bf16[8,128,128]{2,1,0:T(8,128)(2,1)S(1)}, u32[]{:S(2)}, u32[]{:S(2)}) collective-permute-start(bf16[8,128,128]{2,1,0:T(8,128)(2,1)S(1)} %add_convert_fusion.1), channel_id=1, source_target_pairs={{0,4},{1,5},{2,6},{3,7},{4,0},{5,1},{6,2},{7,3},{8,12},{9,13},{10,... | collective-permute-start | bytes 786440 | tf_op jit(solution)/shard_map/ppermute | solution.py:395
  38.3 5.1 %copy-start.2 = (bf16[1,8,128,128]{3,2,1,0:T(8,128)(2,1)S(1)}, bf16[1,8,128,128]{3,2,1,0:T(8,128)(2,1)}, u32[]{:S(2)}) copy-start(bf16[1,8,128,128]{3,2,1,0:T(8,128)(2,1)} %param.9) | copy-start | bytes 786436
  38.3 9.7 %copy-start.1 = (f32[8192]{0:T(1024)S(1)}, f32[8192]{0:T(1024)}, u32[]{:S(2)}) copy-start(f32[8192]{0:T(1024)} %param.10) | copy-start | bytes 98308
  44.5 7.0 %collective-permute-start.9 = (bf16[8,128,128]{2,1,0:T(8,128)(2,1)S(1)}, bf16[8,128,128]{2,1,0:T(8,128)(2,1)S(1)}, u32[]{:S(2)}, u32[]{:S(2)}) collective-permute-start(bf16[8,128,128]{2,1,0:T(8,128)(2,1)S(1)} %get-tuple-element.71.refs_0_), channel_id=1, source_target_pairs={{0,4},{1,5},{2,6},{3,7},{4,0},{5,1},{6,2},{7,3},{8,12},{9,13},{10,... | collective-permute-start | bytes 786440 | tf_op jit(solution)/shard_map/ppermute | solution.py:395
  45.7 5.8 %collective-permute-start.14 = (bf16[8,128,128]{2,1,0:T(8,128)(2,1)S(1)}, bf16[8,128,128]{2,1,0:T(8,128)(2,1)S(1)}, u32[]{:S(2)}, u32[]{:S(2)}) collective-permute-start(bf16[8,128,128]{2,1,0:T(8,128)(2,1)S(1)} %get-tuple-element.71.refs_0_), channel_id=1, source_target_pairs={{0,1},{1,0},{2,3},{3,2},{4,8},{5,9},{6,10},{7,11},{8,4},{9,5},{10,... | collective-permute-start | bytes 786440 | tf_op jit(solution)/shard_map/ppermute | solution.py:395
  45.8 10.7 %collective-permute-start.11 = (bf16[8,128,128]{2,1,0:T(8,128)(2,1)S(1)}, bf16[8,128,128]{2,1,0:T(8,128)(2,1)S(1)}, u32[]{:S(2)}, u32[]{:S(2)}) collective-permute-start(bf16[8,128,128]{2,1,0:T(8,128)(2,1)S(1)} %get-tuple-element.71.refs_0_), channel_id=1, source_target_pairs={{0,2},{1,3},{2,0},{3,1},{4,6},{5,7},{6,4},{7,5},{8,10},{9,11},{10,... | collective-permute-start | bytes 786440 | tf_op jit(solution)/shard_map/ppermute | solution.py:395
  51.5 9.2 %collective-permute-start.10 = (bf16[8,128,128]{2,1,0:T(8,128)(2,1)S(1)}, bf16[8,128,128]{2,1,0:T(8,128)(2,1)S(1)}, u32[]{:S(2)}, u32[]{:S(2)}) collective-permute-start(bf16[8,128,128]{2,1,0:T(8,128)(2,1)S(1)} %collective-permute-done.9.refs_1_), channel_id=1, source_target_pairs={{0,1},{1,0},{2,3},{3,2},{4,8},{5,9},{6,10},{7,11},{8,4},{9,5},{10,... | collective-permute-start | bytes 786440 | tf_op jit(solution)/shard_map/ppermute | solution.py:395
  51.5 9.5 %collective-permute-start.15 = (bf16[8,128,128]{2,1,0:T(8,128)(2,1)S(1)}, bf16[8,128,128]{2,1,0:T(8,128)(2,1)S(1)}, u32[]{:S(2)}, u32[]{:S(2)}) collective-permute-start(bf16[8,128,128]{2,1,0:T(8,128)(2,1)S(1)} %collective-permute-done.14), channel_id=1, source_target_pairs={{0,4},{1,5},{2,6},{3,7},{4,0},{5,1},{6,2},{7,3},{8,12},{9,13},{10,... | collective-permute-start | bytes 786440 | tf_op jit(solution)/shard_map/ppermute | solution.py:395
  55.0 7.4 %collective-permute-start.13 = (bf16[8,128,128]{2,1,0:T(8,128)(2,1)S(1)}, bf16[8,128,128]{2,1,0:T(8,128)(2,1)S(1)}, u32[]{:S(2)}, u32[]{:S(2)}) collective-permute-start(bf16[8,128,128]{2,1,0:T(8,128)(2,1)S(1)} %collective-permute-done.9.refs_1_), channel_id=1, source_target_pairs={{0,2},{1,3},{2,0},{3,1},{4,6},{5,7},{6,4},{7,5},{8,10},{9,11},{10,... | collective-permute-start | bytes 786440 | tf_op jit(solution)/shard_map/ppermute | solution.py:395
  60.7 6.4 %collective-permute-start.12 = (bf16[8,128,128]{2,1,0:T(8,128)(2,1)S(1)}, bf16[8,128,128]{2,1,0:T(8,128)(2,1)S(1)}, u32[]{:S(2)}, u32[]{:S(2)}) collective-permute-start(bf16[8,128,128]{2,1,0:T(8,128)(2,1)S(1)} %collective-permute-done.10), channel_id=1, source_target_pairs={{0,4},{1,5},{2,6},{3,7},{4,0},{5,1},{6,2},{7,3},{8,12},{9,13},{10,... | collective-permute-start | bytes 786440 | tf_op jit(solution)/shard_map/ppermute | solution.py:395
  61.0 7.5 %collective-permute-start.17 = (bf16[8,128,128]{2,1,0:T(8,128)(2,1)S(1)}, bf16[8,128,128]{2,1,0:T(8,128)(2,1)S(1)}, u32[]{:S(2)}, u32[]{:S(2)}) collective-permute-start(bf16[8,128,128]{2,1,0:T(8,128)(2,1)S(1)} %broadcast_select_fusion.1.refs_1_), channel_id=1, source_target_pairs={{0,2},{1,3},{2,0},{3,1},{4,6},{5,7},{6,4},{7,5},{8,10},{9,11},{10,... | collective-permute-start | bytes 786440 | tf_op jit(solution)/shard_map/ppermute | solution.py:395
  62.4 5.9 %copy-start.3 = (s32[1,4]{1,0:T(1,128)S(1)}, s32[1,4]{1,0:T(1,128)}, u32[]{:S(2)}) copy-start(s32[1,4]{1,0:T(1,128)} %param.13) | copy-start | bytes 52
  67.2 6.4 %collective-permute-start.16 = (bf16[8,128,128]{2,1,0:T(8,128)(2,1)S(1)}, bf16[8,128,128]{2,1,0:T(8,128)(2,1)S(1)}, u32[]{:S(2)}, u32[]{:S(2)}) collective-permute-start(bf16[8,128,128]{2,1,0:T(8,128)(2,1)S(1)} %broadcast_select_fusion.refs_1_), channel_id=1, source_target_pairs={{0,2},{1,3},{2,0},{3,1},{4,6},{5,7},{6,4},{7,5},{8,10},{9,11},{10,... | collective-permute-start | bytes 786440 | tf_op jit(solution)/shard_map/ppermute | solution.py:395

commit v5 on v4

--- a/solution.py
+++ b/solution.py
@@ -331,7 +331,7 @@
     columns, width = query_weight.shape
     unit_width = blocks * HB
     first, last = carried is None, tables is not None
-    info = dict(count=count, chunk=512, first=first, last=last, following=following, width=width)
+    info = dict(count=count, chunk=columns, first=first, last=last, following=following, width=width)
     vmem = pl.BlockSpec(memory_space=pltpu.VMEM)
     args = [jnp.stack([*units, *later]), *streams, gain, *ahead]
     in_specs = [pl.BlockSpec(memory_space=pltpu.SMEM)] + [vmem] * (2 * count + 1)

time: 75.5 us -> 75.2 us (level)
  Pallas kernels: 46.3 us -> 43.9 us
  waiting for transfers between devices: 2.5 us -> 4.65 us
    pallas_call x5, Pallas kernels: 16.2 us -> 13.8 us  [query_units(): pl.pallas_call(functools.partial(query_kernel, info), in_specs=in_specs +...]
    ppermute x18, waiting for transfers between devices: 2.5 us -> 4.65 us  [send(): return lax.ppermute(value.astype(bf16), ('tensor', 'replica'), pairs)]
  transfers between devices with their start and end apart: 18 -> 18, of which waited for: 3 -> 3; matrix products, arithmetic and copies ran while one was open for 2% -> 2% of each run, Pallas kernels for 53% -> 50%
where the time goes in v5:
time: 75.2 us; the launch traced here: 74.9 us
  Pallas kernels  43.9 us (58%)
  starting transfers between devices  22 us (29%)
  waiting for transfers between devices  4.65 us (6%)
  other arithmetic  1.62 us (2%)
  between operations  1.55 us (2%)
  local copies, waits for them, and re-layouts  1.19 us (2%)
    pallas_call x5, Pallas kernels, down_units(): pl.pallas_call(functools.partial(down_kernel, count, first, len(later), c...  29.1 us
    ppermute x18, starting transfers between devices, send(): return lax.ppermute(value.astype(bf16), ('tensor', 'replica'), pairs)  22 us
    pallas_call x5, Pallas kernels, query_units(): pl.pallas_call(functools.partial(query_kernel, info), in_specs=in_specs +...  13.8 us
    ppermute x18, waiting for transfers between devices, send(): return lax.ppermute(value.astype(bf16), ('tensor', 'replica'), pairs)  4.65 us
  transfers between devices with their start and end apart: 18, of which 3 were waited for; matrix products, arithmetic and copies ran while one was open for 2% of the time, Pallas kernels for 50%

profile of v5, /device:TPU:0, one launch (start us, length us, event | category | flops | bytes accessed | tf_op | source)
XLA Modules:
  0.0 74.9 jit_solution(2004536071495650627)
XLA Ops:
  0.7 1.2 %copy-done = bf16[1,3584,128]{2,1,0:T(8,128)(2,1)S(1)} copy-done((bf16[1,3584,128]{2,1,0:T(8,128)(2,1)S(1)}, bf16[1,3584,128]{2,1,0:T(8,128)(2,1)}, u32[]{:S(2)}) %copy-start) | copy-done | bytes 917528
  1.8 4.1 %down_units.5 = (bf16[8,128,128]{2,1,0:T(8,128)(2,1)S(1)}, bf16[128,3584]{1,0:T(8,128)(2,1)S(1)}, bf16[256,128]{1,0:T(8,128)(2,1)S(1)}) custom-call(s32[1]{0:T(128)} %bitcast.7.units, bf16[3584,128]{1,0:T(8,128)(2,1)S(1)} %bitcast.20, bf16[3584,8192]{1,0:T(8,128)(2,1)} %refs_2_.1), custom_call_target="tpu_custom_call" | custom-call | flops 939524096 | bytes 7340032 | tf_op jit(solution)/shard_map/down_units/pallas_call | solution.py:228
  5.9 3.0 %collective-permute-start = (bf16[8,128,128]{2,1,0:T(8,128)(2,1)S(1)}, bf16[8,128,128]{2,1,0:T(8,128)(2,1)S(1)}, u32[]{:S(2)}, u32[]{:S(2)}) collective-permute-start(bf16[8,128,128]{2,1,0:T(8,128)(2,1)S(1)} %get-tuple-element.54), channel_id=1, source_target_pairs={{0,2},{1,3},{2,0},{3,1},{4,6},{5,7},{6,4},{7,5},{8,10},{9,11},{10,... | collective-permute-start | bytes 786440 | tf_op jit(solution)/shard_map/ppermute | solution.py:395
  8.9 0.1 pad_add_fusion.3.units
  9.0 6.6 %down_units.6 = (f32[8,128,128]{2,1,0:T(8,128)S(1)}, bf16[8,128,128]{2,1,0:T(8,128)(2,1)S(1)}) custom-call(s32[2]{0:T(128)S(1)} %pad_add_fusion.3.units, bf16[128,3584]{1,0:T(8,128)(2,1)S(1)} %get-tuple-element.63.refs_0_.refs_1_, bf16[3584,8192]{1,0:T(8,128)(2,1)} %refs_2_.1, bf16[256,128]{1,0:T(8,128)(2,1)S(1)} %get-tuple-element.52.refs_2_.refs_3_.refs_4_), custom_call_target="tpu_custom_call" | custom-call | flops 1879048192 | bytes 14680064 | tf_op jit(solution)/shard_map/down_units/pallas_call | solution.py:228
  15.6 0.1 collective-permute-start.1
  15.7 0.1 pad_add_fusion.2.units
  15.8 0.1 pad_add_fusion.1.units
  15.9 0.0 collective-permute-done
  15.9 0.1 fusion
  15.9 2.2 %collective-permute-start.2 = (bf16[8,128,128]{2,1,0:T(8,128)(2,1)S(1)}, bf16[8,128,128]{2,1,0:T(8,128)(2,1)S(1)}, u32[]{:S(2)}, u32[]{:S(2)}) collective-permute-start(bf16[8,128,128]{2,1,0:T(8,128)(2,1)S(1)} %fusion), channel_id=1, source_target_pairs={{0,4},{1,5},{2,6},{3,7},{4,0},{5,1},{6,2},{7,3},{8,12},{9,13},{10,... | collective-permute-start | bytes 786440 | tf_op jit(solution)/shard_map/ppermute | solution.py:395
  18.1 6.6 %down_units.7 = (f32[8,128,128]{2,1,0:T(8,128)S(1)}, bf16[8,128,128]{2,1,0:T(8,128)(2,1)S(1)}) custom-call(s32[2]{0:T(128)S(1)} %pad_add_fusion.2.units, bf16[128,3584]{1,0:T(8,128)(2,1)S(1)} %get-tuple-element.63.refs_0_.refs_1_, bf16[3584,8192]{1,0:T(8,128)(2,1)} %refs_2_.1, bf16[256,128]{1,0:T(8,128)(2,1)S(1)} %get-tuple-element.52.refs_2_.refs_3_.refs_4_), custom_call_target="tpu_custom_call" | custom-call | flops 1879048192 | bytes 14680064 | tf_op jit(solution)/shard_map/down_units/pallas_call | solution.py:228
  24.7 0.0 collective-permute-done.1
  24.7 0.1 fusion.1
  24.7 0.4 collective-permute-start.5
  25.2 1.6 %collective-permute-start.3 = (bf16[8,128,128]{2,1,0:T(8,128)(2,1)S(1)}, bf16[8,128,128]{2,1,0:T(8,128)(2,1)S(1)}, u32[]{:S(2)}, u32[]{:S(2)}) collective-permute-start(bf16[8,128,128]{2,1,0:T(8,128)(2,1)S(1)} %get-tuple-element.61), channel_id=1, source_target_pairs={{0,2},{1,3},{2,0},{3,1},{4,6},{5,7},{6,4},{7,5},{8,10},{9,11},{10,... | collective-permute-start | bytes 786440 | tf_op jit(solution)/shard_map/ppermute | solution.py:395
  26.8 0.0 collective-permute-done.2
  26.8 0.1 add_convert_fusion.2
  26.9 0.1 collective-permute-start.4
  26.9 6.8 %down_units.8 = (f32[8,128,128]{2,1,0:T(8,128)S(1)}, bf16[8,128,128]{2,1,0:T(8,128)(2,1)S(1)}) custom-call(s32[2]{0:T(128)S(1)} %pad_add_fusion.1.units, bf16[128,3584]{1,0:T(8,128)(2,1)S(1)} %get-tuple-element.63.refs_0_.refs_1_, bf16[3584,8192]{1,0:T(8,128)(2,1)} %refs_2_.1, bf16[256,128]{1,0:T(8,128)(2,1)S(1)} %get-tuple-element.52.refs_2_.refs_3_.refs_4_), custom_call_target="tpu_custom_call" | custom-call | flops 1879048192 | bytes 14680064 | tf_op jit(solution)/shard_map/down_units/pallas_call | solution.py:228
  33.7 0.5 collective-permute-start.7
  34.2 0.0 collective-permute-done.5
  34.2 0.1 fusion.2
  34.4 0.0 collective-permute-done.3
  34.4 0.0 collective-permute-done.4
  34.4 0.1 add_convert_fusion.1
  34.5 0.3 collective-permute-start.6
  34.8 3.5 %collective-permute-start.8 = (bf16[8,128,128]{2,1,0:T(8,128)(2,1)S(1)}, bf16[8,128,128]{2,1,0:T(8,128)(2,1)S(1)}, u32[]{:S(2)}, u32[]{:S(2)}) collective-permute-start(bf16[8,128,128]{2,1,0:T(8,128)(2,1)S(1)} %add_convert_fusion.1), channel_id=1, source_target_pairs={{0,4},{1,5},{2,6},{3,7},{4,0},{5,1},{6,2},{7,3},{8,12},{9,13},{10,... | collective-permute-start | bytes 786440 | tf_op jit(solution)/shard_map/ppermute | solution.py:395
  38.3 0.1 pad_add_fusion.units
  38.3 5.0 %down_units.9 = (f32[8,128,128]{2,1,0:T(8,128)S(1)}, bf16[1024,1024]{1,0:T(8,128)(2,1)S(1)}, bf16[1024,1024]{1,0:T(8,128)(2,1)S(1)}) custom-call(s32[3]{0:T(128)S(1)} %pad_add_fusion.units, bf16[1024,8192]{1,0:T(8,128)(2,1)} %refs_5_.5, bf16[128,3584]{1,0:T(8,128)(2,1)S(1)} %get-tuple-element.63.refs_0_.refs_1_, bf16[3584,8192]{1,0:T(8,128)(2,1)} %refs_2_.1, ...), custom_call_target="tpu_custom_call" | custom-call | flops 939524096 | bytes 7340032 | tf_op jit(solution)/shard_map/down_units/pallas_call | solution.py:228
  43.4 0.0 collective-permute-done.7.refs_0_
  43.4 0.0 collective-permute-done.6.refs_1_
  43.4 0.0 collective-permute-done.8.refs_2_
  43.4 1.0 %update.1 = (bf16[8,128,128]{2,1,0:T(8,128)(2,1)}, bf16[8,128,128]{2,1,0:T(8,128)(2,1)S(1)}) custom-call(f32[8,128,128]{2,1,0:T(8,128)S(1)} %get-tuple-element.64.own_ref, bf16[8,128,128]{2,1,0:T(8,128)(2,1)S(1)} %collective-permute-done.7.refs_0_, bf16[8,128,128]{2,1,0:T(8,128)(2,1)S(1)} %collective-permute-done.6.refs_1_, ...), custom_call_target="tpu_custom_call" | custom-call | tf_op jit(solution)/shard_map/update/pallas_call | solution.py:260
  44.5 1.2 %collective-permute-start.9 = (bf16[8,128,128]{2,1,0:T(8,128)(2,1)S(1)}, bf16[8,128,128]{2,1,0:T(8,128)(2,1)S(1)}, u32[]{:S(2)}, u32[]{:S(2)}) collective-permute-start(bf16[8,128,128]{2,1,0:T(8,128)(2,1)S(1)} %get-tuple-element.71.refs_0_), channel_id=1, source_target_pairs={{0,4},{1,5},{2,6},{3,7},{4,0},{5,1},{6,2},{7,3},{8,12},{9,13},{10,... | collective-permute-start | bytes 786440 | tf_op jit(solution)/shard_map/ppermute | solution.py:395
  45.7 0.0 collective-permute-start.14
  45.7 0.1 pad_add_fusion.4.units
  45.7 0.1 pad_add_fusion.5.units
  45.8 1.5 %collective-permute-start.11 = (bf16[8,128,128]{2,1,0:T(8,128)(2,1)S(1)}, bf16[8,128,128]{2,1,0:T(8,128)(2,1)S(1)}, u32[]{:S(2)}, u32[]{:S(2)}) collective-permute-start(bf16[8,128,128]{2,1,0:T(8,128)(2,1)S(1)} %get-tuple-element.71.refs_0_), channel_id=1, source_target_pairs={{0,2},{1,3},{2,0},{3,1},{4,6},{5,7},{6,4},{7,5},{8,10},{9,11},{10,... | collective-permute-start | bytes 786440 | tf_op jit(solution)/shard_map/ppermute | solution.py:395
  47.3 0.1 pad_add_fusion.6.units
  48.1 2.5 %query_units.5 = (f32[1024,128]{1,0:T(8,128)S(1)}, f32[128,128]{1,0:T(8,128)S(1)}, bf16[1024,1024]{1,0:T(8,128)(2,1)S(1)}) custom-call(s32[2]{0:T(128)S(1)} %pad_add_fusion.4.units, bf16[8,128,128]{2,1,0:T(8,128)(2,1)S(1)} %get-tuple-element.71.refs_0_, f32[64,128]{1,0:T(8,128)S(1)} %bitcast.21, bf16[1024,1024]{1,0:T(8,128)(2,1)S(1)} %get-tuple-element.72.refs_2_, ...), custom_call_target="tpu_custom_call" | custom-call | flops 268435456 | bytes 2097152 | tf_op jit(solution)/shard_map/query_units/pallas_call | solution.py:351
  50.6 0.9 %collective-permute-done.9.refs_1_ = bf16[8,128,128]{2,1,0:T(8,128)(2,1)S(1)} collective-permute-done((bf16[8,128,128]{2,1,0:T(8,128)(2,1)S(1)}, bf16[8,128,128]{2,1,0:T(8,128)(2,1)S(1)}, u32[]{:S(2)}, u32[]{:S(2)}) %collective-permute-start.9) | collective-permute-done | bytes 262176 | tf_op jit(solution)/shard_map/ppermute | solution.py:395
  51.5 0.0 collective-permute-start.10
  51.5 0.0 collective-permute-done.14
  51.5 3.4 %collective-permute-start.15 = (bf16[8,128,128]{2,1,0:T(8,128)(2,1)S(1)}, bf16[8,128,128]{2,1,0:T(8,128)(2,1)S(1)}, u32[]{:S(2)}, u32[]{:S(2)}) collective-permute-start(bf16[8,128,128]{2,1,0:T(8,128)(2,1)S(1)} %collective-permute-done.14), channel_id=1, source_target_pairs={{0,4},{1,5},{2,6},{3,7},{4,0},{5,1},{6,2},{7,3},{8,12},{9,13},{10,... | collective-permute-start | bytes 786440 | tf_op jit(solution)/shard_map/ppermute | solution.py:395
  54.9 0.1 pad_add_fusion.7.units
  55.0 1.6 %collective-permute-start.13 = (bf16[8,128,128]{2,1,0:T(8,128)(2,1)S(1)}, bf16[8,128,128]{2,1,0:T(8,128)(2,1)S(1)}, u32[]{:S(2)}, u32[]{:S(2)}) collective-permute-start(bf16[8,128,128]{2,1,0:T(8,128)(2,1)S(1)} %collective-permute-done.9.refs_1_), channel_id=1, source_target_pairs={{0,2},{1,3},{2,0},{3,1},{4,6},{5,7},{6,4},{7,5},{8,10},{9,11},{10,... | collective-permute-start | bytes 786440 | tf_op jit(solution)/shard_map/ppermute | solution.py:395
  56.6 0.0 collective-permute-done.11.refs_0_
  56.6 3.7 %query_units.6 = (f32[1024,128]{1,0:T(8,128)S(1)}, f32[128,128]{1,0:T(8,128)S(1)}, bf16[1024,1024]{1,0:T(8,128)(2,1)S(1)}, bf16[1024,1024]{1,0:T(8,128)(2,1)S(1)}) custom-call(s32[4]{0:T(128)S(1)} %pad_add_fusion.5.units, bf16[8,128,128]{2,1,0:T(8,128)(2,1)S(1)} %collective-permute-done.11.refs_0_, bf16[8,128,128]{2,1,0:T(8,128)(2,1)S(1)} %collective-permute-done.9.refs_1_, ...), custom_call_target="tpu_custom_call" | custom-call | flops 536870912 | bytes 4194304 | tf_op jit(solution)/shard_map/query_units/pallas_call | solution.py:351
  60.3 0.0 collective-permute-done.10
  60.3 0.4 collective-permute-start.12
  60.8 0.0 collective-permute-done.15
  60.8 1.2 %collective-permute-start.17 = (bf16[8,128,128]{2,1,0:T(8,128)(2,1)S(1)}, bf16[8,128,128]{2,1,0:T(8,128)(2,1)S(1)}, u32[]{:S(2)}, u32[]{:S(2)}) collective-permute-start(bf16[8,128,128]{2,1,0:T(8,128)(2,1)S(1)} %broadcast_select_fusion.1.refs_1_), channel_id=1, source_target_pairs={{0,2},{1,3},{2,0},{3,1},{4,6},{5,7},{6,4},{7,5},{8,10},{9,11},{10,... | collective-permute-start | bytes 786440 | tf_op jit(solution)/shard_map/ppermute | solution.py:395
  62.0 0.0 collective-permute-done.13.refs_0_
  62.0 3.7 %query_units.7 = (f32[1024,128]{1,0:T(8,128)S(1)}, f32[128,128]{1,0:T(8,128)S(1)}, bf16[1024,1024]{1,0:T(8,128)(2,1)S(1)}, bf16[1024,1024]{1,0:T(8,128)(2,1)S(1)}) custom-call(s32[4]{0:T(128)S(1)} %pad_add_fusion.6.units, bf16[8,128,128]{2,1,0:T(8,128)(2,1)S(1)} %collective-permute-done.13.refs_0_, bf16[8,128,128]{2,1,0:T(8,128)(2,1)S(1)} %broadcast_select_fusion.1.refs_1_, ...), custom_call_target="tpu_custom_call" | custom-call | flops 536870912 | bytes 4194304 | tf_op jit(solution)/shard_map/query_units/pallas_call | solution.py:351
  65.7 1.1 %collective-permute-done.12 = bf16[8,128,128]{2,1,0:T(8,128)(2,1)S(1)} collective-permute-done((bf16[8,128,128]{2,1,0:T(8,128)(2,1)S(1)}, bf16[8,128,128]{2,1,0:T(8,128)(2,1)S(1)}, u32[]{:S(2)}, u32[]{:S(2)}) %collective-permute-start.12) | collective-permute-done | bytes 262176 | tf_op jit(solution)/shard_map/ppermute | solution.py:395
  66.8 1.1 %collective-permute-start.16 = (bf16[8,128,128]{2,1,0:T(8,128)(2,1)S(1)}, bf16[8,128,128]{2,1,0:T(8,128)(2,1)S(1)}, u32[]{:S(2)}, u32[]{:S(2)}) collective-permute-start(bf16[8,128,128]{2,1,0:T(8,128)(2,1)S(1)} %broadcast_select_fusion.refs_1_), channel_id=1, source_target_pairs={{0,2},{1,3},{2,0},{3,1},{4,6},{5,7},{6,4},{7,5},{8,10},{9,11},{10,... | collective-permute-start | bytes 786440 | tf_op jit(solution)/shard_map/ppermute | solution.py:395
  67.9 0.1 select_reduce_fusion.1
  68.0 0.1 select_reduce_fusion
  68.1 0.0 collective-permute-done.17.refs_0_
  68.1 2.1 %query_units.8 = (f32[1024,128]{1,0:T(8,128)S(1)}, f32[128,128]{1,0:T(8,128)S(1)}, bf16[1024,1024]{1,0:T(8,128)(2,1)S(1)}) custom-call(s32[3]{0:T(128)S(1)} %pad_add_fusion.7.units, bf16[8,128,128]{2,1,0:T(8,128)(2,1)S(1)} %collective-permute-done.17.refs_0_, bf16[8,128,128]{2,1,0:T(8,128)(2,1)S(1)} %broadcast_select_fusion.refs_1_, f32[64,128]{1,0:T(8,128)S(1)} %bitcast.24, ...), custom_call_target="tpu_custom_call" | custom-call | flops 536870912 | bytes 4194304 | tf_op jit(solution)/shard_map/query_units/pallas_call | solution.py:351
  70.3 0.3 fusion.3
  70.6 2.7 %collective-permute-done.16.refs_0_ = bf16[8,128,128]{2,1,0:T(8,128)(2,1)S(1)} collective-permute-done((bf16[8,128,128]{2,1,0:T(8,128)(2,1)S(1)}, bf16[8,128,128]{2,1,0:T(8,128)(2,1)S(1)}, u32[]{:S(2)}, u32[]{:S(2)}) %collective-permute-start.16) | collective-permute-done | bytes 262176 | tf_op jit(solution)/shard_map/ppermute | solution.py:395
  73.2 1.7 %query_units.9 = bf16[1024,128]{1,0:T(8,128)(2,1)} custom-call(s32[1]{0:T(128)} %bitcast.7.units, bf16[8,128,128]{2,1,0:T(8,128)(2,1)S(1)} %collective-permute-done.16.refs_0_, f32[64,128]{1,0:T(8,128)S(1)} %bitcast.25, bf16[1024,1024]{1,0:T(8,128)(2,1)S(1)} %get-tuple-element.95.refs_2_, f32[1024,128]{1,0:T(8,128)S(1)} %get-tuple-element.96.refs_3_, ...), custom_call_target="tpu_custom_call" | custom-call | flops 268435456 | bytes 2097152 | tf_op jit(solution)/shard_map/query_units/pallas_call | solution.py:351
  (12 shorter events, 0.1 us)
Async XLA Ops:
  0.7 1.2 %copy-start = (bf16[1,3584,128]{2,1,0:T(8,128)(2,1)S(1)}, bf16[1,3584,128]{2,1,0:T(8,128)(2,1)}, u32[]{:S(2)}) copy-start(bf16[1,3584,128]{2,1,0:T(8,128)(2,1)} %param.7) | copy-start | bytes 2752516
  5.9 9.9 %collective-permute-start = (bf16[8,128,128]{2,1,0:T(8,128)(2,1)S(1)}, bf16[8,128,128]{2,1,0:T(8,128)(2,1)S(1)}, u32[]{:S(2)}, u32[]{:S(2)}) collective-permute-start(bf16[8,128,128]{2,1,0:T(8,128)(2,1)S(1)} %get-tuple-element.54), channel_id=1, source_target_pairs={{0,2},{1,3},{2,0},{3,1},{4,6},{5,7},{6,4},{7,5},{8,10},{9,11},{10,... | collective-permute-start | bytes 786440 | tf_op jit(solution)/shard_map/ppermute | solution.py:395
  15.6 9.1 %collective-permute-start.1 = (bf16[8,128,128]{2,1,0:T(8,128)(2,1)S(1)}, bf16[8,128,128]{2,1,0:T(8,128)(2,1)S(1)}, u32[]{:S(2)}, u32[]{:S(2)}) collective-permute-start(bf16[8,128,128]{2,1,0:T(8,128)(2,1)S(1)} %get-tuple-element.57), channel_id=1, source_target_pairs={{0,2},{1,3},{2,0},{3,1},{4,6},{5,7},{6,4},{7,5},{8,10},{9,11},{10,... | collective-permute-start | bytes 786440 | tf_op jit(solution)/shard_map/ppermute | solution.py:395
  15.9 10.8 %collective-permute-start.2 = (bf16[8,128,128]{2,1,0:T(8,128)(2,1)S(1)}, bf16[8,128,128]{2,1,0:T(8,128)(2,1)S(1)}, u32[]{:S(2)}, u32[]{:S(2)}) collective-permute-start(bf16[8,128,128]{2,1,0:T(8,128)(2,1)S(1)} %fusion), channel_id=1, source_target_pairs={{0,4},{1,5},{2,6},{3,7},{4,0},{5,1},{6,2},{7,3},{8,12},{9,13},{10,... | collective-permute-start | bytes 786440 | tf_op jit(solution)/shard_map/ppermute | solution.py:395
  24.7 9.5 %collective-permute-start.5 = (bf16[8,128,128]{2,1,0:T(8,128)(2,1)S(1)}, bf16[8,128,128]{2,1,0:T(8,128)(2,1)S(1)}, u32[]{:S(2)}, u32[]{:S(2)}) collective-permute-start(bf16[8,128,128]{2,1,0:T(8,128)(2,1)S(1)} %fusion.1), channel_id=1, source_target_pairs={{0,4},{1,5},{2,6},{3,7},{4,0},{5,1},{6,2},{7,3},{8,12},{9,13},{10,... | collective-permute-start | bytes 786440 | tf_op jit(solution)/shard_map/ppermute | solution.py:395
  25.2 9.2 %collective-permute-start.3 = (bf16[8,128,128]{2,1,0:T(8,128)(2,1)S(1)}, bf16[8,128,128]{2,1,0:T(8,128)(2,1)S(1)}, u32[]{:S(2)}, u32[]{:S(2)}) collective-permute-start(bf16[8,128,128]{2,1,0:T(8,128)(2,1)S(1)} %get-tuple-element.61), channel_id=1, source_target_pairs={{0,2},{1,3},{2,0},{3,1},{4,6},{5,7},{6,4},{7,5},{8,10},{9,11},{10,... | collective-permute-start | bytes 786440 | tf_op jit(solution)/shard_map/ppermute | solution.py:395
  26.9 7.5 %collective-permute-start.4 = (bf16[8,128,128]{2,1,0:T(8,128)(2,1)S(1)}, bf16[8,128,128]{2,1,0:T(8,128)(2,1)S(1)}, u32[]{:S(2)}, u32[]{:S(2)}) collective-permute-start(bf16[8,128,128]{2,1,0:T(8,128)(2,1)S(1)} %add_convert_fusion.2), channel_id=1, source_target_pairs={{0,1},{1,0},{2,3},{3,2},{4,8},{5,9},{6,10},{7,11},{8,4},{9,5},{10,... | collective-permute-start | bytes 786440 | tf_op jit(solution)/shard_map/ppermute | solution.py:395
  33.7 9.7 %collective-permute-start.7 = (bf16[8,128,128]{2,1,0:T(8,128)(2,1)S(1)}, bf16[8,128,128]{2,1,0:T(8,128)(2,1)S(1)}, u32[]{:S(2)}, u32[]{:S(2)}) collective-permute-start(bf16[8,128,128]{2,1,0:T(8,128)(2,1)S(1)} %get-tuple-element.66), channel_id=1, source_target_pairs={{0,2},{1,3},{2,0},{3,1},{4,6},{5,7},{6,4},{7,5},{8,10},{9,11},{10,... | collective-permute-start | bytes 786440 | tf_op jit(solution)/shard_map/ppermute | solution.py:395
  34.5 8.9 %collective-permute-start.6 = (bf16[8,128,128]{2,1,0:T(8,128)(2,1)S(1)}, bf16[8,128,128]{2,1,0:T(8,128)(2,1)S(1)}, u32[]{:S(2)}, u32[]{:S(2)}) collective-permute-start(bf16[8,128,128]{2,1,0:T(8,128)(2,1)S(1)} %fusion.2), channel_id=1, source_target_pairs={{0,1},{1,0},{2,3},{3,2},{4,8},{5,9},{6,10},{7,11},{8,4},{9,5},{10,... | collective-permute-start | bytes 786440 | tf_op jit(solution)/shard_map/ppermute | solution.py:395
  34.8 8.6 %collective-permute-start.8 = (bf16[8,128,128]{2,1,0:T(8,128)(2,1)S(1)}, bf16[8,128,128]{2,1,0:T(8,128)(2,1)S(1)}, u32[]{:S(2)}, u32[]{:S(2)}) collective-permute-start(bf16[8,128,128]{2,1,0:T(8,128)(2,1)S(1)} %add_convert_fusion.1), channel_id=1, source_target_pairs={{0,4},{1,5},{2,6},{3,7},{4,0},{5,1},{6,2},{7,3},{8,12},{9,13},{10,... | collective-permute-start | bytes 786440 | tf_op jit(solution)/shard_map/ppermute | solution.py:395
  38.3 5.1 %copy-start.2 = (bf16[1,8,128,128]{3,2,1,0:T(8,128)(2,1)S(1)}, bf16[1,8,128,128]{3,2,1,0:T(8,128)(2,1)}, u32[]{:S(2)}) copy-start(bf16[1,8,128,128]{3,2,1,0:T(8,128)(2,1)} %param.9) | copy-start | bytes 786436
  38.3 9.7 %copy-start.1 = (f32[8192]{0:T(1024)S(1)}, f32[8192]{0:T(1024)}, u32[]{:S(2)}) copy-start(f32[8192]{0:T(1024)} %param.10) | copy-start | bytes 98308
  44.5 7.0 %collective-permute-start.9 = (bf16[8,128,128]{2,1,0:T(8,128)(2,1)S(1)}, bf16[8,128,128]{2,1,0:T(8,128)(2,1)S(1)}, u32[]{:S(2)}, u32[]{:S(2)}) collective-permute-start(bf16[8,128,128]{2,1,0:T(8,128)(2,1)S(1)} %get-tuple-element.71.refs_0_), channel_id=1, source_target_pairs={{0,4},{1,5},{2,6},{3,7},{4,0},{5,1},{6,2},{7,3},{8,12},{9,13},{10,... | collective-permute-start | bytes 786440 | tf_op jit(solution)/shard_map/ppermute | solution.py:395
  45.7 5.8 %collective-permute-start.14 = (bf16[8,128,128]{2,1,0:T(8,128)(2,1)S(1)}, bf16[8,128,128]{2,1,0:T(8,128)(2,1)S(1)}, u32[]{:S(2)}, u32[]{:S(2)}) collective-permute-start(bf16[8,128,128]{2,1,0:T(8,128)(2,1)S(1)} %get-tuple-element.71.refs_0_), channel_id=1, source_target_pairs={{0,1},{1,0},{2,3},{3,2},{4,8},{5,9},{6,10},{7,11},{8,4},{9,5},{10,... | collective-permute-start | bytes 786440 | tf_op jit(solution)/shard_map/ppermute | solution.py:395
  45.8 10.8 %collective-permute-start.11 = (bf16[8,128,128]{2,1,0:T(8,128)(2,1)S(1)}, bf16[8,128,128]{2,1,0:T(8,128)(2,1)S(1)}, u32[]{:S(2)}, u32[]{:S(2)}) collective-permute-start(bf16[8,128,128]{2,1,0:T(8,128)(2,1)S(1)} %get-tuple-element.71.refs_0_), channel_id=1, source_target_pairs={{0,2},{1,3},{2,0},{3,1},{4,6},{5,7},{6,4},{7,5},{8,10},{9,11},{10,... | collective-permute-start | bytes 786440 | tf_op jit(solution)/shard_map/ppermute | solution.py:395
  51.5 8.9 %collective-permute-start.10 = (bf16[8,128,128]{2,1,0:T(8,128)(2,1)S(1)}, bf16[8,128,128]{2,1,0:T(8,128)(2,1)S(1)}, u32[]{:S(2)}, u32[]{:S(2)}) collective-permute-start(bf16[8,128,128]{2,1,0:T(8,128)(2,1)S(1)} %collective-permute-done.9.refs_1_), channel_id=1, source_target_pairs={{0,1},{1,0},{2,3},{3,2},{4,8},{5,9},{6,10},{7,11},{8,4},{9,5},{10,... | collective-permute-start | bytes 786440 | tf_op jit(solution)/shard_map/ppermute | solution.py:395
  51.5 9.3 %collective-permute-start.15 = (bf16[8,128,128]{2,1,0:T(8,128)(2,1)S(1)}, bf16[8,128,128]{2,1,0:T(8,128)(2,1)S(1)}, u32[]{:S(2)}, u32[]{:S(2)}) collective-permute-start(bf16[8,128,128]{2,1,0:T(8,128)(2,1)S(1)} %collective-permute-done.14), channel_id=1, source_target_pairs={{0,4},{1,5},{2,6},{3,7},{4,0},{5,1},{6,2},{7,3},{8,12},{9,13},{10,... | collective-permute-start | bytes 786440 | tf_op jit(solution)/shard_map/ppermute | solution.py:395
  55.0 7.0 %collective-permute-start.13 = (bf16[8,128,128]{2,1,0:T(8,128)(2,1)S(1)}, bf16[8,128,128]{2,1,0:T(8,128)(2,1)S(1)}, u32[]{:S(2)}, u32[]{:S(2)}) collective-permute-start(bf16[8,128,128]{2,1,0:T(8,128)(2,1)S(1)} %collective-permute-done.9.refs_1_), channel_id=1, source_target_pairs={{0,2},{1,3},{2,0},{3,1},{4,6},{5,7},{6,4},{7,5},{8,10},{9,11},{10,... | collective-permute-start | bytes 786440 | tf_op jit(solution)/shard_map/ppermute | solution.py:395
  60.3 6.4 %collective-permute-start.12 = (bf16[8,128,128]{2,1,0:T(8,128)(2,1)S(1)}, bf16[8,128,128]{2,1,0:T(8,128)(2,1)S(1)}, u32[]{:S(2)}, u32[]{:S(2)}) collective-permute-start(bf16[8,128,128]{2,1,0:T(8,128)(2,1)S(1)} %collective-permute-done.10), channel_id=1, source_target_pairs={{0,4},{1,5},{2,6},{3,7},{4,0},{5,1},{6,2},{7,3},{8,12},{9,13},{10,... | collective-permute-start | bytes 786440 | tf_op jit(solution)/shard_map/ppermute | solution.py:395
  60.8 7.3 %collective-permute-start.17 = (bf16[8,128,128]{2,1,0:T(8,128)(2,1)S(1)}, bf16[8,128,128]{2,1,0:T(8,128)(2,1)S(1)}, u32[]{:S(2)}, u32[]{:S(2)}) collective-permute-start(bf16[8,128,128]{2,1,0:T(8,128)(2,1)S(1)} %broadcast_select_fusion.1.refs_1_), channel_id=1, source_target_pairs={{0,2},{1,3},{2,0},{3,1},{4,6},{5,7},{6,4},{7,5},{8,10},{9,11},{10,... | collective-permute-start | bytes 786440 | tf_op jit(solution)/shard_map/ppermute | solution.py:395
  62.0 5.9 %copy-start.3 = (s32[1,4]{1,0:T(1,128)S(1)}, s32[1,4]{1,0:T(1,128)}, u32[]{:S(2)}) copy-start(s32[1,4]{1,0:T(1,128)} %param.13) | copy-start | bytes 52
  66.8 6.4 %collective-permute-start.16 = (bf16[8,128,128]{2,1,0:T(8,128)(2,1)S(1)}, bf16[8,128,128]{2,1,0:T(8,128)(2,1)S(1)}, u32[]{:S(2)}, u32[]{:S(2)}) collective-permute-start(bf16[8,128,128]{2,1,0:T(8,128)(2,1)S(1)} %broadcast_select_fusion.refs_1_), channel_id=1, source_target_pairs={{0,2},{1,3},{2,0},{3,1},{4,6},{5,7},{6,4},{7,5},{8,10},{9,11},{10,... | collective-permute-start | bytes 786440 | tf_op jit(solution)/shard_map/ppermute | solution.py:395

commit v6 on v5

--- a/solution.py
+++ b/solution.py
@@ -454,12 +454,13 @@
     inner3, state = after(inner3, state)
     unit3 = jnp.where(inner, inner3, send(inner3, TWINS))
     side2 = send(unit2, ACROSS)
-    state, ahead = query([side1, unit2], [theirs[1], mine[2]], [theirs[2], mine[3]], ahead, state)
+    now, kept = ahead
+    state, ahead = query([side1], [theirs[1]], [theirs[2], mine[3]], [now], state)
     unit3, state = after(unit3, state)
     prefix, lengths, _ = after(prefix_len[0], seg_lengths[0], unit3)
     tables = rotary_tables(positions_of(prefix, lengths, tokens))
     side3 = send(unit3, ACROSS)
-    state, ahead = query([side2, unit3], [theirs[2], mine[3]], [theirs[3]], ahead, state)
+    state, ahead = query([unit2, side2, unit3], [mine[2], theirs[2], mine[3]], [theirs[3]], [kept, *ahead], state)
     query_one, = query_units([side3], [theirs[3]], [], gain, query_weight, ahead, state, tables)
     return (updated[None], query_one[None])
 

time: 75.2 us -> 75.2 us (level)
  Pallas kernels: 43.9 us -> 45.3 us
  waiting for transfers between devices: 4.65 us -> 3.27 us
    pallas_call x5, Pallas kernels: 13.8 us -> 15.2 us  [query_units(): pl.pallas_call(functools.partial(query_kernel, info), in_specs=in_specs +...]
    ppermute x18, waiting for transfers between devices: 4.65 us -> 3.27 us  [send(): return lax.ppermute(value.astype(bf16), ('tensor', 'replica'), pairs)]
  transfers between devices with their start and end apart: 18 -> 18, of which waited for: 3 -> 3; matrix products, arithmetic and copies ran while one was open for 2% -> 2% of each run, Pallas kernels for 50% -> 51%
where the time goes in v6:
time: 75.2 us; the launch traced here: 74.9 us
  Pallas kernels  45.3 us (60%)
  starting transfers between devices  22 us (29%)
  waiting for transfers between devices  3.27 us (4%)
  other arithmetic  1.64 us (2%)
  between operations  1.55 us (2%)
  local copies, waits for them, and re-layouts  1.19 us (2%)
    pallas_call x5, Pallas kernels, down_units(): pl.pallas_call(functools.partial(down_kernel, count, first, len(later), c...  29.1 us
    ppermute x18, starting transfers between devices, send(): return lax.ppermute(value.astype(bf16), ('tensor', 'replica'), pairs)  22 us
    pallas_call x5, Pallas kernels, query_units(): pl.pallas_call(functools.partial(query_kernel, info), in_specs=in_specs +...  15.2 us
    ppermute x18, waiting for transfers between devices, send(): return lax.ppermute(value.astype(bf16), ('tensor', 'replica'), pairs)  3.27 us
  transfers between devices with their start and end apart: 18, of which 3 were waited for; matrix products, arithmetic and copies ran while one was open for 2% of the time, Pallas kernels for 51%

profile of v6, /device:TPU:0, one launch (start us, length us, event | category | flops | bytes accessed | tf_op | source)
XLA Modules:
  0.0 74.9 jit_solution(2384250053083795714)
XLA Ops:
  0.7 1.2 %copy-done = bf16[1,3584,128]{2,1,0:T(8,128)(2,1)S(1)} copy-done((bf16[1,3584,128]{2,1,0:T(8,128)(2,1)S(1)}, bf16[1,3584,128]{2,1,0:T(8,128)(2,1)}, u32[]{:S(2)}) %copy-start) | copy-done | bytes 917528
  1.8 4.1 %down_units.5 = (bf16[8,128,128]{2,1,0:T(8,128)(2,1)S(1)}, bf16[128,3584]{1,0:T(8,128)(2,1)S(1)}, bf16[256,128]{1,0:T(8,128)(2,1)S(1)}) custom-call(s32[1]{0:T(128)} %bitcast.7.units, bf16[3584,128]{1,0:T(8,128)(2,1)S(1)} %bitcast.20, bf16[3584,8192]{1,0:T(8,128)(2,1)} %refs_2_.1), custom_call_target="tpu_custom_call" | custom-call | flops 939524096 | bytes 7340032 | tf_op jit(solution)/shard_map/down_units/pallas_call | solution.py:228
  5.9 3.0 %collective-permute-start = (bf16[8,128,128]{2,1,0:T(8,128)(2,1)S(1)}, bf16[8,128,128]{2,1,0:T(8,128)(2,1)S(1)}, u32[]{:S(2)}, u32[]{:S(2)}) collective-permute-start(bf16[8,128,128]{2,1,0:T(8,128)(2,1)S(1)} %get-tuple-element.54), channel_id=1, source_target_pairs={{0,2},{1,3},{2,0},{3,1},{4,6},{5,7},{6,4},{7,5},{8,10},{9,11},{10,... | collective-permute-start | bytes 786440 | tf_op jit(solution)/shard_map/ppermute | solution.py:395
  8.9 0.1 pad_add_fusion.3.units
  9.0 6.6 %down_units.6 = (f32[8,128,128]{2,1,0:T(8,128)S(1)}, bf16[8,128,128]{2,1,0:T(8,128)(2,1)S(1)}) custom-call(s32[2]{0:T(128)S(1)} %pad_add_fusion.3.units, bf16[128,3584]{1,0:T(8,128)(2,1)S(1)} %get-tuple-element.63.refs_0_.refs_1_, bf16[3584,8192]{1,0:T(8,128)(2,1)} %refs_2_.1, bf16[256,128]{1,0:T(8,128)(2,1)S(1)} %get-tuple-element.52.refs_2_.refs_3_.refs_4_), custom_call_target="tpu_custom_call" | custom-call | flops 1879048192 | bytes 14680064 | tf_op jit(solution)/shard_map/down_units/pallas_call | solution.py:228
  15.6 0.1 collective-permute-start.1
  15.7 0.1 pad_add_fusion.2.units
  15.8 0.1 pad_add_fusion.1.units
  15.9 0.0 collective-permute-done
  15.9 0.1 fusion
  15.9 2.2 %collective-permute-start.2 = (bf16[8,128,128]{2,1,0:T(8,128)(2,1)S(1)}, bf16[8,128,128]{2,1,0:T(8,128)(2,1)S(1)}, u32[]{:S(2)}, u32[]{:S(2)}) collective-permute-start(bf16[8,128,128]{2,1,0:T(8,128)(2,1)S(1)} %fusion), channel_id=1, source_target_pairs={{0,4},{1,5},{2,6},{3,7},{4,0},{5,1},{6,2},{7,3},{8,12},{9,13},{10,... | collective-permute-start | bytes 786440 | tf_op jit(solution)/shard_map/ppermute | solution.py:395
  18.1 6.6 %down_units.7 = (f32[8,128,128]{2,1,0:T(8,128)S(1)}, bf16[8,128,128]{2,1,0:T(8,128)(2,1)S(1)}) custom-call(s32[2]{0:T(128)S(1)} %pad_add_fusion.2.units, bf16[128,3584]{1,0:T(8,128)(2,1)S(1)} %get-tuple-element.63.refs_0_.refs_1_, bf16[3584,8192]{1,0:T(8,128)(2,1)} %refs_2_.1, bf16[256,128]{1,0:T(8,128)(2,1)S(1)} %get-tuple-element.52.refs_2_.refs_3_.refs_4_), custom_call_target="tpu_custom_call" | custom-call | flops 1879048192 | bytes 14680064 | tf_op jit(solution)/shard_map/down_units/pallas_call | solution.py:228
  24.7 0.0 collective-permute-done.1
  24.7 0.1 fusion.1
  24.7 0.4 collective-permute-start.5
  25.2 1.6 %collective-permute-start.3 = (bf16[8,128,128]{2,1,0:T(8,128)(2,1)S(1)}, bf16[8,128,128]{2,1,0:T(8,128)(2,1)S(1)}, u32[]{:S(2)}, u32[]{:S(2)}) collective-permute-start(bf16[8,128,128]{2,1,0:T(8,128)(2,1)S(1)} %get-tuple-element.61), channel_id=1, source_target_pairs={{0,2},{1,3},{2,0},{3,1},{4,6},{5,7},{6,4},{7,5},{8,10},{9,11},{10,... | collective-permute-start | bytes 786440 | tf_op jit(solution)/shard_map/ppermute | solution.py:395
  26.8 0.0 collective-permute-done.2
  26.8 0.1 add_convert_fusion.2
  26.9 0.1 collective-permute-start.4
  26.9 6.8 %down_units.8 = (f32[8,128,128]{2,1,0:T(8,128)S(1)}, bf16[8,128,128]{2,1,0:T(8,128)(2,1)S(1)}) custom-call(s32[2]{0:T(128)S(1)} %pad_add_fusion.1.units, bf16[128,3584]{1,0:T(8,128)(2,1)S(1)} %get-tuple-element.63.refs_0_.refs_1_, bf16[3584,8192]{1,0:T(8,128)(2,1)} %refs_2_.1, bf16[256,128]{1,0:T(8,128)(2,1)S(1)} %get-tuple-element.52.refs_2_.refs_3_.refs_4_), custom_call_target="tpu_custom_call" | custom-call | flops 1879048192 | bytes 14680064 | tf_op jit(solution)/shard_map/down_units/pallas_call | solution.py:228
  33.7 0.5 collective-permute-start.7
  34.2 0.0 collective-permute-done.5
  34.2 0.1 fusion.2
  34.4 0.0 collective-permute-done.3
  34.4 0.0 collective-permute-done.4
  34.4 0.1 add_convert_fusion.1
  34.5 0.3 collective-permute-start.6
  34.8 3.5 %collective-permute-start.8 = (bf16[8,128,128]{2,1,0:T(8,128)(2,1)S(1)}, bf16[8,128,128]{2,1,0:T(8,128)(2,1)S(1)}, u32[]{:S(2)}, u32[]{:S(2)}) collective-permute-start(bf16[8,128,128]{2,1,0:T(8,128)(2,1)S(1)} %add_convert_fusion.1), channel_id=1, source_target_pairs={{0,4},{1,5},{2,6},{3,7},{4,0},{5,1},{6,2},{7,3},{8,12},{9,13},{10,... | collective-permute-start | bytes 786440 | tf_op jit(solution)/shard_map/ppermute | solution.py:395
  38.3 0.1 pad_add_fusion.units
  38.3 5.0 %down_units.9 = (f32[8,128,128]{2,1,0:T(8,128)S(1)}, bf16[1024,1024]{1,0:T(8,128)(2,1)S(1)}, bf16[1024,1024]{1,0:T(8,128)(2,1)S(1)}) custom-call(s32[3]{0:T(128)S(1)} %pad_add_fusion.units, bf16[1024,8192]{1,0:T(8,128)(2,1)} %refs_7_.1, bf16[128,3584]{1,0:T(8,128)(2,1)S(1)} %get-tuple-element.63.refs_0_.refs_1_, bf16[3584,8192]{1,0:T(8,128)(2,1)} %refs_2_.1, ...), custom_call_target="tpu_custom_call" | custom-call | flops 939524096 | bytes 7340032 | tf_op jit(solution)/shard_map/down_units/pallas_call | solution.py:228
  43.4 0.0 collective-permute-done.7.refs_0_
  43.4 0.0 collective-permute-done.6.refs_1_
  43.4 0.0 collective-permute-done.8.refs_2_
  43.4 1.0 %update.1 = (bf16[8,128,128]{2,1,0:T(8,128)(2,1)}, bf16[8,128,128]{2,1,0:T(8,128)(2,1)S(1)}) custom-call(f32[8,128,128]{2,1,0:T(8,128)S(1)} %get-tuple-element.64.own_ref, bf16[8,128,128]{2,1,0:T(8,128)(2,1)S(1)} %collective-permute-done.7.refs_0_, bf16[8,128,128]{2,1,0:T(8,128)(2,1)S(1)} %collective-permute-done.6.refs_1_, ...), custom_call_target="tpu_custom_call" | custom-call | tf_op jit(solution)/shard_map/update/pallas_call | solution.py:260
  44.5 1.2 %collective-permute-start.9 = (bf16[8,128,128]{2,1,0:T(8,128)(2,1)S(1)}, bf16[8,128,128]{2,1,0:T(8,128)(2,1)S(1)}, u32[]{:S(2)}, u32[]{:S(2)}) collective-permute-start(bf16[8,128,128]{2,1,0:T(8,128)(2,1)S(1)} %get-tuple-element.71.refs_0_), channel_id=1, source_target_pairs={{0,4},{1,5},{2,6},{3,7},{4,0},{5,1},{6,2},{7,3},{8,12},{9,13},{10,... | collective-permute-start | bytes 786440 | tf_op jit(solution)/shard_map/ppermute | solution.py:395
  45.7 0.0 collective-permute-start.15
  45.7 0.1 pad_add_fusion.4.units
  45.7 0.1 pad_add_fusion.5.units
  45.8 1.5 %collective-permute-start.11 = (bf16[8,128,128]{2,1,0:T(8,128)(2,1)S(1)}, bf16[8,128,128]{2,1,0:T(8,128)(2,1)S(1)}, u32[]{:S(2)}, u32[]{:S(2)}) collective-permute-start(bf16[8,128,128]{2,1,0:T(8,128)(2,1)S(1)} %get-tuple-element.71.refs_0_), channel_id=1, source_target_pairs={{0,2},{1,3},{2,0},{3,1},{4,6},{5,7},{6,4},{7,5},{8,10},{9,11},{10,... | collective-permute-start | bytes 786440 | tf_op jit(solution)/shard_map/ppermute | solution.py:395
  47.3 0.1 pad_add_fusion.6.units
  48.1 2.5 %query_units.5 = (f32[1024,128]{1,0:T(8,128)S(1)}, f32[128,128]{1,0:T(8,128)S(1)}, bf16[1024,1024]{1,0:T(8,128)(2,1)S(1)}) custom-call(s32[2]{0:T(128)S(1)} %pad_add_fusion.4.units, bf16[8,128,128]{2,1,0:T(8,128)(2,1)S(1)} %get-tuple-element.71.refs_0_, f32[64,128]{1,0:T(8,128)S(1)} %bitcast.21, bf16[1024,1024]{1,0:T(8,128)(2,1)S(1)} %get-tuple-element.72.refs_2_, ...), custom_call_target="tpu_custom_call" | custom-call | flops 268435456 | bytes 2097152 | tf_op jit(solution)/shard_map/query_units/pallas_call | solution.py:351
  50.6 0.9 %collective-permute-done.9.refs_1_ = bf16[8,128,128]{2,1,0:T(8,128)(2,1)S(1)} collective-permute-done((bf16[8,128,128]{2,1,0:T(8,128)(2,1)S(1)}, bf16[8,128,128]{2,1,0:T(8,128)(2,1)S(1)}, u32[]{:S(2)}, u32[]{:S(2)}) %collective-permute-start.9) | collective-permute-done | bytes 262176 | tf_op jit(solution)/shard_map/ppermute | solution.py:395
  51.5 0.0 collective-permute-start.10
  51.5 0.0 collective-permute-done.15
  51.5 3.4 %collective-permute-start.16 = (bf16[8,128,128]{2,1,0:T(8,128)(2,1)S(1)}, bf16[8,128,128]{2,1,0:T(8,128)(2,1)S(1)}, u32[]{:S(2)}, u32[]{:S(2)}) collective-permute-start(bf16[8,128,128]{2,1,0:T(8,128)(2,1)S(1)} %collective-permute-done.15), channel_id=1, source_target_pairs={{0,4},{1,5},{2,6},{3,7},{4,0},{5,1},{6,2},{7,3},{8,12},{9,13},{10,... | collective-permute-start | bytes 786440 | tf_op jit(solution)/shard_map/ppermute | solution.py:395
  54.9 0.1 pad_add_fusion.7.units
  55.0 1.6 %collective-permute-start.13 = (bf16[8,128,128]{2,1,0:T(8,128)(2,1)S(1)}, bf16[8,128,128]{2,1,0:T(8,128)(2,1)S(1)}, u32[]{:S(2)}, u32[]{:S(2)}) collective-permute-start(bf16[8,128,128]{2,1,0:T(8,128)(2,1)S(1)} %collective-permute-done.9.refs_1_), channel_id=1, source_target_pairs={{0,2},{1,3},{2,0},{3,1},{4,6},{5,7},{6,4},{7,5},{8,10},{9,11},{10,... | collective-permute-start | bytes 786440 | tf_op jit(solution)/shard_map/ppermute | solution.py:395
  56.6 0.0 collective-permute-done.11.refs_0_
  56.6 3.7 %query_units.6 = (f32[1024,128]{1,0:T(8,128)S(1)}, f32[128,128]{1,0:T(8,128)S(1)}, bf16[1024,1024]{1,0:T(8,128)(2,1)S(1)}, bf16[1024,1024]{1,0:T(8,128)(2,1)S(1)}) custom-call(s32[4]{0:T(128)S(1)} %pad_add_fusion.5.units, bf16[8,128,128]{2,1,0:T(8,128)(2,1)S(1)} %collective-permute-done.11.refs_0_, bf16[8,128,128]{2,1,0:T(8,128)(2,1)S(1)} %collective-permute-done.9.refs_1_, ...), custom_call_target="tpu_custom_call" | custom-call | flops 536870912 | bytes 4194304 | tf_op jit(solution)/shard_map/query_units/pallas_call | solution.py:351
  60.3 0.0 collective-permute-done.10
  60.3 0.4 collective-permute-start.12
  60.8 0.0 collective-permute-done.16
  60.8 1.1 %collective-permute-start.17 = (bf16[8,128,128]{2,1,0:T(8,128)(2,1)S(1)}, bf16[8,128,128]{2,1,0:T(8,128)(2,1)S(1)}, u32[]{:S(2)}, u32[]{:S(2)}) collective-permute-start(bf16[8,128,128]{2,1,0:T(8,128)(2,1)S(1)} %broadcast_select_fusion.1.refs_0_), channel_id=1, source_target_pairs={{0,2},{1,3},{2,0},{3,1},{4,6},{5,7},{6,4},{7,5},{8,10},{9,11},{10,... | collective-permute-start | bytes 786440 | tf_op jit(solution)/shard_map/ppermute | solution.py:395
  62.0 0.0 collective-permute-done.13.refs_0_
  62.0 3.6 %query_units.7 = (f32[1024,128]{1,0:T(8,128)S(1)}, f32[128,128]{1,0:T(8,128)S(1)}, bf16[1024,1024]{1,0:T(8,128)(2,1)S(1)}, bf16[1024,1024]{1,0:T(8,128)(2,1)S(1)}) custom-call(s32[3]{0:T(128)S(1)} %pad_add_fusion.6.units, bf16[8,128,128]{2,1,0:T(8,128)(2,1)S(1)} %collective-permute-done.13.refs_0_, f32[64,128]{1,0:T(8,128)S(1)} %bitcast.23, ...), custom_call_target="tpu_custom_call" | custom-call | flops 268435456 | bytes 2097152 | tf_op jit(solution)/shard_map/query_units/pallas_call | solution.py:351
  65.6 1.2 %collective-permute-done.12 = bf16[8,128,128]{2,1,0:T(8,128)(2,1)S(1)} collective-permute-done((bf16[8,128,128]{2,1,0:T(8,128)(2,1)S(1)}, bf16[8,128,128]{2,1,0:T(8,128)(2,1)S(1)}, u32[]{:S(2)}, u32[]{:S(2)}) %collective-permute-start.12) | collective-permute-done | bytes 262176 | tf_op jit(solution)/shard_map/ppermute | solution.py:395
  66.8 1.1 %collective-permute-start.14 = (bf16[8,128,128]{2,1,0:T(8,128)(2,1)S(1)}, bf16[8,128,128]{2,1,0:T(8,128)(2,1)S(1)}, u32[]{:S(2)}, u32[]{:S(2)}) collective-permute-start(bf16[8,128,128]{2,1,0:T(8,128)(2,1)S(1)} %broadcast_select_fusion.refs_2_), channel_id=1, source_target_pairs={{0,2},{1,3},{2,0},{3,1},{4,6},{5,7},{6,4},{7,5},{8,10},{9,11},{10,... | collective-permute-start | bytes 786440 | tf_op jit(solution)/shard_map/ppermute | solution.py:395
  67.9 0.1 select_reduce_fusion.1
  68.0 0.1 select_reduce_fusion
  68.1 0.0 collective-permute-done.17.refs_1_
  68.1 3.7 %query_units.8 = (f32[1024,128]{1,0:T(8,128)S(1)}, f32[128,128]{1,0:T(8,128)S(1)}, bf16[1024,1024]{1,0:T(8,128)(2,1)S(1)}) custom-call(s32[4]{0:T(128)S(1)} %pad_add_fusion.7.units, bf16[8,128,128]{2,1,0:T(8,128)(2,1)S(1)} %broadcast_select_fusion.1.refs_0_, bf16[8,128,128]{2,1,0:T(8,128)(2,1)S(1)} %collective-permute-done.17.refs_1_, ...), custom_call_target="tpu_custom_call" | custom-call | flops 805306368 | bytes 6291456 | tf_op jit(solution)/shard_map/query_units/pallas_call | solution.py:351
  71.8 0.3 fusion.3
  72.1 1.2 %collective-permute-done.14.refs_0_ = bf16[8,128,128]{2,1,0:T(8,128)(2,1)S(1)} collective-permute-done((bf16[8,128,128]{2,1,0:T(8,128)(2,1)S(1)}, bf16[8,128,128]{2,1,0:T(8,128)(2,1)S(1)}, u32[]{:S(2)}, u32[]{:S(2)}) %collective-permute-start.14) | collective-permute-done | bytes 262176 | tf_op jit(solution)/shard_map/ppermute | solution.py:395
  73.3 1.7 %query_units.9 = bf16[1024,128]{1,0:T(8,128)(2,1)} custom-call(s32[1]{0:T(128)} %bitcast.7.units, bf16[8,128,128]{2,1,0:T(8,128)(2,1)S(1)} %collective-permute-done.14.refs_0_, f32[64,128]{1,0:T(8,128)S(1)} %bitcast.25, bf16[1024,1024]{1,0:T(8,128)(2,1)S(1)} %get-tuple-element.95.refs_2_, f32[1024,128]{1,0:T(8,128)S(1)} %get-tuple-element.96.refs_3_, ...), custom_call_target="tpu_custom_call" | custom-call | flops 268435456 | bytes 2097152 | tf_op jit(solution)/shard_map/query_units/pallas_call | solution.py:351
  (12 shorter events, 0.1 us)
Async XLA Ops:
  0.7 1.2 %copy-start = (bf16[1,3584,128]{2,1,0:T(8,128)(2,1)S(1)}, bf16[1,3584,128]{2,1,0:T(8,128)(2,1)}, u32[]{:S(2)}) copy-start(bf16[1,3584,128]{2,1,0:T(8,128)(2,1)} %param.7) | copy-start | bytes 2752516
  5.9 9.9 %collective-permute-start = (bf16[8,128,128]{2,1,0:T(8,128)(2,1)S(1)}, bf16[8,128,128]{2,1,0:T(8,128)(2,1)S(1)}, u32[]{:S(2)}, u32[]{:S(2)}) collective-permute-start(bf16[8,128,128]{2,1,0:T(8,128)(2,1)S(1)} %get-tuple-element.54), channel_id=1, source_target_pairs={{0,2},{1,3},{2,0},{3,1},{4,6},{5,7},{6,4},{7,5},{8,10},{9,11},{10,... | collective-permute-start | bytes 786440 | tf_op jit(solution)/shard_map/ppermute | solution.py:395
  15.6 9.1 %collective-permute-start.1 = (bf16[8,128,128]{2,1,0:T(8,128)(2,1)S(1)}, bf16[8,128,128]{2,1,0:T(8,128)(2,1)S(1)}, u32[]{:S(2)}, u32[]{:S(2)}) collective-permute-start(bf16[8,128,128]{2,1,0:T(8,128)(2,1)S(1)} %get-tuple-element.57), channel_id=1, source_target_pairs={{0,2},{1,3},{2,0},{3,1},{4,6},{5,7},{6,4},{7,5},{8,10},{9,11},{10,... | collective-permute-start | bytes 786440 | tf_op jit(solution)/shard_map/ppermute | solution.py:395
  15.9 10.8 %collective-permute-start.2 = (bf16[8,128,128]{2,1,0:T(8,128)(2,1)S(1)}, bf16[8,128,128]{2,1,0:T(8,128)(2,1)S(1)}, u32[]{:S(2)}, u32[]{:S(2)}) collective-permute-start(bf16[8,128,128]{2,1,0:T(8,128)(2,1)S(1)} %fusion), channel_id=1, source_target_pairs={{0,4},{1,5},{2,6},{3,7},{4,0},{5,1},{6,2},{7,3},{8,12},{9,13},{10,... | collective-permute-start | bytes 786440 | tf_op jit(solution)/shard_map/ppermute | solution.py:395
  24.7 9.5 %collective-permute-start.5 = (bf16[8,128,128]{2,1,0:T(8,128)(2,1)S(1)}, bf16[8,128,128]{2,1,0:T(8,128)(2,1)S(1)}, u32[]{:S(2)}, u32[]{:S(2)}) collective-permute-start(bf16[8,128,128]{2,1,0:T(8,128)(2,1)S(1)} %fusion.1), channel_id=1, source_target_pairs={{0,4},{1,5},{2,6},{3,7},{4,0},{5,1},{6,2},{7,3},{8,12},{9,13},{10,... | collective-permute-start | bytes 786440 | tf_op jit(solution)/shard_map/ppermute | solution.py:395
  25.2 9.2 %collective-permute-start.3 = (bf16[8,128,128]{2,1,0:T(8,128)(2,1)S(1)}, bf16[8,128,128]{2,1,0:T(8,128)(2,1)S(1)}, u32[]{:S(2)}, u32[]{:S(2)}) collective-permute-start(bf16[8,128,128]{2,1,0:T(8,128)(2,1)S(1)} %get-tuple-element.61), channel_id=1, source_target_pairs={{0,2},{1,3},{2,0},{3,1},{4,6},{5,7},{6,4},{7,5},{8,10},{9,11},{10,... | collective-permute-start | bytes 786440 | tf_op jit(solution)/shard_map/ppermute | solution.py:395
  26.9 7.5 %collective-permute-start.4 = (bf16[8,128,128]{2,1,0:T(8,128)(2,1)S(1)}, bf16[8,128,128]{2,1,0:T(8,128)(2,1)S(1)}, u32[]{:S(2)}, u32[]{:S(2)}) collective-permute-start(bf16[8,128,128]{2,1,0:T(8,128)(2,1)S(1)} %add_convert_fusion.2), channel_id=1, source_target_pairs={{0,1},{1,0},{2,3},{3,2},{4,8},{5,9},{6,10},{7,11},{8,4},{9,5},{10,... | collective-permute-start | bytes 786440 | tf_op jit(solution)/shard_map/ppermute | solution.py:395
  33.7 9.7 %collective-permute-start.7 = (bf16[8,128,128]{2,1,0:T(8,128)(2,1)S(1)}, bf16[8,128,128]{2,1,0:T(8,128)(2,1)S(1)}, u32[]{:S(2)}, u32[]{:S(2)}) collective-permute-start(bf16[8,128,128]{2,1,0:T(8,128)(2,1)S(1)} %get-tuple-element.66), channel_id=1, source_target_pairs={{0,2},{1,3},{2,0},{3,1},{4,6},{5,7},{6,4},{7,5},{8,10},{9,11},{10,... | collective-permute-start | bytes 786440 | tf_op jit(solution)/shard_map/ppermute | solution.py:395
  34.5 8.9 %collective-permute-start.6 = (bf16[8,128,128]{2,1,0:T(8,128)(2,1)S(1)}, bf16[8,128,128]{2,1,0:T(8,128)(2,1)S(1)}, u32[]{:S(2)}, u32[]{:S(2)}) collective-permute-start(bf16[8,128,128]{2,1,0:T(8,128)(2,1)S(1)} %fusion.2), channel_id=1, source_target_pairs={{0,1},{1,0},{2,3},{3,2},{4,8},{5,9},{6,10},{7,11},{8,4},{9,5},{10,... | collective-permute-start | bytes 786440 | tf_op jit(solution)/shard_map/ppermute | solution.py:395
  34.8 8.6 %collective-permute-start.8 = (bf16[8,128,128]{2,1,0:T(8,128)(2,1)S(1)}, bf16[8,128,128]{2,1,0:T(8,128)(2,1)S(1)}, u32[]{:S(2)}, u32[]{:S(2)}) collective-permute-start(bf16[8,128,128]{2,1,0:T(8,128)(2,1)S(1)} %add_convert_fusion.1), channel_id=1, source_target_pairs={{0,4},{1,5},{2,6},{3,7},{4,0},{5,1},{6,2},{7,3},{8,12},{9,13},{10,... | collective-permute-start | bytes 786440 | tf_op jit(solution)/shard_map/ppermute | solution.py:395
  38.3 5.1 %copy-start.2 = (bf16[1,8,128,128]{3,2,1,0:T(8,128)(2,1)S(1)}, bf16[1,8,128,128]{3,2,1,0:T(8,128)(2,1)}, u32[]{:S(2)}) copy-start(bf16[1,8,128,128]{3,2,1,0:T(8,128)(2,1)} %param.9) | copy-start | bytes 786436
  38.3 9.7 %copy-start.1 = (f32[8192]{0:T(1024)S(1)}, f32[8192]{0:T(1024)}, u32[]{:S(2)}) copy-start(f32[8192]{0:T(1024)} %param.10) | copy-start | bytes 98308
  44.5 7.0 %collective-permute-start.9 = (bf16[8,128,128]{2,1,0:T(8,128)(2,1)S(1)}, bf16[8,128,128]{2,1,0:T(8,128)(2,1)S(1)}, u32[]{:S(2)}, u32[]{:S(2)}) collective-permute-start(bf16[8,128,128]{2,1,0:T(8,128)(2,1)S(1)} %get-tuple-element.71.refs_0_), channel_id=1, source_target_pairs={{0,4},{1,5},{2,6},{3,7},{4,0},{5,1},{6,2},{7,3},{8,12},{9,13},{10,... | collective-permute-start | bytes 786440 | tf_op jit(solution)/shard_map/ppermute | solution.py:395
  45.7 5.8 %collective-permute-start.15 = (bf16[8,128,128]{2,1,0:T(8,128)(2,1)S(1)}, bf16[8,128,128]{2,1,0:T(8,128)(2,1)S(1)}, u32[]{:S(2)}, u32[]{:S(2)}) collective-permute-start(bf16[8,128,128]{2,1,0:T(8,128)(2,1)S(1)} %get-tuple-element.71.refs_0_), channel_id=1, source_target_pairs={{0,1},{1,0},{2,3},{3,2},{4,8},{5,9},{6,10},{7,11},{8,4},{9,5},{10,... | collective-permute-start | bytes 786440 | tf_op jit(solution)/shard_map/ppermute | solution.py:395
  45.8 10.8 %collective-permute-start.11 = (bf16[8,128,128]{2,1,0:T(8,128)(2,1)S(1)}, bf16[8,128,128]{2,1,0:T(8,128)(2,1)S(1)}, u32[]{:S(2)}, u32[]{:S(2)}) collective-permute-start(bf16[8,128,128]{2,1,0:T(8,128)(2,1)S(1)} %get-tuple-element.71.refs_0_), channel_id=1, source_target_pairs={{0,2},{1,3},{2,0},{3,1},{4,6},{5,7},{6,4},{7,5},{8,10},{9,11},{10,... | collective-permute-start | bytes 786440 | tf_op jit(solution)/shard_map/ppermute | solution.py:395
  51.5 8.9 %collective-permute-start.10 = (bf16[8,128,128]{2,1,0:T(8,128)(2,1)S(1)}, bf16[8,128,128]{2,1,0:T(8,128)(2,1)S(1)}, u32[]{:S(2)}, u32[]{:S(2)}) collective-permute-start(bf16[8,128,128]{2,1,0:T(8,128)(2,1)S(1)} %collective-permute-done.9.refs_1_), channel_id=1, source_target_pairs={{0,1},{1,0},{2,3},{3,2},{4,8},{5,9},{6,10},{7,11},{8,4},{9,5},{10,... | collective-permute-start | bytes 786440 | tf_op jit(solution)/shard_map/ppermute | solution.py:395
  51.5 9.3 %collective-permute-start.16 = (bf16[8,128,128]{2,1,0:T(8,128)(2,1)S(1)}, bf16[8,128,128]{2,1,0:T(8,128)(2,1)S(1)}, u32[]{:S(2)}, u32[]{:S(2)}) collective-permute-start(bf16[8,128,128]{2,1,0:T(8,128)(2,1)S(1)} %collective-permute-done.15), channel_id=1, source_target_pairs={{0,4},{1,5},{2,6},{3,7},{4,0},{5,1},{6,2},{7,3},{8,12},{9,13},{10,... | collective-permute-start | bytes 786440 | tf_op jit(solution)/shard_map/ppermute | solution.py:395
  55.0 7.0 %collective-permute-start.13 = (bf16[8,128,128]{2,1,0:T(8,128)(2,1)S(1)}, bf16[8,128,128]{2,1,0:T(8,128)(2,1)S(1)}, u32[]{:S(2)}, u32[]{:S(2)}) collective-permute-start(bf16[8,128,128]{2,1,0:T(8,128)(2,1)S(1)} %collective-permute-done.9.refs_1_), channel_id=1, source_target_pairs={{0,2},{1,3},{2,0},{3,1},{4,6},{5,7},{6,4},{7,5},{8,10},{9,11},{10,... | collective-permute-start | bytes 786440 | tf_op jit(solution)/shard_map/ppermute | solution.py:395
  60.3 6.4 %collective-permute-start.12 = (bf16[8,128,128]{2,1,0:T(8,128)(2,1)S(1)}, bf16[8,128,128]{2,1,0:T(8,128)(2,1)S(1)}, u32[]{:S(2)}, u32[]{:S(2)}) collective-permute-start(bf16[8,128,128]{2,1,0:T(8,128)(2,1)S(1)} %collective-permute-done.10), channel_id=1, source_target_pairs={{0,4},{1,5},{2,6},{3,7},{4,0},{5,1},{6,2},{7,3},{8,12},{9,13},{10,... | collective-permute-start | bytes 786440 | tf_op jit(solution)/shard_map/ppermute | solution.py:395
  60.8 7.3 %collective-permute-start.17 = (bf16[8,128,128]{2,1,0:T(8,128)(2,1)S(1)}, bf16[8,128,128]{2,1,0:T(8,128)(2,1)S(1)}, u32[]{:S(2)}, u32[]{:S(2)}) collective-permute-start(bf16[8,128,128]{2,1,0:T(8,128)(2,1)S(1)} %broadcast_select_fusion.1.refs_0_), channel_id=1, source_target_pairs={{0,2},{1,3},{2,0},{3,1},{4,6},{5,7},{6,4},{7,5},{8,10},{9,11},{10,... | collective-permute-start | bytes 786440 | tf_op jit(solution)/shard_map/ppermute | solution.py:395
  62.0 5.9 %copy-start.3 = (s32[1,4]{1,0:T(1,128)S(1)}, s32[1,4]{1,0:T(1,128)}, u32[]{:S(2)}) copy-start(s32[1,4]{1,0:T(1,128)} %param.13) | copy-start | bytes 52
  66.8 6.4 %collective-permute-start.14 = (bf16[8,128,128]{2,1,0:T(8,128)(2,1)S(1)}, bf16[8,128,128]{2,1,0:T(8,128)(2,1)S(1)}, u32[]{:S(2)}, u32[]{:S(2)}) collective-permute-start(bf16[8,128,128]{2,1,0:T(8,128)(2,1)S(1)} %broadcast_select_fusion.refs_2_), channel_id=1, source_target_pairs={{0,2},{1,3},{2,0},{3,1},{4,6},{5,7},{6,4},{7,5},{8,10},{9,11},{10,... | collective-permute-start | bytes 786440 | tf_op jit(solution)/shard_map/ppermute | solution.py:395
